TPU v7x, 128 devices: a whole 4x4x4 slice. The times are simulated.
128 devices in a mesh: state: 32 (over z, x, core), blk: 4 (over y).
Axes of the slice: x: 4, y: 4, z: 4, core: 2. Of those that a mesh axis runs over, the one named last changes fastest.
Arguments:
- snapshots: bfloat16 [32, 64, 524288], P('blk', None, 'state'), may hold values from -8 to 8
- weights: float32 [524288], P('state'), may hold values from 0.03 to 1.75
- degrees: int32 [524288], P('state'), may hold values from 0 to 383, as said below
- pivots: int32 [16, 8], P('blk'), may hold values from 0 to 524287
Outputs:
- modes: bfloat16 [16, 2, 8, 524288], P('blk', None, None, 'state')
- energy: float32 [16, 8, 384], P('blk')
Inputs may be any that keep to these rules, and one draw needn't show every extreme that they name: `degrees`: the degree of row r is floor(r * 384 / 524288) or one more.
All inputs are finite; a program needn't handle non-finite values.
Results may differ from a plain program's by a relative error of at most 0.0082.
Values may be sent and summed in bfloat16 or wider, within the bound.
No kernel may reach another device: no remote copies, remote signals or barrier semaphores. Data moves between devices by JAX's collectives and lax.ppermute only.
A program may use at most 192 MiB of HBM per device.

v0:
```python
import math

import jax
import jax.numpy as jnp
from jax import lax
from jax.sharding import PartitionSpec as P

NF = 16
DEGREES = 384
ITERS = 6


def dft_rows(harmonics, window_len):
    steps_t = jnp.arange(window_len, dtype=jnp.int32)
    orders = jnp.arange(1, harmonics + 1, dtype=jnp.int32)
    window = 0.5 - 0.5 * jnp.cos(2.0 * math.pi * steps_t.astype(jnp.float32) / window_len)
    window_norm = jnp.sqrt(jnp.sum(window * window))
    turns = orders[:, None] * steps_t[None, :] % window_len
    argument = 2.0 * math.pi * turns.astype(jnp.float32) / window_len
    cosine = window * jnp.cos(argument) / window_norm
    sine = -window * jnp.sin(argument) / window_norm
    return jnp.stack([cosine, sine], axis=1).astype(jnp.bfloat16)


def matmul_high(left, right):
    return jnp.einsum("fab,fbk->fak", left, right, precision=lax.Precision.HIGHEST)


def orthonormal(column_re_all, column_im_all):
    count = column_re_all.shape[2]
    done_re = []
    done_im = []
    for column in range(count):
        vec_re = column_re_all[:, :, column]
        vec_im = column_im_all[:, :, column]
        for earlier in range(column):
            base_re = done_re[earlier]
            base_im = done_im[earlier]
            coef_re = jnp.sum(base_re * vec_re + base_im * vec_im, axis=1, keepdims=True)
            coef_im = jnp.sum(base_re * vec_im - base_im * vec_re, axis=1, keepdims=True)
            vec_re, vec_im = (
                vec_re - (coef_re * base_re - coef_im * base_im),
                vec_im - (coef_re * base_im + coef_im * base_re),
            )
        inverse_norm = lax.rsqrt(
            jnp.sum(vec_re * vec_re + vec_im * vec_im, axis=1, keepdims=True) + 1e-06
        )
        done_re.append(vec_re * inverse_norm)
        done_im.append(vec_im * inverse_norm)
    return (jnp.stack(done_re, axis=2), jnp.stack(done_im, axis=2))


def leading_basis(gram, row_count, modes_kept):
    blocks = gram.shape[1] // 2
    herm_re = (gram[:, :blocks, :blocks] + gram[:, blocks:, blocks:]) / row_count
    herm_im = (gram[:, :blocks, blocks:] - gram[:, blocks:, :blocks]) / row_count
    block_pos = jnp.arange(blocks, dtype=jnp.float32)
    mode_pos = jnp.arange(modes_kept, dtype=jnp.float32)
    start_re = jnp.cos(
        math.pi * (mode_pos[None, :] + 0.5) * (block_pos[:, None] + 0.5) / blocks
    ) * math.sqrt(2.0 / blocks)
    basis_re = jnp.broadcast_to(start_re, (gram.shape[0], blocks, modes_kept))
    basis_im = jnp.zeros_like(basis_re)
    for sweep_index in range(ITERS):
        next_re = matmul_high(herm_re, basis_re) - matmul_high(herm_im, basis_im)
        next_im = matmul_high(herm_re, basis_im) + matmul_high(herm_im, basis_re)
        basis_re, basis_im = orthonormal(next_re, next_im)
    return (basis_re, basis_im)


def expansion(basis_re, basis_im):
    trans_re = jnp.swapaxes(basis_re, 1, 2)
    trans_im = jnp.swapaxes(basis_im, 1, 2)
    upper_rows = jnp.concatenate([trans_re, -trans_im], axis=2)
    lower_rows = jnp.concatenate([trans_im, trans_re], axis=2)
    return jnp.concatenate([upper_rows, lower_rows], axis=1).astype(jnp.bfloat16)


def phased(expanded, pivot_re, pivot_im, modes_kept):
    part_re = expanded[:, :modes_kept]
    part_im = expanded[:, modes_kept:]
    inverse_mag = lax.rsqrt(pivot_re * pivot_re + pivot_im * pivot_im + 1.0)[:, :, None]
    scale_re = pivot_re[:, :, None]
    scale_im = pivot_im[:, :, None]
    out_re = (part_re * scale_re + part_im * scale_im) * inverse_mag
    out_im = (part_im * scale_re - part_re * scale_im) * inverse_mag
    return (out_re, out_im)


def per_device(snapshots, weights, degrees, pivots):
    blocks_dev, window_len, rows_dev = snapshots.shape
    freq_dev, modes_kept = pivots.shape
    dft_table = dft_rows(NF, window_len).reshape(2 * NF, window_len)
    spectra = jnp.einsum("kt,btr->kbr", dft_table, snapshots, preferred_element_type=jnp.float32)
    spectra = spectra.astype(jnp.bfloat16).reshape(NF, 2, blocks_dev, rows_dev)
    coeffs = lax.all_to_all(spectra, "blk", split_axis=0, concat_axis=2, tiled=True)
    total_blocks = coeffs.shape[2]
    stacked = coeffs.reshape(freq_dev, 2 * total_blocks, rows_dev)
    weighted = (stacked * weights).astype(jnp.bfloat16)
    gram_part = jnp.einsum("far,fbr->fab", stacked, weighted, preferred_element_type=jnp.float32)
    row_count = rows_dev * lax.axis_size("state")
    row_start = lax.axis_index("state") * rows_dev
    local_rows = pivots - row_start
    inside = (local_rows >= 0) & (local_rows < rows_dev)
    clipped = jnp.clip(local_rows, 0, rows_dev - 1)
    gram = lax.psum(gram_part, "state")
    basis_re, basis_im = leading_basis(gram, row_count, modes_kept)
    expand_mat = expansion(basis_re, basis_im)
    expanded = jnp.einsum("fka,far->fkr", expand_mat, stacked, preferred_element_type=jnp.float32)
    local_re = jnp.take_along_axis(expanded[:, :modes_kept], clipped[:, :, None], axis=2)[:, :, 0]
    local_im = jnp.take_along_axis(expanded[:, modes_kept:], clipped[:, :, None], axis=2)[:, :, 0]
    local_re = jnp.where(inside, local_re, 0.0)
    local_im = jnp.where(inside, local_im, 0.0)
    pivot_re, pivot_im = lax.psum((local_re, local_im), "state")
    out_re, out_im = phased(expanded, pivot_re, pivot_im, modes_kept)
    modes_out = jnp.stack([out_re, out_im], axis=1).astype(jnp.bfloat16)
    weighted_sq = weights * (out_re * out_re + out_im * out_im)
    one_hot = (degrees[:, None] == jnp.arange(DEGREES, dtype=jnp.int32)[None, :]).astype(
        jnp.float32
    )
    energy_part = jnp.einsum("fkr,rl->fkl", weighted_sq, one_hot, precision=lax.Precision.HIGHEST)
    energy = lax.psum(energy_part, "state") * (DEGREES / row_count)
    return (modes_out, energy)


def solution(mesh):
    placed = (P("blk", None, "state"), P("state"), P("state"), P("blk", None))
    return jax.shard_map(
        per_device,
        mesh=mesh,
        in_specs=placed,
        out_specs=(P("blk", None, None, "state"), P("blk", None, None)),
        check_vma=False,
    )
```

profile of v0, /device:TPU:8, one launch (start us, length us, event | category | flops | bytes accessed | tf_op | source)
XLA Modules:
  0.0 520.2 jit_solution(8761102154943642399)
XLA Ops:
  7.2 0.7 multiply_reduce_fusion
  8.7 11.3 %convolution_convert_fusion = bf16[32,8,16384]{2,0,1:T(8,128)(2,1)} fusion(bf16[32,64,1]{1,0,2:T(8,128)(2,1)S(1)} %bitcast.1080, bf16[8,64,16384]{2,1,0:T(8,128)(2,1)} %param.6), kind=kOutput, calls=%fused_computation.5 | convolution fusion | flops 541065216 | bytes 25169920 | tf_op jit(solution)/shard_map/kt,btr->kbr/dot_general | solution.py:94
  20.0 14.1 %reshape.22571 = bf16[16,2,8,16384]{3,1,0,2:T(2,128)(2,1)} reshape(bf16[32,8,16384]{2,0,1:T(8,128)(2,1)} %convolution_convert_fusion) | data formatting | bytes 16777216 | tf_op jit(solution)/shard_map/reshape | solution.py:95
  34.1 8.0 %copy.62 = bf16[16,2,8,16384]{3,1,2,0:T(2,128)(2,1)} copy(bf16[16,2,8,16384]{3,1,0,2:T(2,128)(2,1)} %reshape.22571) | data formatting | bytes 16777216 | tf_op jit(solution)/shard_map/reshape | solution.py:95
  42.1 6.2 %all-to-all-start = ((bf16[16,2,8,16384]{3,1,2,0:T(2,128)(2,1)}), bf16[16,2,8,16384]{3,1,2,0:T(2,128)(2,1)}, u32[]{:S(2)}, u32[]{:S(2)}) async-start(bf16[16,2,8,16384]{3,1,2,0:T(2,128)(2,1)} %copy.62), calls=%async_computation | async-start | bytes 16777216 | tf_op jit(solution)/shard_map/all_to_all | solution.py:96
  48.3 0.5 all-reduce.3.cloned.1.call-start
  48.9 92.1 %all-to-all-done = bf16[16,2,8,16384]{3,1,2,0:T(2,128)(2,1)} async-done(((bf16[16,2,8,16384]{3,1,2,0:T(2,128)(2,1)}), bf16[16,2,8,16384]{3,1,2,0:T(2,128)(2,1)}, u32[]{:S(2)}, u32[]{:S(2)}) %all-to-all-start) | async-done | bytes 8388640 | tf_op jit(solution)/shard_map/all_to_all | solution.py:96
  141.0 11.9 %copy.63 = bf16[4,4,2,8,16384]{4,3,0,2,1:T(8,128)(2,1)} copy(bf16[4,4,2,8,16384]{4,2,3,1,0:T(2,128)(2,1)} %bitcast.2) | data formatting | bytes 16777216 | tf_op jit(solution)/shard_map/all_to_all | solution.py:96
  152.9 8.7 %fusion.3 = f32[4,64,64]{2,1,0:T(8,128)} fusion(bf16[4,64,16384]{2,1,0:T(8,128)(2,1)} %bitcast.1078, f32[16384]{0:T(1024)S(1)} %copy-done.4), kind=kOutput, calls=%fused_computation.7 | convolution fusion | flops 549453824 | bytes 8519680 | tf_op jit(solution)/shard_map/far,fbr->fab/dot_general | solution.py:100
  161.8 101.2 %all-reduce.3.cloned.1.call-done = f32[4,64,64]{2,1,0:T(8,128)} async-done(((f32[4,64,64]{2,1,0:T(8,128)}), f32[4,64,64]{2,1,0:T(8,128)}) %all-reduce.3.cloned.1.call-update) | async-done | bytes 65552 | tf_op jit(solution)/shard_map/psum | solution.py:106
  263.0 1.0 fusion.12
  265.9 0.4 add_reduce_fusion.146
  266.5 0.4 add_reduce_fusion.145
  272.1 0.4 add_reduce_fusion.118
  272.7 0.5 add_reduce_fusion.117
  278.5 0.4 add_reduce_fusion.90
  284.7 0.4 add_reduce_fusion.62
  285.3 0.4 add_reduce_fusion.61
  290.9 0.4 add_reduce_fusion.34
  297.1 0.4 add_reduce_fusion.6
  301.8 1.2 fusion.13
  303.0 1.8 fusion.261
  304.8 0.8 copy-done
  305.6 2.0 gather_fusion
  307.7 0.8 gather_fusion.1
  308.6 65.7 %all-reduce = (f32[4,8]{1,0:T(4,128)S(1)}, f32[4,8]{1,0:T(4,128)S(1)}) all-reduce(f32[4,8]{1,0:T(4,128)S(1)} %bitcast_select_fusion, f32[4,8]{1,0:T(4,128)S(1)} %get-tuple-element.531), channel_id=1, replica_groups=mesh['state'=32,'blk'=4] {'state'}, use_global_device_ids=true, to_apply=%region_387.389 | all-reduce | flops 64 | bytes 512 | tf_op jit(solution)/shard_map/psum | solution.py:114
  374.2 3.0 convert_bitcast_fusion.1
  377.3 0.4 copy-done.1
  377.7 9.3 %fusion.1 = f32[4,8,384]{2,1,0:T(8,128)S(1)} fusion(s32[16384]{0:T(1024)S(1)} %copy-done.5, f32[16384]{0:T(1024)S(1)} %copy-done.4, f32[4,8]{1,0:T(4,128)S(1)} %add_rsqrt_fusion, f32[4,8]{1,0:T(4,128)S(1)} %get-tuple-element.529, f32[4,8]{1,0:T(4,128)S(1)} %get-tuple-element.530, f32[4,16,16384]{2,1,0:T(8,128)S(1)} %copy-done.1), kind=kOutput, calls=%fused_computation.4 | convolution fusion | flops 2428502016 | bytes 4374912 | tf_op jit(solution)/shard_map/fkr,rl->fkl/dot_general | solution.py:121
  387.0 123.8 %psum.31 = f32[4,8,384]{2,1,0:T(8,128)S(1)} all-reduce(f32[4,8,384]{2,1,0:T(8,128)S(1)} %fusion.1), channel_id=1, replica_groups=mesh['state'=32,'blk'=4] {'state'}, use_global_device_ids=true, to_apply=%region_388.390 | all-reduce | flops 12288 | bytes 98304 | tf_op jit(solution)/shard_map/psum | solution.py:122
  510.8 0.6 broadcast_multiply_fusion
  511.6 1.5 copy.109
  (294 shorter events, 34.5 us)
Async XLA Ops:
  42.1 6.7 %copy-start.3 = (s32[4,8]{1,0:T(4,128)S(1)}, s32[4,8]{1,0:T(4,128)}, u32[]{:S(2)}) copy-start(s32[4,8]{1,0:T(4,128)} %param.9) | copy-start | bytes 388
  42.1 98.9 %all-to-all-start = ((bf16[16,2,8,16384]{3,1,2,0:T(2,128)(2,1)}), bf16[16,2,8,16384]{3,1,2,0:T(2,128)(2,1)}, u32[]{:S(2)}, u32[]{:S(2)}) async-start(bf16[16,2,8,16384]{3,1,2,0:T(2,128)(2,1)} %copy.62), calls=%async_computation | async-start | bytes 16777216 | tf_op jit(solution)/shard_map/all_to_all | solution.py:96
  48.3 214.7 %all-reduce.3.cloned.1.call-start = ((), (), s32[]{:S(2)}) async-start(), calls=%async_computation.1 | async-start | bytes 262144 | tf_op jit(solution)/shard_map/psum | solution.py:106
  141.0 11.9 %copy-start.4 = (f32[16384]{0:T(1024)S(1)}, f32[16384]{0:T(1024)}, u32[]{:S(2)}) copy-start(f32[16384]{0:T(1024)} %param.7) | copy-start | bytes 196612
  269.3 32.5 %copy-start.2 = (bf16[4,4,2,8,16384]{4,3,0,2,1:T(8,128)(2,1)S(1)}, bf16[4,4,2,8,16384]{4,3,0,2,1:T(8,128)(2,1)}, u32[]{:S(2)}) copy-start(bf16[4,4,2,8,16384]{4,3,0,2,1:T(8,128)(2,1)} %copy.63) | copy-start | bytes 25165828
  303.0 2.6 copy-start
  374.2 3.5 copy-start.1
  374.2 3.5 copy-start.5
Sparse Core Ops, SparseCore 0:
  161.8 101.1 all-reduce.2
where the time goes:
time: 524 us; the launch traced here: 520 us
  waiting for transfers between devices  193 us (37%)
  blocking collectives  189 us (36%)
  local copies, waits for them, and re-layouts  41.6 us (8%)
  other arithmetic  37.8 us (7%)
  matrix products  35.8 us (7%)
  between operations  15.6 us (3%)
  starting transfers between devices  6.61 us (1%)
    psum x1, blocking collectives, per_device(): energy = lax.psum(energy_part, 'state') * (DEGREES / row_count)  124 us
    psum x1, waiting for transfers between devices, per_device(): gram = lax.psum(gram_part, 'state')  101 us
    all_to_all x1, waiting for transfers between devices, per_device(): lax.all_to_all(spectra, 'blk', split_axis=0, concat_axis=2, tiled=True)  92.1 us
    psum x1, blocking collectives, per_device(): pivot_re, pivot_im = lax.psum((local_re, local_im), 'state')  65.7 us
    reshape x2, local copies, waits for them, and re-layouts, per_device(): spectra = spectra.astype(jnp.bfloat16).reshape(NF, 2, blocks_dev, rows_dev)  22.1 us
    reduce_sum x48, other arithmetic, orthonormal(): jnp.sum(base_re * vec_re + base_im * vec_im, axis=1, keepdims=True)  13.7 us
    all_to_all x1, local copies, waits for them, and re-layouts, per_device(): lax.all_to_all(spectra, 'blk', split_axis=0, concat_axis=2, tiled=True)  11.9 us
    dot_general x1, matrix products, per_device(): jnp.einsum('kt,btr->kbr', dft_table, snapshots, preferred_element_type=jn...  11.3 us
  transfers between devices with their start and end apart: 2, of which 2 were waited for; matrix products, arithmetic and copies ran while one was open for 0% of the time, Pallas kernels for 0%

commit v1 on v0

v1 whole, which is shorter than its diff:
```python
import math

import jax
import jax.numpy as jnp
import numpy as np
from jax import lax
from jax.experimental import pallas as pl
from jax.experimental.pallas import tpu as pltpu
from jax.sharding import Mesh
from jax.sharding import PartitionSpec as P

NF = 16
DEGREES = 384
ITERS = 6
MODES = 8
WINDOW = 64
GROUPS = 4
PER_GROUP = 8
OWNED = 4
PAIR = 2
HALVES = 2
BLOCKS = GROUPS * PER_GROUP
STATE = (4, 4, 2)
DEVICES = 32
LEVELS = DEGREES // DEVICES
F32 = jnp.float32
BF16 = jnp.bfloat16
VMEM = 48 * 1024 * 1024


def dft_table():
    t = np.arange(WINDOW, dtype=np.int32)
    order = np.arange(1, NF + 1, dtype=np.int32)
    two_pi = np.float32(2.0 * math.pi)
    window = np.float32(0.5) - np.float32(0.5) * np.cos(two_pi * t.astype(np.float32) / np.float32(WINDOW))
    norm = np.sqrt(np.sum(window * window))
    turns = order[:, None] * t[None, :] % WINDOW
    angle = two_pi * turns.astype(np.float32) / np.float32(WINDOW)
    table = np.stack([window * np.cos(angle) / norm, -window * np.sin(angle) / norm], axis=1)
    return table.astype(BF16)


def spectral_lhs():
    table = dft_table()
    lhs = np.zeros((GROUPS, OWNED, 2, PER_GROUP, PER_GROUP, WINDOW), dtype=BF16)
    for owner in range(GROUPS):
        for i in range(OWNED):
            for b in range(PER_GROUP):
                lhs[owner, i, :, b, b, :] = table[OWNED * owner + i]
    return lhs.reshape(GROUPS, OWNED * 2 * PER_GROUP, PER_GROUP * WINDOW)


def start_basis():
    b = np.arange(BLOCKS, dtype=np.float32)
    j = np.arange(MODES, dtype=np.float32)
    v0 = np.cos(np.float32(math.pi) * (j[:, None] + np.float32(0.5)) * (b[None, :] + np.float32(0.5)) / np.float32(BLOCKS))
    v0 = (v0 * np.float32(math.sqrt(2.0 / BLOCKS))).reshape(MODES, GROUPS, PER_GROUP)
    out = np.zeros((GROUPS, 2, MODES, 2, GROUPS, 2, PER_GROUP), dtype=np.float32)
    for y in range(GROUPS):
        for slot in range(GROUPS):
            for part in range(2):
                out[y, part, :, :, slot, part, :] = v0[:, None, (y - slot) % GROUPS]
    return out.reshape(GROUPS, 2, MODES, 128)


def spectra_call(place, snapshots, half, tile):
    blocks_dev, window_len, rows_dev = snapshots.shape
    rows = OWNED * 2 * PER_GROUP
    depth = blocks_dev * window_len
    part = rows_dev // HALVES
    steps = part // tile
    lhs_all = jnp.asarray(spectral_lhs())

    def kernel(place_ref, lhs_ref, x_ref, *rest):
        outs, lhs = rest[:-1], rest[-1]

        @pl.when(pl.program_id(0) == 0)
        def _():
            for slot in range(GROUPS):
                owner = lax.rem(place_ref[0] + slot, GROUPS)
                lhs[slot * rows : (slot + 1) * rows, :] = lhs_ref[owner]

        data = x_ref[...].reshape(depth, tile)
        result = jnp.dot(lhs[...], data, preferred_element_type=F32).astype(BF16)
        for n, out in enumerate(outs):
            out[...] = result[n * 32 : (n + 1) * 32]

    out = pl.pallas_call(
        kernel,
        grid_spec=pltpu.PrefetchScalarGridSpec(
            num_scalar_prefetch=1,
            grid=(steps,),
            in_specs=[
                pl.BlockSpec((GROUPS, rows, depth), lambda n, p: (0, 0, 0)),
                pl.BlockSpec((blocks_dev, window_len, tile), lambda n, p: (0, 0, n + half * steps)),
            ],
            out_specs=[pl.BlockSpec((32, tile), lambda n, p: (0, n))] * (GROUPS * PAIR),
            scratch_shapes=[pltpu.VMEM((GROUPS * rows, depth), BF16)],
        ),
        out_shape=[jax.ShapeDtypeStruct((32, part), BF16)] * (GROUPS * PAIR),
        compiler_params=pltpu.CompilerParams(vmem_limit_bytes=VMEM),
        cost_estimate=pl.CostEstimate(
            flops=2 * GROUPS * rows * depth * part,
            bytes_accessed=2 * (depth + GROUPS * rows) * part,
            transcendentals=0,
        ),
        name="spectra",
    )(place, lhs_all, snapshots)
    return [[out[slot * PAIR + i] for slot in range(GROUPS)] for i in range(PAIR)]


def odd_lanes(shape):
    return (lax.broadcasted_iota(jnp.int32, shape, len(shape) - 1) & 8) == 8


def low_lanes(shape):
    return lax.broadcasted_iota(jnp.int32, shape, len(shape) - 1) < 64


def turned(value):
    axis = value.ndim - 1
    return jnp.where(
        odd_lanes(value.shape), pltpu.roll(value, 8, axis), -pltpu.roll(value, 120, axis)
    )


def gram_call(half, pieces, weights, pivot_local, before, tile):
    part = pieces[0].shape[1]
    steps = part // tile

    def kernel(p_ref, w_ref, *rest):
        x_refs, rest = rest[:GROUPS], rest[GROUPS:]
        out_ref, acc = rest[-2:]
        n = pl.program_id(0)

        @pl.when(n == 0)
        def _():
            acc[...] = jnp.zeros_like(acc)

        lane = lax.broadcasted_iota(jnp.int32, (MODES, tile), 1) + (n + half * steps) * tile
        for f in range(PAIR):
            x = jnp.concatenate([r[16 * f : 16 * f + 16] for r in x_refs], axis=0)
            wx = x.astype(F32) * w_ref[...]
            hot = jnp.where(lane == p_ref[f], 1.0, 0.0)
            left = jnp.concatenate([wx, hot, jnp.zeros_like(hot)], axis=0).astype(BF16)
            acc[f, :, :64] += lax.dot_general(
                left, x, (((1,), (1,)), ((), ())), preferred_element_type=F32
            )

        @pl.when(n == steps - 1)
        def _():
            for f in range(PAIR):
                total = acc[f]
                total = total + pltpu.roll(total, 64, 1)
                g = total[:64].reshape(GROUPS, 2, PER_GROUP, 128)
                upper = g[:, 0].reshape(BLOCKS, 128)
                lower = g[:, 1].reshape(BLOCKS, 128)
                cross = jnp.where(
                    odd_lanes(upper.shape),
                    pltpu.roll(lower, 8, 1) - upper,
                    upper + pltpu.roll(lower, 120, 1),
                )
                packed = jnp.where(low_lanes((16, 128)), cross[:16], cross[16:])
                packed = jnp.concatenate([packed, total[64:72]], axis=0)
                if before is not None:
                    packed = packed + rest[0][f]
                out_ref[f] = packed

    whole = pl.BlockSpec((PAIR, 24, 128), lambda n: (0, 0, 0))
    return pl.pallas_call(
        kernel,
        grid=(steps,),
        in_specs=[
            pl.BlockSpec((PAIR, MODES, 1), lambda n: (0, 0, 0)),
            pl.BlockSpec((1, tile), lambda n: (0, n + half * steps)),
        ]
        + [pl.BlockSpec((32, tile), lambda n: (0, n))] * GROUPS
        + [whole] * (before is not None),
        out_specs=whole,
        out_shape=jax.ShapeDtypeStruct((PAIR, 24, 128), F32),
        scratch_shapes=[pltpu.VMEM((PAIR, 80, 128), F32)],
        compiler_params=pltpu.CompilerParams(vmem_limit_bytes=VMEM),
        cost_estimate=pl.CostEstimate(
            flops=2 * PAIR * 64 * 256 * part, bytes_accessed=4 * 64 * part, transcendentals=0
        ),
        name="gram",
    )(pivot_local, weights, *pieces, *([] if before is None else [before]))


def split3(value):
    high = value.astype(BF16)
    rest = value - high.astype(F32)
    mid = rest.astype(BF16)
    low = (rest - mid.astype(F32)).astype(BF16)
    return high, mid, low


def right_side(cross):
    turn = turned(cross)
    full = jnp.concatenate(
        [
            piece
            for g in range(GROUPS)
            for piece in (cross[8 * g : 8 * g + 8], turn[8 * g : 8 * g + 8])
        ],
        axis=0,
    )
    full = jnp.concatenate([full, turned(full)], axis=1)
    high, mid, low = split3(full)
    return jnp.concatenate([high, mid, high, mid, low, high], axis=0)


def leading_basis(crosses, begin):
    count = len(crosses)
    rights = [right_side(cross) for cross in crosses]
    vec = jnp.stack([begin[0]] * count)
    alt = jnp.stack([begin[1]] * count)
    low_lane = low_lanes((MODES, 128))
    row = lax.broadcasted_iota(jnp.int32, (count, MODES, 1), 1)
    for _ in range(ITERS):
        new = []
        for f in range(count):
            high, mid, low = split3(vec[f])
            mixed = jnp.where(low_lane, high.astype(F32), low.astype(F32)).astype(BF16)
            left = jnp.concatenate([high, mid, mixed], axis=1)
            new.append(jnp.dot(left, rights[f], preferred_element_type=F32))
        new = jnp.stack(new)
        vec, alt = new[:, :, :128], new[:, :, 128:]
        scale = jnp.ones((count, MODES, 1), F32)
        for j in range(MODES):
            q = jnp.broadcast_to(vec[:, j : j + 1], vec.shape)
            q_alt = jnp.broadcast_to(alt[:, j : j + 1], vec.shape)
            power = jnp.sum(q * q, axis=2, keepdims=True)
            scale = jnp.where(row == j, lax.rsqrt(power * 0.5 + 1e-06), scale)
            if j < MODES - 1:
                inverse = jnp.where(row > j, 1.0 / (power + 2e-06), 0.0)
                coef_re = jnp.sum(vec * q, axis=2, keepdims=True) * inverse
                coef_im = jnp.sum(vec * q_alt, axis=2, keepdims=True) * inverse
                vec, alt = (
                    vec - (coef_re * q + coef_im * q_alt),
                    alt - (coef_re * q_alt - coef_im * q),
                )
        vec = vec * scale
        alt = alt * scale
    return vec, alt


def modes_call(pair, place, start, weights, degrees, sums, early, late, before, row_count, tile):
    rows_dev = weights.shape[1]
    steps = rows_dev // tile
    part_steps = steps // HALVES
    bands = tile * DEGREES // row_count

    def kernel(place_ref, start_ref, w_ref, deg_ref, sum_ref, *rest):
        x_refs, rest = rest[: HALVES * GROUPS], rest[HALVES * GROUPS :]
        modes_ref, energy_ref, expand, phase = rest[-4:]
        n = pl.program_id(0)

        @pl.when(n == 0)
        def _():
            total = jnp.sum(sum_ref[...], axis=0)
            crosses = []
            for f in range(PAIR):
                packed = total[f, :16] * (1.0 / row_count)
                swap = pltpu.roll(packed, 64, 1)
                low = low_lanes(packed.shape)
                crosses.append(
                    jnp.concatenate(
                        [jnp.where(low, packed, swap), jnp.where(low, swap, packed)], axis=0
                    )
                )
            vec, alt = leading_basis(crosses, start_ref[place_ref[0]])
            odd = odd_lanes(vec.shape)
            low = low_lanes(vec.shape)
            upper = jnp.where(odd, -vec, vec).astype(BF16).astype(F32)
            lower = jnp.where(odd, alt, -alt).astype(BF16).astype(F32)
            at = jnp.where(low, total[:, 16:24], 0.0)
            z_re = jnp.sum(upper * at, axis=2, keepdims=True)
            z_im = jnp.sum(lower * at, axis=2, keepdims=True)
            inverse = lax.rsqrt(z_re * z_re + z_im * z_im + 1.0)
            phase[0] = jnp.broadcast_to(z_re * inverse, vec.shape)
            phase[1] = jnp.broadcast_to(z_im * inverse, vec.shape)
            expand[:, :8] = upper
            expand[:, 8:] = lower
            energy_ref[...] = jnp.zeros_like(energy_ref) if before is None else rest[1][...]

        w = w_ref[...]
        base = place_ref[1] + n * bands
        lane = lax.broadcasted_iota(jnp.int32, (MODES, 128), 1)
        first = n < part_steps
        for f in range(PAIR):
            rows = slice(16 * f, 16 * f + 16)
            x = jnp.concatenate(
                [
                    jnp.where(first, x_refs[k][rows], x_refs[GROUPS + k][rows])
                    for k in range(GROUPS)
                ],
                axis=0,
            )
            psi = jnp.dot(expand[f][:, :64].astype(BF16), x, preferred_element_type=F32)
            s_re = phase[0, f, :, :1]
            s_im = phase[1, f, :, :1]
            p_re, p_im = psi[:8], psi[8:]
            out_re = p_re * s_re + p_im * s_im
            out_im = p_im * s_re - p_re * s_im
            modes_ref[f, 0] = out_re.astype(BF16)
            modes_ref[f, 1] = out_im.astype(BF16)
            power = w * (out_re * out_re + out_im * out_im)
            for m in range(bands + 1):
                level = jnp.sum(
                    jnp.where(deg_ref[...] == base + m, power, 0.0), axis=1, keepdims=True
                )
                spot = (pair * PAIR + f) * 32 + place_ref[2] + n * bands + m
                energy_ref[...] += jnp.where(lane == spot, level * (DEGREES / row_count), 0.0)

    in_specs = [
        pl.BlockSpec((GROUPS, 2, MODES, 128), lambda n, p: (0, 0, 0, 0)),
        pl.BlockSpec((1, tile), lambda n, p: (0, n)),
        pl.BlockSpec((1, tile), lambda n, p: (0, n)),
        pl.BlockSpec(sums.shape, lambda n, p: (0, 0, 0, 0)),
    ]
    in_specs += [
        pl.BlockSpec((32, tile), lambda n, p: (0, jnp.minimum(n, part_steps - 1)))
    ] * GROUPS
    in_specs += [
        pl.BlockSpec((32, tile), lambda n, p: (0, jnp.maximum(n - part_steps, 0)))
    ] * GROUPS
    args = [place, start, weights, degrees, sums, *early, *late]
    aliases = {}
    if before is not None:
        in_specs += [
            pl.BlockSpec(memory_space=pl.ANY),
            pl.BlockSpec((MODES, 128), lambda n, p: (0, 0)),
        ]
        aliases = {len(args): 0}
        args += list(before)
    return pl.pallas_call(
        kernel,
        grid_spec=pltpu.PrefetchScalarGridSpec(
            num_scalar_prefetch=1,
            grid=(steps,),
            in_specs=in_specs,
            out_specs=[
                pl.BlockSpec((PAIR, 2, MODES, tile), lambda n, p: (pair, 0, 0, n)),
                pl.BlockSpec((MODES, 128), lambda n, p: (0, 0)),
            ],
            scratch_shapes=[
                pltpu.VMEM((PAIR, 16, 128), F32),
                pltpu.VMEM((2, PAIR, MODES, 128), F32),
            ],
        ),
        out_shape=[
            jax.ShapeDtypeStruct((OWNED, 2, MODES, rows_dev), BF16),
            jax.ShapeDtypeStruct((MODES, 128), F32),
        ],
        input_output_aliases=aliases,
        compiler_params=pltpu.CompilerParams(vmem_limit_bytes=VMEM),
        cost_estimate=pl.CostEstimate(
            flops=2 * PAIR * 64 * 256 * rows_dev + 10**9,
            bytes_accessed=PAIR * 2 * 80 * rows_dev,
            transcendentals=0,
        ),
        name="modes",
    )(*args)


def energy_call(gathered):
    chips = gathered.shape[0]

    def kernel(in_ref, out_ref):
        out_ref[...] = jnp.zeros_like(out_ref)
        lane = lax.broadcasted_iota(jnp.int32, (MODES, 128), 1)
        for c in range(chips):
            value = in_ref[c]
            for f in range(OWNED):
                begin = c * 2 * LEVELS
                piece = jnp.where((lane >= 32 * f) & (lane < 32 * f + 2 * LEVELS + 1), value, 0.0)
                shift = (begin - 32 * f) % 128
                piece = pltpu.roll(piece, shift, 1) if shift else piece
                column = begin // 128
                split = 128 - begin % 128
                if split >= 2 * LEVELS + 1:
                    out_ref[f, :, column * 128 : column * 128 + 128] += piece
                else:
                    head = jnp.where(lane >= begin % 128, piece, 0.0)
                    out_ref[f, :, column * 128 : column * 128 + 128] += head
                    if (column + 1) * 128 < DEGREES:
                        out_ref[f, :, (column + 1) * 128 : (column + 2) * 128] += piece - head

    return pl.pallas_call(
        kernel,
        out_shape=jax.ShapeDtypeStruct((OWNED, MODES, DEGREES), F32),
        name="energy",
    )(gathered)


def gather_chips(value):
    value = value + lax.ppermute(value, "core", [(0, 1), (1, 0)])
    chips = STATE[0] * STATE[1]
    spread = jnp.broadcast_to(value[None], (chips,) + value.shape)
    return lax.all_to_all(spread, ("z", "x"), 0, 0, tiled=True)


def per_device(snapshots, weights, degrees, pivots):
    rows_dev = snapshots.shape[2]
    row_count = rows_dev * DEVICES
    core = lax.axis_index("core").astype(jnp.int32)
    state = (lax.axis_index(("z", "x", "core"))).astype(jnp.int32)
    y = lax.axis_index("blk").astype(jnp.int32)
    place = jnp.stack([y, state * LEVELS, core * LEVELS])
    pivot_local = (pivots - state * rows_dev)[:, :, None]
    weights = weights.reshape(1, rows_dev)
    degrees = degrees.reshape(1, rows_dev)
    start = jnp.asarray(start_basis())

    halves = [spectra_call(place, snapshots, half, 2048) for half in range(HALVES)]
    pieces = {}
    for pair in range(PAIR):
        for half in range(HALVES):
            sent = halves[half][pair]
            pieces[pair, half] = [sent[0]] + [
                lax.ppermute(sent[k], "blk", [(g, (g + k) % GROUPS) for g in range(GROUPS)])
                for k in range(1, GROUPS)
            ]
    before = None
    for pair in range(PAIR):
        gram = None
        for half in range(HALVES):
            gram = gram_call(
                half, pieces[pair, half], weights, pivot_local[PAIR * pair : PAIR * pair + PAIR], gram, 4096
            )
        before = modes_call(
            pair, place, start, weights, degrees, gather_chips(gram),
            pieces[pair, 0], pieces[pair, 1], before, row_count, 4096,
        )
    modes, energy = before
    return modes, energy_call(gather_chips(energy))


def solution(mesh):
    fine = Mesh(mesh.devices.reshape(*STATE, GROUPS), ("z", "x", "core", "blk"))
    state = ("z", "x", "core")
    return jax.shard_map(
        per_device,
        mesh=fine,
        in_specs=(P("blk", None, state), P(state), P(state), P("blk", None)),
        out_specs=(P("blk", None, None, state), P("blk", None, None)),
        check_vma=False,
    )
```

time: 524 us -> 158 us (0.30)
  blocking collectives: 189 us -> 14.7 us
  waiting for transfers between devices: 193 us -> 55.5 us
  Pallas kernels: 0 us -> 46 us
  other arithmetic: 37.8 us -> 0.09 us
  matrix products: 35.8 us -> 0 us
  local copies, waits for them, and re-layouts: 41.6 us -> 6.11 us
  starting transfers between devices: 6.61 us -> 33.9 us
  between operations: 15.6 us -> 0.79 us
    psum x2 -> x0, blocking collectives: 189 us -> none  [the longest x1 124 us: per_device(): energy = lax.psum(energy_part, 'state') * (DEGREES / row_count)]
    psum x1 -> x0, waiting for transfers between devices: 101 us -> none  [per_device(): gram = lax.psum(gram_part, 'state')]
    all_to_all x1 -> x2, waiting for transfers between devices: 92.1 us -> 0.01 us  [gather_chips(): return lax.all_to_all(spread, ('z', 'x'), 0, 0, tiled=True)]
    ppermute x0 -> x15, waiting for transfers between devices: none -> 55.5 us  [the longest x12 53.2 us: per_device(): lax.ppermute(sent[k], 'blk', [(g, (g + k) % GROUPS) for g in range(GROUPS)])]
    pallas_call x0 -> x9, Pallas kernels: none -> 46 us  [the longest x2 21.3 us: modes_call(): pl.pallas_call(kernel, grid_spec=pltpu.PrefetchScalarGridSpec(num_scalar_...]
    dot_general x28 -> x0, matrix products: 35.8 us -> none  [the longest x1 11.3 us: per_device(): jnp.einsum('kt,btr->kbr', dft_table, snapshots, preferred_element_type=jn...]
    reduce_sum x97 -> x0, other arithmetic: 23.1 us -> none  [the longest x48 13.7 us: orthonormal(): jnp.sum(base_re * vec_re + base_im * vec_im, axis=1, keepdims=True)]
    reshape x2 -> x0, local copies, waits for them, and re-layouts: 22.1 us -> none  [per_device(): spectra = spectra.astype(jnp.bfloat16).reshape(NF, 2, blocks_dev, rows_dev)]
  transfers between devices with their start and end apart: 2 -> 17, of which waited for: 2 -> 9; matrix products, arithmetic and copies ran while one was open for 0% -> 1% of each run, Pallas kernels for 0% -> 17%
where the time goes in v1:
time: 158 us; the launch traced here: 157 us
  waiting for transfers between devices  55.5 us (35%)
  Pallas kernels  46 us (29%)
  starting transfers between devices  33.9 us (21%)
  blocking collectives  14.7 us (9%)
  local copies, waits for them, and re-layouts  6.11 us (4%)
    ppermute x12, waiting for transfers between devices, per_device(): lax.ppermute(sent[k], 'blk', [(g, (g + k) % GROUPS) for g in range(GROUPS)])  53.2 us
    pallas_call x2, Pallas kernels, modes_call(): pl.pallas_call(kernel, grid_spec=pltpu.PrefetchScalarGridSpec(num_scalar_...  21.3 us
    ppermute x12, starting transfers between devices, per_device(): lax.ppermute(sent[k], 'blk', [(g, (g + k) % GROUPS) for g in range(GROUPS)])  17.9 us
    all_to_all x2, starting transfers between devices, gather_chips(): return lax.all_to_all(spread, ('z', 'x'), 0, 0, tiled=True)  15.8 us
    all_to_all x1, blocking collectives, gather_chips(): return lax.all_to_all(spread, ('z', 'x'), 0, 0, tiled=True)  14.7 us
    pallas_call x2, Pallas kernels, spectra_call(): pl.pallas_call(kernel, grid_spec=pltpu.PrefetchScalarGridSpec(num_scalar_...  14.5 us
    pallas_call x4, Pallas kernels, gram_call(): pl.pallas_call(kernel, grid=(steps,), in_specs=[pl.BlockSpec((PAIR, MODES...  8.67 us
    unnamed x20, local copies, waits for them, and re-layouts  4.38 us
  transfers between devices with their start and end apart: 17, of which 9 were waited for; matrix products, arithmetic and copies ran while one was open for 1% of the time, Pallas kernels for 17%

profile of v1, /device:TPU:8, one launch (start us, length us, event | category | flops | bytes accessed | tf_op | source)
XLA Modules:
  0.0 157.2 jit_solution(6732195288396767472)
XLA Ops:
  0.7 0.9 copy-done
  1.7 7.1 %spectra.3 = (bf16[32,8192]{1,0:T(8,128)(2,1)S(1)}, bf16[32,8192]{1,0:T(8,128)(2,1)S(1)}, bf16[32,8192]{1,0:T(8,128)(2,1)S(1)}, bf16[32,8192]{1,0:T(8,128)(2,1)S...) custom-call(s32[3]{0:T(128)S(1)} %pad_add_fusion.place_ref, ...), custom_call_target="tpu_custom_call" | custom-call | flops 2147483648 | bytes 12582912 | tf_op jit(solution)/shard_map/spectra/pallas_call | solution.py:88
  8.8 0.8 copy-done.5
  9.6 0.8 copy-done.6
  10.3 1.6 %collective-permute-start.10 = (bf16[32,8192]{1,0:T(8,128)(2,1)S(1)}, bf16[32,8192]{1,0:T(8,128)(2,1)S(1)}, u32[]{:S(2)}, u32[]{:S(2)}) collective-permute-start(bf16[32,8192]{1,0:T(8,128)(2,1)S(1)} %get-tuple-element.35), channel_id=1, source_target_pairs={{0,1},{1,2},{2,3},{3,0},{4,5},{5,6},{6,7},{7,4},{8,9},{9,10},{10,1... | collective-permute-start | bytes 1572872 | tf_op jit(solution)/shard_map/ppermute | solution.py:422
  11.9 0.9 collective-permute-start.11
  12.8 2.5 %collective-permute-start.12 = (bf16[32,8192]{1,0:T(8,128)(2,1)}, bf16[32,8192]{1,0:T(8,128)(2,1)S(1)}, u32[]{:S(2)}, u32[]{:S(2)}) collective-permute-start(bf16[32,8192]{1,0:T(8,128)(2,1)} %get-tuple-element.37), channel_id=1, source_target_pairs={{0,3},{1,0},{2,1},{3,2},{4,7},{5,4},{6,5},{7,6},{8,11},{9,8},{10,9... | collective-permute-start | bytes 1572872 | tf_op jit(solution)/shard_map/ppermute | solution.py:422
  15.3 7.4 %spectra.2 = (bf16[32,8192]{1,0:T(8,128)(2,1)S(1)}, bf16[32,8192]{1,0:T(8,128)(2,1)S(1)}, bf16[32,8192]{1,0:T(8,128)(2,1)}, bf16[32,8192]{1,0:T(8,128)(2,1)}, bf...) custom-call(s32[3]{0:T(128)S(1)} %pad_add_fusion.place_ref, ...), custom_call_target="tpu_custom_call" | custom-call | flops 2147483648 | bytes 12582912 | tf_op jit(solution)/shard_map/spectra/pallas_call | solution.py:88
  22.7 0.8 copy-done.2
  23.5 3.4 %collective-permute-start.8 = (bf16[32,8192]{1,0:T(8,128)(2,1)}, bf16[32,8192]{1,0:T(8,128)(2,1)}, u32[]{:S(2)}, u32[]{:S(2)}) collective-permute-start(bf16[32,8192]{1,0:T(8,128)(2,1)} %get-tuple-element.32), channel_id=1, source_target_pairs={{0,2},{1,3},{2,0},{3,1},{4,6},{5,7},{6,4},{7,5},{8,10},{9,11},{10,... | collective-permute-start | bytes 1572872 | tf_op jit(solution)/shard_map/ppermute | solution.py:422
  26.9 7.0 %collective-permute-done.10.rest_1_ = bf16[32,8192]{1,0:T(8,128)(2,1)S(1)} collective-permute-done((bf16[32,8192]{1,0:T(8,128)(2,1)S(1)}, bf16[32,8192]{1,0:T(8,128)(2,1)S(1)}, u32[]{:S(2)}, u32[]{:S(2)}) %collective-permute-start.10) | collective-permute-done | bytes 524320 | tf_op jit(solution)/shard_map/ppermute | solution.py:422
  33.9 4.0 %collective-permute-start.3 = (bf16[32,8192]{1,0:T(8,128)(2,1)}, bf16[32,8192]{1,0:T(8,128)(2,1)}, u32[]{:S(2)}, u32[]{:S(2)}) collective-permute-start(bf16[32,8192]{1,0:T(8,128)(2,1)} %copy-done.6), channel_id=1, source_target_pairs={{0,1},{1,2},{2,3},{3,0},{4,5},{5,6},{6,7},{7,4},{8,9},{9,10},{10,1... | collective-permute-start | bytes 1572872 | tf_op jit(solution)/shard_map/ppermute | solution.py:422
  38.0 10.3 %collective-permute-done.12.rest_3_ = bf16[32,8192]{1,0:T(8,128)(2,1)S(1)} collective-permute-done((bf16[32,8192]{1,0:T(8,128)(2,1)}, bf16[32,8192]{1,0:T(8,128)(2,1)S(1)}, u32[]{:S(2)}, u32[]{:S(2)}) %collective-permute-start.12) | collective-permute-done | bytes 524320 | tf_op jit(solution)/shard_map/ppermute | solution.py:422
  48.3 1.4 gram.6.rest_4_
  49.7 6.7 %collective-permute-done.7.rest_1_.rest_5_ = bf16[32,8192]{1,0:T(8,128)(2,1)} collective-permute-done((bf16[32,8192]{1,0:T(8,128)(2,1)}, bf16[32,8192]{1,0:T(8,128)(2,1)}, u32[]{:S(2)}, u32[]{:S(2)}) %collective-permute-start.7) | collective-permute-done | bytes 524320 | tf_op jit(solution)/shard_map/ppermute | solution.py:422
  56.4 6.0 %collective-permute-done.9.rest_3_.rest_7_ = bf16[32,8192]{1,0:T(8,128)(2,1)} collective-permute-done((bf16[32,8192]{1,0:T(8,128)(2,1)}, bf16[32,8192]{1,0:T(8,128)(2,1)}, u32[]{:S(2)}, u32[]{:S(2)}) %collective-permute-start.9) | collective-permute-done | bytes 524320 | tf_op jit(solution)/shard_map/ppermute | solution.py:422
  62.4 2.4 %gram.7 = f32[2,24,128]{2,1,0:T(8,128)S(1)} custom-call(s32[2,8,1]{2,1,0:T(8,128)S(1)} %copy.13.p_ref, f32[1,16384]{1,0:T(1,128)S(1)} %bitcast.10, bf16[32,8192]{1,0:T(8,128)(2,1)S(1)} %copy-done.3, bf16[32,8192]{1,0:T(8,128)(2,1)} %collective-permute-done.7.rest_1_.rest_5_, bf16[32,8192]{1,0:T(8,128)(2,1)} %collective-permute-done.8.rest_2_.rest_6_, ...), custom_call_target="tpu_custom_call" | custom-call | flops 536870912 | bytes 2097152 | tf_op jit(solution)/shard_map/gram/pallas_call | solution.py:170
  65.5 13.4 %collective-permute-done.3.rest_1_ = bf16[32,8192]{1,0:T(8,128)(2,1)} collective-permute-done((bf16[32,8192]{1,0:T(8,128)(2,1)}, bf16[32,8192]{1,0:T(8,128)(2,1)}, u32[]{:S(2)}, u32[]{:S(2)}) %collective-permute-start.3) | collective-permute-done | bytes 524320 | tf_op jit(solution)/shard_map/ppermute | solution.py:422
  78.9 5.0 %collective-permute-start.2 = (bf16[32,8192]{1,0:T(8,128)(2,1)}, bf16[32,8192]{1,0:T(8,128)(2,1)}, u32[]{:S(2)}, u32[]{:S(2)}) collective-permute-start(bf16[32,8192]{1,0:T(8,128)(2,1)} %get-tuple-element.25), channel_id=1, source_target_pairs={{0,3},{1,0},{2,1},{3,2},{4,7},{5,4},{6,5},{7,6},{8,11},{9,8},{10,9... | collective-permute-start | bytes 1572872 | tf_op jit(solution)/shard_map/ppermute | solution.py:422
  84.7 7.9 %all-to-all-start.1 = ((f32[16,2,24,128]{3,2,1,0:T(8,128)}), f32[16,2,24,128]{3,2,1,0:T(8,128)}, u32[]{:S(2)}, u32[]{:S(2)}) async-start(f32[16,2,24,128]{3,2,1,0:T(8,128)} %broadcast_in_dim.7), calls=%async_computation.1 | async-start | bytes 786432 | tf_op jit(solution)/shard_map/all_to_all | solution.py:401
  92.7 2.4 %gram.4.rest_4_ = f32[2,24,128]{2,1,0:T(8,128)S(1)} custom-call(s32[2,8,1]{2,1,0:T(8,128)S(1)} %copy.11.p_ref, f32[1,16384]{1,0:T(1,128)S(1)} %bitcast.11, bf16[32,8192]{1,0:T(8,128)(2,1)S(1)} %get-tuple-element.26.rest_0_, bf16[32,8192]{1,0:T(8,128)(2,1)} %collective-permute-done.3.rest_1_, bf16[32,8192]{1,0:T(8,128)(2,1)} %collective-permute-done.4.rest_2_, ...), custom_call_target="tpu_custom_call" | custom-call | flops 536870912 | bytes 2097152 | tf_op jit(solution)/shard_map/gram/pallas_call | solution.py:170
  95.2 1.0 collective-permute-done.1.rest_2_.rest_6_
  96.1 8.9 %collective-permute-done.2.rest_3_.rest_7_ = bf16[32,8192]{1,0:T(8,128)(2,1)} collective-permute-done((bf16[32,8192]{1,0:T(8,128)(2,1)}, bf16[32,8192]{1,0:T(8,128)(2,1)}, u32[]{:S(2)}, u32[]{:S(2)}) %collective-permute-start.2) | collective-permute-done | bytes 524320 | tf_op jit(solution)/shard_map/ppermute | solution.py:422
  105.0 2.4 %gram.5 = f32[2,24,128]{2,1,0:T(8,128)S(1)} custom-call(s32[2,8,1]{2,1,0:T(8,128)S(1)} %copy.11.p_ref, f32[1,16384]{1,0:T(1,128)S(1)} %bitcast.12, bf16[32,8192]{1,0:T(8,128)(2,1)S(1)} %get-tuple-element.22.rest_0_.rest_4_, bf16[32,8192]{1,0:T(8,128)(2,1)} %collective-permute-done.rest_1_.rest_5_, bf16[32,8192]{1,0:T(8,128)(2,1)} %collective-permute-done.1.rest_2_.rest_6_, ...), custom_call_target="tpu_custom_call" | custom-call | flops 536870912 | bytes 2097152 | tf_op jit(solution)/shard_map/gram/pallas_call | solution.py:170
  107.5 1.2 collective-permute-done.6
  109.5 7.9 %all-to-all-start = ((f32[16,2,24,128]{3,2,1,0:T(8,128)}), f32[16,2,24,128]{3,2,1,0:T(8,128)}, u32[]{:S(2)}, u32[]{:S(2)}) async-start(f32[16,2,24,128]{3,2,1,0:T(8,128)} %broadcast_in_dim.6), calls=%async_computation | async-start | bytes 786432 | tf_op jit(solution)/shard_map/all_to_all | solution.py:401
  117.4 1.0 copy-done.4
  118.5 10.5 %modes.2 = (bf16[4,2,8,16384]{3,2,1,0:T(8,128)(2,1)}, f32[8,128]{1,0:T(8,128)S(1)}) custom-call(s32[3]{0:T(128)S(1)} %pad_add_fusion.place_ref, f32[4,2,8,128]{3,2,1,0:T(8,128)S(1)} %copy-done.8, f32[1,16384]{1,0:T(1,128)S(1)} %bitcast.13, s32[1,16384]{1,0:T(1,128)S(1)} %bitcast.15, f32[16,2,24,128]{3,2,1,0:T(8,128)} %all-to-all-done.1.sum_ref, ...), custom_call_target="tpu_custom_call" | custom-call | flops 2073741824 | bytes 5242880 | tf_op jit(solution)/shard_map/modes/pallas_call | solution.py:337
  129.0 10.7 %modes.3 = (bf16[4,2,8,16384]{3,2,1,0:T(8,128)(2,1)}, f32[8,128]{1,0:T(8,128)S(1)}) custom-call(s32[3]{0:T(128)S(1)} %pad_add_fusion.place_ref, f32[4,2,8,128]{3,2,1,0:T(8,128)S(1)} %copy-done.8, f32[1,16384]{1,0:T(1,128)S(1)} %bitcast.14, s32[1,16384]{1,0:T(1,128)S(1)} %bitcast.16, ...), custom_call_target="tpu_custom_call", output_to_operand_aliasing={{0}: (13, {})} | custom-call | flops 2073741824 | bytes 5242880 | tf_op jit(solution)/shard_map/modes/pallas_call | solution.py:337
  139.7 1.2 collective-permute-done.14
  140.9 14.7 %all_to_all.15.in_ref = f32[16,8,128]{2,1,0:T(8,128)} all-to-all(f32[16,8,128]{2,1,0:T(8,128)S(1)} %broadcast_in_dim.8), channel_id=1, replica_groups=mesh['z'=4,'x'=4,'core'=2,'blk'=4] {'z','x'}, dimensions={0} | all-to-all | bytes 131072 | tf_op jit(solution)/shard_map/all_to_all | solution.py:401
  155.7 1.6 %energy.1 = f32[4,8,384]{2,1,0:T(8,128)} custom-call(f32[16,8,128]{2,1,0:T(8,128)} %all_to_all.15.in_ref), custom_call_target="tpu_custom_call" | custom-call | tf_op jit(solution)/shard_map/energy/pallas_call | solution.py:390
  (43 shorter events, 2.6 us)
Async XLA Ops:
  0.7 1.0 copy-start
  8.8 0.8 copy-start.5
  9.6 0.8 copy-start.6
  10.3 23.6 %collective-permute-start.10 = (bf16[32,8192]{1,0:T(8,128)(2,1)S(1)}, bf16[32,8192]{1,0:T(8,128)(2,1)S(1)}, u32[]{:S(2)}, u32[]{:S(2)}) collective-permute-start(bf16[32,8192]{1,0:T(8,128)(2,1)S(1)} %get-tuple-element.35), channel_id=1, source_target_pairs={{0,1},{1,2},{2,3},{3,0},{4,5},{5,6},{6,7},{7,4},{8,9},{9,10},{10,1... | collective-permute-start | bytes 1572872 | tf_op jit(solution)/shard_map/ppermute | solution.py:422
  11.9 22.0 %collective-permute-start.11 = (bf16[32,8192]{1,0:T(8,128)(2,1)}, bf16[32,8192]{1,0:T(8,128)(2,1)S(1)}, u32[]{:S(2)}, u32[]{:S(2)}) collective-permute-start(bf16[32,8192]{1,0:T(8,128)(2,1)} %get-tuple-element.36), channel_id=1, source_target_pairs={{0,2},{1,3},{2,0},{3,1},{4,6},{5,7},{6,4},{7,5},{8,10},{9,11},{10,... | collective-permute-start | bytes 1572872 | tf_op jit(solution)/shard_map/ppermute | solution.py:422
  12.8 25.1 %copy-start.9 = (s32[4,8]{1,0:T(4,128)S(1)}, s32[4,8]{1,0:T(4,128)}, u32[]{:S(2)}) copy-start(s32[4,8]{1,0:T(4,128)} %param.10) | copy-start | bytes 388
  12.8 35.5 %copy-start.1 = (f32[16384]{0:T(1024)S(1)}, f32[16384]{0:T(1024)}, u32[]{:S(2)}) copy-start(f32[16384]{0:T(1024)} %param.8) | copy-start | bytes 196612
  12.8 35.5 %collective-permute-start.12 = (bf16[32,8192]{1,0:T(8,128)(2,1)}, bf16[32,8192]{1,0:T(8,128)(2,1)S(1)}, u32[]{:S(2)}, u32[]{:S(2)}) collective-permute-start(bf16[32,8192]{1,0:T(8,128)(2,1)} %get-tuple-element.37), channel_id=1, source_target_pairs={{0,3},{1,0},{2,1},{3,2},{4,7},{5,4},{6,5},{7,6},{8,11},{9,8},{10,9... | collective-permute-start | bytes 1572872 | tf_op jit(solution)/shard_map/ppermute | solution.py:422
  22.7 0.8 copy-start.2
  23.5 32.9 %collective-permute-start.7 = (bf16[32,8192]{1,0:T(8,128)(2,1)}, bf16[32,8192]{1,0:T(8,128)(2,1)}, u32[]{:S(2)}, u32[]{:S(2)}) collective-permute-start(bf16[32,8192]{1,0:T(8,128)(2,1)} %get-tuple-element.31), channel_id=1, source_target_pairs={{0,1},{1,2},{2,3},{3,0},{4,5},{5,6},{6,7},{7,4},{8,9},{9,10},{10,1... | collective-permute-start | bytes 1572872 | tf_op jit(solution)/shard_map/ppermute | solution.py:422
  23.5 32.9 %collective-permute-start.8 = (bf16[32,8192]{1,0:T(8,128)(2,1)}, bf16[32,8192]{1,0:T(8,128)(2,1)}, u32[]{:S(2)}, u32[]{:S(2)}) collective-permute-start(bf16[32,8192]{1,0:T(8,128)(2,1)} %get-tuple-element.32), channel_id=1, source_target_pairs={{0,2},{1,3},{2,0},{3,1},{4,6},{5,7},{6,4},{7,5},{8,10},{9,11},{10,... | collective-permute-start | bytes 1572872 | tf_op jit(solution)/shard_map/ppermute | solution.py:422
  33.9 28.5 %collective-permute-start.9 = (bf16[32,8192]{1,0:T(8,128)(2,1)}, bf16[32,8192]{1,0:T(8,128)(2,1)}, u32[]{:S(2)}, u32[]{:S(2)}) collective-permute-start(bf16[32,8192]{1,0:T(8,128)(2,1)} %get-tuple-element.33), channel_id=1, source_target_pairs={{0,3},{1,0},{2,1},{3,2},{4,7},{5,4},{6,5},{7,6},{8,11},{9,8},{10,9... | collective-permute-start | bytes 1572872 | tf_op jit(solution)/shard_map/ppermute | solution.py:422
  33.9 45.0 %collective-permute-start.3 = (bf16[32,8192]{1,0:T(8,128)(2,1)}, bf16[32,8192]{1,0:T(8,128)(2,1)}, u32[]{:S(2)}, u32[]{:S(2)}) collective-permute-start(bf16[32,8192]{1,0:T(8,128)(2,1)} %copy-done.6), channel_id=1, source_target_pairs={{0,1},{1,2},{2,3},{3,0},{4,5},{5,6},{6,7},{7,4},{8,9},{9,10},{10,1... | collective-permute-start | bytes 1572872 | tf_op jit(solution)/shard_map/ppermute | solution.py:422
  38.0 24.4 %copy-start.3 = (bf16[32,8192]{1,0:T(8,128)(2,1)S(1)}, bf16[32,8192]{1,0:T(8,128)(2,1)}, u32[]{:S(2)}) copy-start(bf16[32,8192]{1,0:T(8,128)(2,1)} %copy-done.2) | copy-start | bytes 1572868
  48.3 44.4 %collective-permute-start.4 = (bf16[32,8192]{1,0:T(8,128)(2,1)}, bf16[32,8192]{1,0:T(8,128)(2,1)}, u32[]{:S(2)}, u32[]{:S(2)}) collective-permute-start(bf16[32,8192]{1,0:T(8,128)(2,1)} %copy-done.5), channel_id=1, source_target_pairs={{0,2},{1,3},{2,0},{3,1},{4,6},{5,7},{6,4},{7,5},{8,10},{9,11},{10,... | collective-permute-start | bytes 1572872 | tf_op jit(solution)/shard_map/ppermute | solution.py:422
  56.4 36.3 %collective-permute-start.5 = (bf16[32,8192]{1,0:T(8,128)(2,1)}, bf16[32,8192]{1,0:T(8,128)(2,1)}, u32[]{:S(2)}, u32[]{:S(2)}) collective-permute-start(bf16[32,8192]{1,0:T(8,128)(2,1)} %get-tuple-element.29), channel_id=1, source_target_pairs={{0,3},{1,0},{2,1},{3,2},{4,7},{5,4},{6,5},{7,6},{8,11},{9,8},{10,9... | collective-permute-start | bytes 1572872 | tf_op jit(solution)/shard_map/ppermute | solution.py:422
  64.8 14.0 %collective-permute-start.13 = (f32[2,24,128]{2,1,0:T(8,128)S(1)}, f32[2,24,128]{2,1,0:T(8,128)S(1)}, u32[]{:S(2)}, u32[]{:S(2)}) collective-permute-start(f32[2,24,128]{2,1,0:T(8,128)S(1)} %gram.7), channel_id=1, source_target_pairs={{0,4},{4,0},{1,5},{5,1},{2,6},{6,2},{3,7},{7,3},{8,12},{12,8},{9,1... | collective-permute-start | bytes 73736 | tf_op jit(solution)/shard_map/ppermute | solution.py:398
  64.9 30.2 %collective-permute-start = (bf16[32,8192]{1,0:T(8,128)(2,1)}, bf16[32,8192]{1,0:T(8,128)(2,1)}, u32[]{:S(2)}, u32[]{:S(2)}) collective-permute-start(bf16[32,8192]{1,0:T(8,128)(2,1)} %get-tuple-element.23), channel_id=1, source_target_pairs={{0,1},{1,2},{2,3},{3,0},{4,5},{5,6},{6,7},{7,4},{8,9},{9,10},{10,1... | collective-permute-start | bytes 1572872 | tf_op jit(solution)/shard_map/ppermute | solution.py:422
  78.9 17.3 %collective-permute-start.1 = (bf16[32,8192]{1,0:T(8,128)(2,1)}, bf16[32,8192]{1,0:T(8,128)(2,1)}, u32[]{:S(2)}, u32[]{:S(2)}) collective-permute-start(bf16[32,8192]{1,0:T(8,128)(2,1)} %get-tuple-element.24), channel_id=1, source_target_pairs={{0,2},{1,3},{2,0},{3,1},{4,6},{5,7},{6,4},{7,5},{8,10},{9,11},{10,... | collective-permute-start | bytes 1572872 | tf_op jit(solution)/shard_map/ppermute | solution.py:422
  78.9 26.1 %collective-permute-start.2 = (bf16[32,8192]{1,0:T(8,128)(2,1)}, bf16[32,8192]{1,0:T(8,128)(2,1)}, u32[]{:S(2)}, u32[]{:S(2)}) collective-permute-start(bf16[32,8192]{1,0:T(8,128)(2,1)} %get-tuple-element.25), channel_id=1, source_target_pairs={{0,3},{1,0},{2,1},{3,2},{4,7},{5,4},{6,5},{7,6},{8,11},{9,8},{10,9... | collective-permute-start | bytes 1572872 | tf_op jit(solution)/shard_map/ppermute | solution.py:422
  84.7 24.0 %all-to-all-start.1 = ((f32[16,2,24,128]{3,2,1,0:T(8,128)}), f32[16,2,24,128]{3,2,1,0:T(8,128)}, u32[]{:S(2)}, u32[]{:S(2)}) async-start(f32[16,2,24,128]{3,2,1,0:T(8,128)} %broadcast_in_dim.7), calls=%async_computation.1 | async-start | bytes 786432 | tf_op jit(solution)/shard_map/all_to_all | solution.py:401
  95.1 22.3 %copy-start.7 = (s32[16384]{0:T(1024)S(1)}, s32[16384]{0:T(1024)}, u32[]{:S(2)}) copy-start(s32[16384]{0:T(1024)} %param.9) | copy-start | bytes 196612
  95.1 22.3 %copy-start.8 = (f32[4,2,8,128]{3,2,1,0:T(8,128)S(1)}, f32[4,2,8,128]{3,2,1,0:T(8,128)}, u32[]{:S(2)}) copy-start(f32[4,2,8,128]{3,2,1,0:T(8,128)} %constant.28.clone.start_ref) | copy-start | bytes 98308
  107.4 1.3 collective-permute-start.6
  109.5 19.5 %all-to-all-start = ((f32[16,2,24,128]{3,2,1,0:T(8,128)}), f32[16,2,24,128]{3,2,1,0:T(8,128)}, u32[]{:S(2)}, u32[]{:S(2)}) async-start(f32[16,2,24,128]{3,2,1,0:T(8,128)} %broadcast_in_dim.6), calls=%async_computation | async-start | bytes 786432 | tf_op jit(solution)/shard_map/all_to_all | solution.py:401
  117.4 1.0 copy-start.4
  139.7 1.2 collective-permute-start.14

commit v2 on v1

--- a/solution.py
+++ b/solution.py
@@ -1,3 +1,4 @@
+import functools
 import math
 
 import jax
@@ -16,6 +17,7 @@
 WINDOW = 64
 GROUPS = 4
 PER_GROUP = 8
+QUAD = 4
 OWNED = 4
 PAIR = 2
 HALVES = 2
@@ -25,7 +27,8 @@
 LEVELS = DEGREES // DEVICES
 F32 = jnp.float32
 BF16 = jnp.bfloat16
-VMEM = 48 * 1024 * 1024
+LARGE = 60 * 1024 * 1024
+SMALL = 24 * 1024 * 1024
 
 
 def dft_table():
@@ -42,86 +45,104 @@
 
 def spectral_lhs():
     table = dft_table()
-    lhs = np.zeros((GROUPS, OWNED, 2, PER_GROUP, PER_GROUP, WINDOW), dtype=BF16)
+    lhs = np.zeros((GROUPS, OWNED, 2, QUAD, QUAD, WINDOW), dtype=BF16)
     for owner in range(GROUPS):
         for i in range(OWNED):
-            for b in range(PER_GROUP):
+            for b in range(QUAD):
                 lhs[owner, i, :, b, b, :] = table[OWNED * owner + i]
-    return lhs.reshape(GROUPS, OWNED * 2 * PER_GROUP, PER_GROUP * WINDOW)
+    return lhs.reshape(GROUPS, OWNED * 2 * QUAD, QUAD * WINDOW)
 
 
 def start_basis():
     b = np.arange(BLOCKS, dtype=np.float32)
     j = np.arange(MODES, dtype=np.float32)
     v0 = np.cos(np.float32(math.pi) * (j[:, None] + np.float32(0.5)) * (b[None, :] + np.float32(0.5)) / np.float32(BLOCKS))
-    v0 = (v0 * np.float32(math.sqrt(2.0 / BLOCKS))).reshape(MODES, GROUPS, PER_GROUP)
-    out = np.zeros((GROUPS, 2, MODES, 2, GROUPS, 2, PER_GROUP), dtype=np.float32)
+    v0 = (v0 * np.float32(math.sqrt(2.0 / BLOCKS))).reshape(MODES, GROUPS, 2, QUAD)
+    out = np.zeros((GROUPS, 2, MODES, 2, GROUPS, 2, 2, QUAD), dtype=np.float32)
     for y in range(GROUPS):
         for slot in range(GROUPS):
             for part in range(2):
-                out[y, part, :, :, slot, part, :] = v0[:, None, (y - slot) % GROUPS]
+                out[y, part, :, :, slot, :, part, :] = v0[:, None, (y - slot) % GROUPS]
     return out.reshape(GROUPS, 2, MODES, 128)
 
 
-def spectra_call(place, snapshots, half, tile):
+def spectra_call(snapshots, half, tile):
     blocks_dev, window_len, rows_dev = snapshots.shape
-    rows = OWNED * 2 * PER_GROUP
-    depth = blocks_dev * window_len
+    rows = OWNED * 2 * QUAD
+    depth = QUAD * window_len
     part = rows_dev // HALVES
     steps = part // tile
     lhs_all = jnp.asarray(spectral_lhs())
 
-    def kernel(place_ref, lhs_ref, x_ref, *rest):
+    def kernel(lhs_ref, x_ref, *rest):
         outs, lhs = rest[:-1], rest[-1]
 
         @pl.when(pl.program_id(0) == 0)
         def _():
             for slot in range(GROUPS):
-                owner = lax.rem(place_ref[0] + slot, GROUPS)
+                owner = lax.rem(lax.axis_index("blk") + slot, GROUPS)
                 lhs[slot * rows : (slot + 1) * rows, :] = lhs_ref[owner]
 
-        data = x_ref[...].reshape(depth, tile)
-        result = jnp.dot(lhs[...], data, preferred_element_type=F32).astype(BF16)
+        data = x_ref[...].reshape(2, depth, tile)
+        result = [jnp.dot(lhs[...], data[q], preferred_element_type=F32) for q in range(2)]
         for n, out in enumerate(outs):
-            out[...] = result[n * 32 : (n + 1) * 32]
+            out[...] = jnp.concatenate(
+                [
+                    result[q][8 * m : 8 * m + 8]
+                    for m in range(PAIR * n, PAIR * n + PAIR)
+                    for q in range(2)
+                ],
+                axis=0,
+            ).astype(BF16)
 
     out = pl.pallas_call(
         kernel,
-        grid_spec=pltpu.PrefetchScalarGridSpec(
-            num_scalar_prefetch=1,
-            grid=(steps,),
-            in_specs=[
-                pl.BlockSpec((GROUPS, rows, depth), lambda n, p: (0, 0, 0)),
-                pl.BlockSpec((blocks_dev, window_len, tile), lambda n, p: (0, 0, n + half * steps)),
-            ],
-            out_specs=[pl.BlockSpec((32, tile), lambda n, p: (0, n))] * (GROUPS * PAIR),
-            scratch_shapes=[pltpu.VMEM((GROUPS * rows, depth), BF16)],
-        ),
+        grid=(steps,),
+        in_specs=[
+            pl.BlockSpec((GROUPS, rows, depth), lambda n: (0, 0, 0)),
+            pl.BlockSpec((blocks_dev, window_len, tile), lambda n: (0, 0, n + half * steps)),
+        ],
+        out_specs=[pl.BlockSpec((32, tile), lambda n: (0, n))] * (GROUPS * PAIR),
+        scratch_shapes=[pltpu.VMEM((GROUPS * rows, depth), BF16)],
         out_shape=[jax.ShapeDtypeStruct((32, part), BF16)] * (GROUPS * PAIR),
-        compiler_params=pltpu.CompilerParams(vmem_limit_bytes=VMEM),
+        compiler_params=pltpu.CompilerParams(vmem_limit_bytes=LARGE),
         cost_estimate=pl.CostEstimate(
-            flops=2 * GROUPS * rows * depth * part,
-            bytes_accessed=2 * (depth + GROUPS * rows) * part,
+            flops=4 * GROUPS * rows * depth * part,
+            bytes_accessed=4 * (depth + GROUPS * rows) * part,
             transcendentals=0,
         ),
         name="spectra",
-    )(place, lhs_all, snapshots)
+    )(lhs_all, snapshots)
     return [[out[slot * PAIR + i] for slot in range(GROUPS)] for i in range(PAIR)]
 
 
 def odd_lanes(shape):
-    return (lax.broadcasted_iota(jnp.int32, shape, len(shape) - 1) & 8) == 8
+    return (lax.broadcasted_iota(jnp.int32, shape, len(shape) - 1) & QUAD) == QUAD
 
 
 def low_lanes(shape):
     return lax.broadcasted_iota(jnp.int32, shape, len(shape) - 1) < 64
 
 
-def turned(value):
+def low_rows(shape):
+    return lax.broadcasted_iota(jnp.int32, shape, len(shape) - 2) % 8 < QUAD
+
+
+def other_lanes(value):
     axis = value.ndim - 1
     return jnp.where(
-        odd_lanes(value.shape), pltpu.roll(value, 8, axis), -pltpu.roll(value, 120, axis)
+        odd_lanes(value.shape), pltpu.roll(value, QUAD, axis), pltpu.roll(value, 128 - QUAD, axis)
     )
+
+
+def other_rows(value):
+    rows = value.shape[0]
+    return pltpu.roll(value.reshape(rows // 8, 8, 128), QUAD, 1).reshape(rows, 128)
+
+
+def turned(value):
+    other = other_lanes(value)
+    return jnp.where(odd_lanes(value.shape), other, -other)
 
 
 def gram_call(half, pieces, weights, pivot_local, before, tile):
@@ -152,14 +173,10 @@
             for f in range(PAIR):
                 total = acc[f]
                 total = total + pltpu.roll(total, 64, 1)
-                g = total[:64].reshape(GROUPS, 2, PER_GROUP, 128)
-                upper = g[:, 0].reshape(BLOCKS, 128)
-                lower = g[:, 1].reshape(BLOCKS, 128)
-                cross = jnp.where(
-                    odd_lanes(upper.shape),
-                    pltpu.roll(lower, 8, 1) - upper,
-                    upper + pltpu.roll(lower, 120, 1),
-                )
+                gram = total[:64]
+                same = low_rows(gram.shape) != odd_lanes(gram.shape)
+                cross = other_lanes(other_rows(gram)) + jnp.where(same, gram, -gram)
+                cross = jnp.where(low_rows((32, 128)), cross[:32], other_rows(cross[32:]))
                 packed = jnp.where(low_lanes((16, 128)), cross[:16], cross[16:])
                 packed = jnp.concatenate([packed, total[64:72]], axis=0)
                 if before is not None:
@@ -179,7 +196,7 @@
         out_specs=whole,
         out_shape=jax.ShapeDtypeStruct((PAIR, 24, 128), F32),
         scratch_shapes=[pltpu.VMEM((PAIR, 80, 128), F32)],
-        compiler_params=pltpu.CompilerParams(vmem_limit_bytes=VMEM),
+        compiler_params=pltpu.CompilerParams(vmem_limit_bytes=SMALL),
         cost_estimate=pl.CostEstimate(
             flops=2 * PAIR * 64 * 256 * part, bytes_accessed=4 * 64 * part, transcendentals=0
         ),
@@ -197,11 +214,11 @@
 
 def right_side(cross):
     turn = turned(cross)
+    first = low_rows(cross.shape)
     full = jnp.concatenate(
         [
-            piece
-            for g in range(GROUPS)
-            for piece in (cross[8 * g : 8 * g + 8], turn[8 * g : 8 * g + 8])
+            jnp.where(first, cross, other_rows(turn)),
+            jnp.where(first, other_rows(cross), turn),
         ],
         axis=0,
     )
@@ -284,34 +301,34 @@
             expand[:, 8:] = lower
             energy_ref[...] = jnp.zeros_like(energy_ref) if before is None else rest[1][...]
 
-        w = w_ref[...]
-        base = place_ref[1] + n * bands
-        lane = lax.broadcasted_iota(jnp.int32, (MODES, 128), 1)
-        first = n < part_steps
-        for f in range(PAIR):
-            rows = slice(16 * f, 16 * f + 16)
-            x = jnp.concatenate(
-                [
-                    jnp.where(first, x_refs[k][rows], x_refs[GROUPS + k][rows])
-                    for k in range(GROUPS)
-                ],
-                axis=0,
-            )
-            psi = jnp.dot(expand[f][:, :64].astype(BF16), x, preferred_element_type=F32)
-            s_re = phase[0, f, :, :1]
-            s_im = phase[1, f, :, :1]
-            p_re, p_im = psi[:8], psi[8:]
-            out_re = p_re * s_re + p_im * s_im
-            out_im = p_im * s_re - p_re * s_im
-            modes_ref[f, 0] = out_re.astype(BF16)
-            modes_ref[f, 1] = out_im.astype(BF16)
-            power = w * (out_re * out_re + out_im * out_im)
-            for m in range(bands + 1):
-                level = jnp.sum(
-                    jnp.where(deg_ref[...] == base + m, power, 0.0), axis=1, keepdims=True
+        def tile_of(half):
+            w = w_ref[...]
+            lane = lax.broadcasted_iota(jnp.int32, (MODES, 128), 1)
+            base = place_ref[1] + n * bands
+            hits = [deg_ref[...] == base + m for m in range(bands + 1)]
+            total = jnp.zeros((MODES, 128), F32)
+            for f in range(PAIR):
+                rows = slice(16 * f, 16 * f + 16)
+                x = jnp.concatenate(
+                    [r[rows] for r in x_refs[GROUPS * half : GROUPS * half + GROUPS]], axis=0
                 )
-                spot = (pair * PAIR + f) * 32 + place_ref[2] + n * bands + m
-                energy_ref[...] += jnp.where(lane == spot, level * (DEGREES / row_count), 0.0)
+                psi = jnp.dot(expand[f][:, :64].astype(BF16), x, preferred_element_type=F32)
+                s_re = phase[0, f, :, :1]
+                s_im = phase[1, f, :, :1]
+                p_re, p_im = psi[:8], psi[8:]
+                out_re = p_re * s_re + p_im * s_im
+                out_im = p_im * s_re - p_re * s_im
+                modes_ref[f, 0] = out_re.astype(BF16)
+                modes_ref[f, 1] = out_im.astype(BF16)
+                power = w * (out_re * out_re + out_im * out_im)
+                for m in range(bands + 1):
+                    level = jnp.sum(jnp.where(hits[m], power, 0.0), axis=1, keepdims=True)
+                    spot = (pair * PAIR + f) * 32 + place_ref[2] + n * bands + m
+                    total = total + jnp.where(lane == spot, level * (DEGREES / row_count), 0.0)
+            energy_ref[...] += total
+
+        for half in range(HALVES):
+            pl.when(n // part_steps == half)(functools.partial(tile_of, half))
 
     in_specs = [
         pl.BlockSpec((GROUPS, 2, MODES, 128), lambda n, p: (0, 0, 0, 0)),
@@ -354,7 +371,7 @@
             jax.ShapeDtypeStruct((MODES, 128), F32),
         ],
         input_output_aliases=aliases,
-        compiler_params=pltpu.CompilerParams(vmem_limit_bytes=VMEM),
+        compiler_params=pltpu.CompilerParams(vmem_limit_bytes=SMALL),
         cost_estimate=pl.CostEstimate(
             flops=2 * PAIR * 64 * 256 * rows_dev + 10**9,
             bytes_accessed=PAIR * 2 * 80 * rows_dev,
@@ -401,6 +418,10 @@
     return lax.all_to_all(spread, ("z", "x"), 0, 0, tiled=True)
 
 
+def after(value, first):
+    return lax.optimization_barrier((value, first))[0]
+
+
 def per_device(snapshots, weights, degrees, pivots):
     rows_dev = snapshots.shape[2]
     row_count = rows_dev * DEVICES
@@ -413,7 +434,7 @@
     degrees = degrees.reshape(1, rows_dev)
     start = jnp.asarray(start_basis())
 
-    halves = [spectra_call(place, snapshots, half, 2048) for half in range(HALVES)]
+    halves = [spectra_call(snapshots, half, 2048) for half in range(HALVES)]
     pieces = {}
     for pair in range(PAIR):
         for half in range(HALVES):
@@ -426,8 +447,9 @@
     for pair in range(PAIR):
         gram = None
         for half in range(HALVES):
+            known = weights if before is None or half < HALVES - 1 else after(weights, before[1])
             gram = gram_call(
-                half, pieces[pair, half], weights, pivot_local[PAIR * pair : PAIR * pair + PAIR], gram, 4096
+                half, pieces[pair, half], known, pivot_local[PAIR * pair : PAIR * pair + PAIR], gram, 4096
             )
         before = modes_call(
             pair, place, start, weights, degrees, gather_chips(gram),

time: 158 us -> 151 us (0.956)
  blocking collectives: 14.7 us -> 29 us
  starting transfers between devices: 33.9 us -> 24.2 us
  waiting for transfers between devices: 55.5 us -> 49 us
  local copies, waits for them, and re-layouts: 6.11 us -> 2.93 us
    all_to_all x1 -> x2, blocking collectives: 14.7 us -> 29 us  [gather_chips(): return lax.all_to_all(spread, ('z', 'x'), 0, 0, tiled=True)]
    all_to_all x2 -> x1, starting transfers between devices: 15.8 us -> 7.93 us  [gather_chips(): return lax.all_to_all(spread, ('z', 'x'), 0, 0, tiled=True)]
    ppermute x12, waiting for transfers between devices: 53.2 us -> 45.5 us  [per_device(): lax.ppermute(sent[k], 'blk', [(g, (g + k) % GROUPS) for g in range(GROUPS)])]
    unnamed x20 -> x22, local copies, waits for them, and re-layouts: 4.38 us -> 1.94 us
    ppermute x12, starting transfers between devices: 17.9 us -> 16.1 us  [per_device(): lax.ppermute(sent[k], 'blk', [(g, (g + k) % GROUPS) for g in range(GROUPS)])]
  transfers between devices with their start and end apart: 17 -> 16, of which waited for: 9 -> 8; matrix products, arithmetic and copies ran while one was open for 1% -> 1% of each run, Pallas kernels for 17% -> 15%
where the time goes in v2:
time: 151 us
  waiting for transfers between devices  49 us (32%)
  Pallas kernels  44.7 us (30%)
  blocking collectives  29 us (19%)
  starting transfers between devices  24.2 us (16%)
  local copies, waits for them, and re-layouts  2.93 us (2%)
    ppermute x12, waiting for transfers between devices, per_device(): lax.ppermute(sent[k], 'blk', [(g, (g + k) % GROUPS) for g in range(GROUPS)])  45.5 us
    all_to_all x2, blocking collectives, gather_chips(): return lax.all_to_all(spread, ('z', 'x'), 0, 0, tiled=True)  29 us
    pallas_call x2, Pallas kernels, modes_call(): pl.pallas_call(kernel, grid_spec=pltpu.PrefetchScalarGridSpec(num_scalar_...  21.4 us
    ppermute x12, starting transfers between devices, per_device(): lax.ppermute(sent[k], 'blk', [(g, (g + k) % GROUPS) for g in range(GROUPS)])  16.1 us
    pallas_call x2, Pallas kernels, spectra_call(): pl.pallas_call(kernel, grid=(steps,), in_specs=[pl.BlockSpec((GROUPS, row...  13 us
    pallas_call x4, Pallas kernels, gram_call(): pl.pallas_call(kernel, grid=(steps,), in_specs=[pl.BlockSpec((PAIR, MODES...  8.68 us
    all_to_all x1, starting transfers between devices, gather_chips(): return lax.all_to_all(spread, ('z', 'x'), 0, 0, tiled=True)  7.93 us
    ppermute x3, waiting for transfers between devices, gather_chips(): value = value + lax.ppermute(value, 'core', [(0, 1), (1, 0)])  3.53 us
  transfers between devices with their start and end apart: 16, of which 8 were waited for; matrix products, arithmetic and copies ran while one was open for 1% of the time, Pallas kernels for 15%

profile of v2, /device:TPU:8, one launch (start us, length us, event | category | flops | bytes accessed | tf_op | source)
XLA Modules:
  0.0 150.8 jit_solution(12258348243328434247)
XLA Ops:
  0.6 6.6 %spectra.3 = (bf16[32,8192]{1,0:T(8,128)(2,1)}, bf16[32,8192]{1,0:T(8,128)(2,1)}, bf16[32,8192]{1,0:T(8,128)(2,1)}, bf16[32,8192]{1,0:T(8,128)(2,1)}, bf16[32,81...) custom-call(bf16[4,32,256]{2,1,0:T(8,128)(2,1)} %constant.29.clone.lhs_ref, ...), custom_call_target="tpu_custom_call" | custom-call | flops 1073741824 | bytes 12582912 | tf_op jit(solution)/shard_map/spectra/pallas_call | solution.py:98
  7.2 1.6 %collective-permute-start.3 = (bf16[32,8192]{1,0:T(8,128)(2,1)}, bf16[32,8192]{1,0:T(8,128)(2,1)S(1)}, u32[]{:S(2)}, u32[]{:S(2)}) collective-permute-start(bf16[32,8192]{1,0:T(8,128)(2,1)} %get-tuple-element.28), channel_id=1, source_target_pairs={{0,1},{1,2},{2,3},{3,0},{4,5},{5,6},{6,7},{7,4},{8,9},{9,10},{10,1... | collective-permute-start | bytes 1572872 | tf_op jit(solution)/shard_map/ppermute | solution.py:443
  8.8 0.9 collective-permute-start.4
  9.6 2.5 %collective-permute-start.5 = (bf16[32,8192]{1,0:T(8,128)(2,1)}, bf16[32,8192]{1,0:T(8,128)(2,1)S(1)}, u32[]{:S(2)}, u32[]{:S(2)}) collective-permute-start(bf16[32,8192]{1,0:T(8,128)(2,1)} %get-tuple-element.30), channel_id=1, source_target_pairs={{0,3},{1,0},{2,1},{3,2},{4,7},{5,4},{6,5},{7,6},{8,11},{9,8},{10,9... | collective-permute-start | bytes 1572872 | tf_op jit(solution)/shard_map/ppermute | solution.py:443
  12.1 6.5 %spectra.2 = (bf16[32,8192]{1,0:T(8,128)(2,1)}, bf16[32,8192]{1,0:T(8,128)(2,1)}, bf16[32,8192]{1,0:T(8,128)(2,1)}, bf16[32,8192]{1,0:T(8,128)(2,1)}, bf16[32,81...) custom-call(bf16[4,32,256]{2,1,0:T(8,128)(2,1)} %constant.29.clone.lhs_ref, ...), custom_call_target="tpu_custom_call" | custom-call | flops 1073741824 | bytes 12582912 | tf_op jit(solution)/shard_map/spectra/pallas_call | solution.py:98
  18.7 3.4 %collective-permute-start.1 = (bf16[32,8192]{1,0:T(8,128)(2,1)}, bf16[32,8192]{1,0:T(8,128)(2,1)}, u32[]{:S(2)}, u32[]{:S(2)}) collective-permute-start(bf16[32,8192]{1,0:T(8,128)(2,1)} %get-tuple-element.25), channel_id=1, source_target_pairs={{0,2},{1,3},{2,0},{3,1},{4,6},{5,7},{6,4},{7,5},{8,10},{9,11},{10,... | collective-permute-start | bytes 1572872 | tf_op jit(solution)/shard_map/ppermute | solution.py:443
  22.1 10.2 %collective-permute-done.3.rest_1_ = bf16[32,8192]{1,0:T(8,128)(2,1)S(1)} collective-permute-done((bf16[32,8192]{1,0:T(8,128)(2,1)}, bf16[32,8192]{1,0:T(8,128)(2,1)S(1)}, u32[]{:S(2)}, u32[]{:S(2)}) %collective-permute-start.3) | collective-permute-done | bytes 524320 | tf_op jit(solution)/shard_map/ppermute | solution.py:443
  32.2 2.8 %collective-permute-start.10 = (bf16[32,8192]{1,0:T(8,128)(2,1)}, bf16[32,8192]{1,0:T(8,128)(2,1)}, u32[]{:S(2)}, u32[]{:S(2)}) collective-permute-start(bf16[32,8192]{1,0:T(8,128)(2,1)} %get-tuple-element.38), channel_id=1, source_target_pairs={{0,1},{1,2},{2,3},{3,0},{4,5},{5,6},{6,7},{7,4},{8,9},{9,10},{10,1... | collective-permute-start | bytes 1572872 | tf_op jit(solution)/shard_map/ppermute | solution.py:443
  35.1 10.1 %collective-permute-done.5.rest_3_ = bf16[32,8192]{1,0:T(8,128)(2,1)S(1)} collective-permute-done((bf16[32,8192]{1,0:T(8,128)(2,1)}, bf16[32,8192]{1,0:T(8,128)(2,1)S(1)}, u32[]{:S(2)}, u32[]{:S(2)}) %collective-permute-start.5) | collective-permute-done | bytes 524320 | tf_op jit(solution)/shard_map/ppermute | solution.py:443
  45.2 9.5 %collective-permute-done.rest_1_.rest_5_ = bf16[32,8192]{1,0:T(8,128)(2,1)S(1)} collective-permute-done((bf16[32,8192]{1,0:T(8,128)(2,1)}, bf16[32,8192]{1,0:T(8,128)(2,1)S(1)}, u32[]{:S(2)}, u32[]{:S(2)}) %collective-permute-start) | collective-permute-done | bytes 524320 | tf_op jit(solution)/shard_map/ppermute | solution.py:443
  54.7 0.9 copy-done.5
  55.5 0.1 copy.11.p_ref
  55.6 1.5 gram.4.rest_4_
  57.1 2.2 %collective-permute-done.2.rest_3_.rest_7_ = bf16[32,8192]{1,0:T(8,128)(2,1)} collective-permute-done((bf16[32,8192]{1,0:T(8,128)(2,1)}, bf16[32,8192]{1,0:T(8,128)(2,1)}, u32[]{:S(2)}, u32[]{:S(2)}) %collective-permute-start.2) | collective-permute-done | bytes 524320 | tf_op jit(solution)/shard_map/ppermute | solution.py:443
  59.3 2.4 %gram.5 = f32[2,24,128]{2,1,0:T(8,128)S(1)} custom-call(s32[2,8,1]{2,1,0:T(8,128)S(1)} %copy.11.p_ref, f32[1,16384]{1,0:T(1,128)S(1)} %bitcast.10, bf16[32,8192]{1,0:T(8,128)(2,1)S(1)} %copy-done.4, bf16[32,8192]{1,0:T(8,128)(2,1)S(1)} %copy-done.6, bf16[32,8192]{1,0:T(8,128)(2,1)} %collective-permute-done.1.rest_2_.rest_6_, ...), custom_call_target="tpu_custom_call" | custom-call | flops 536870912 | bytes 2097152 | tf_op jit(solution)/shard_map/gram/pallas_call | solution.py:187
  61.8 1.2 collective-permute-done.6
  63.0 0.8 broadcast_in_dim.6
  63.7 7.9 %all-to-all-start = ((f32[16,2,24,128]{3,2,1,0:T(8,128)}), f32[16,2,24,128]{3,2,1,0:T(8,128)}, u32[]{:S(2)}, u32[]{:S(2)}) async-start(f32[16,2,24,128]{3,2,1,0:T(8,128)} %broadcast_in_dim.6), calls=%async_computation | async-start | bytes 786432 | tf_op jit(solution)/shard_map/all_to_all | solution.py:418
  71.7 0.8 collective-permute-start.7
  72.5 1.6 %collective-permute-start.8 = (bf16[32,8192]{1,0:T(8,128)(2,1)}, bf16[32,8192]{1,0:T(8,128)(2,1)}, u32[]{:S(2)}, u32[]{:S(2)}) collective-permute-start(bf16[32,8192]{1,0:T(8,128)(2,1)} %get-tuple-element.35), channel_id=1, source_target_pairs={{0,2},{1,3},{2,0},{3,1},{4,6},{5,7},{6,4},{7,5},{8,10},{9,11},{10,... | collective-permute-start | bytes 1572872 | tf_op jit(solution)/shard_map/ppermute | solution.py:443
  74.0 2.5 %collective-permute-start.9 = (bf16[32,8192]{1,0:T(8,128)(2,1)}, bf16[32,8192]{1,0:T(8,128)(2,1)}, u32[]{:S(2)}, u32[]{:S(2)}) collective-permute-start(bf16[32,8192]{1,0:T(8,128)(2,1)} %get-tuple-element.36), channel_id=1, source_target_pairs={{0,3},{1,0},{2,1},{3,2},{4,7},{5,4},{6,5},{7,6},{8,11},{9,8},{10,9... | collective-permute-start | bytes 1572872 | tf_op jit(solution)/shard_map/ppermute | solution.py:443
  76.7 13.6 %collective-permute-done.12.rest_3_ = bf16[32,8192]{1,0:T(8,128)(2,1)} collective-permute-done((bf16[32,8192]{1,0:T(8,128)(2,1)}, bf16[32,8192]{1,0:T(8,128)(2,1)}, u32[]{:S(2)}, u32[]{:S(2)}) %collective-permute-start.12) | collective-permute-done | bytes 524320 | tf_op jit(solution)/shard_map/ppermute | solution.py:443
  90.3 2.4 %gram.6.rest_4_ = f32[2,24,128]{2,1,0:T(8,128)S(1)} custom-call(s32[2,8,1]{2,1,0:T(8,128)S(1)} %copy.13.p_ref, f32[1,16384]{1,0:T(1,128)S(1)} %bitcast.11, bf16[32,8192]{1,0:T(8,128)(2,1)S(1)} %copy-done.1, bf16[32,8192]{1,0:T(8,128)(2,1)} %collective-permute-done.10.rest_1_, bf16[32,8192]{1,0:T(8,128)(2,1)} %collective-permute-done.11.rest_2_, ...), custom_call_target="tpu_custom_call" | custom-call | flops 536870912 | bytes 2097152 | tf_op jit(solution)/shard_map/gram/pallas_call | solution.py:187
  92.8 1.0 copy-done.7
  93.8 10.6 %modes.2 = (bf16[4,2,8,16384]{3,2,1,0:T(8,128)(2,1)}, f32[8,128]{1,0:T(8,128)S(1)}) custom-call(s32[3]{0:T(128)S(1)} %pad_add_fusion.place_ref, f32[4,2,8,128]{3,2,1,0:T(8,128)S(1)} %copy-done.9, f32[1,16384]{1,0:T(1,128)S(1)} %bitcast.12, s32[1,16384]{1,0:T(1,128)S(1)} %bitcast.15, f32[16,2,24,128]{3,2,1,0:T(8,128)} %all-to-all-done.sum_ref, ...), custom_call_target="tpu_custom_call" | custom-call | flops 2073741824 | bytes 5242880 | tf_op jit(solution)/shard_map/modes/pallas_call | solution.py:354
  104.5 2.4 %gram.7 = f32[2,24,128]{2,1,0:T(8,128)S(1)} custom-call(s32[2,8,1]{2,1,0:T(8,128)S(1)} %copy.13.p_ref, f32[1,16384]{1,0:T(1,128)S(1)} %bitcast.13, bf16[32,8192]{1,0:T(8,128)(2,1)S(1)} %copy-done.2, bf16[32,8192]{1,0:T(8,128)(2,1)} %collective-permute-done.7.rest_1_.rest_5_, bf16[32,8192]{1,0:T(8,128)(2,1)} %collective-permute-done.8.rest_2_.rest_6_, ...), custom_call_target="tpu_custom_call" | custom-call | flops 536870912 | bytes 2097152 | tf_op jit(solution)/shard_map/gram/pallas_call | solution.py:187
  107.0 1.2 collective-permute-done.13
  108.3 18.1 %all_to_all.15.sum_ref = f32[16,2,24,128]{3,2,1,0:T(8,128)S(1)} all-to-all(f32[16,2,24,128]{3,2,1,0:T(8,128)S(1)} %broadcast_in_dim.7), channel_id=1, replica_groups=mesh['z'=4,'x'=4,'core'=2,'blk'=4] {'z','x'}, dimensions={0} | all-to-all | bytes 786432 | tf_op jit(solution)/shard_map/all_to_all | solution.py:418
  126.3 10.8 %modes.3 = (bf16[4,2,8,16384]{3,2,1,0:T(8,128)(2,1)}, f32[8,128]{1,0:T(8,128)S(1)}) custom-call(s32[3]{0:T(128)S(1)} %pad_add_fusion.place_ref, f32[4,2,8,128]{3,2,1,0:T(8,128)S(1)} %copy-done.9, f32[1,16384]{1,0:T(1,128)S(1)} %bitcast.14, s32[1,16384]{1,0:T(1,128)S(1)} %bitcast.16, ...), custom_call_target="tpu_custom_call", output_to_operand_aliasing={{0}: (13, {})} | custom-call | flops 2073741824 | bytes 5242880 | tf_op jit(solution)/shard_map/modes/pallas_call | solution.py:354
  137.1 1.2 collective-permute-done.14
  138.3 10.9 %all_to_all.16.in_ref = f32[16,8,128]{2,1,0:T(8,128)} all-to-all(f32[16,8,128]{2,1,0:T(8,128)S(1)} %broadcast_in_dim.8), channel_id=1, replica_groups=mesh['z'=4,'x'=4,'core'=2,'blk'=4] {'z','x'}, dimensions={0} | all-to-all | bytes 131072 | tf_op jit(solution)/shard_map/all_to_all | solution.py:418
  149.2 1.6 %energy.1 = f32[4,8,384]{2,1,0:T(8,128)} custom-call(f32[16,8,128]{2,1,0:T(8,128)} %all_to_all.16.in_ref), custom_call_target="tpu_custom_call" | custom-call | tf_op jit(solution)/shard_map/energy/pallas_call | solution.py:407
  (44 shorter events, 0.5 us)
Async XLA Ops:
  7.2 25.0 %collective-permute-start.3 = (bf16[32,8192]{1,0:T(8,128)(2,1)}, bf16[32,8192]{1,0:T(8,128)(2,1)S(1)}, u32[]{:S(2)}, u32[]{:S(2)}) collective-permute-start(bf16[32,8192]{1,0:T(8,128)(2,1)} %get-tuple-element.28), channel_id=1, source_target_pairs={{0,1},{1,2},{2,3},{3,0},{4,5},{5,6},{6,7},{7,4},{8,9},{9,10},{10,1... | collective-permute-start | bytes 1572872 | tf_op jit(solution)/shard_map/ppermute | solution.py:443
  8.8 23.5 %collective-permute-start.4 = (bf16[32,8192]{1,0:T(8,128)(2,1)}, bf16[32,8192]{1,0:T(8,128)(2,1)S(1)}, u32[]{:S(2)}, u32[]{:S(2)}) collective-permute-start(bf16[32,8192]{1,0:T(8,128)(2,1)} %get-tuple-element.29), channel_id=1, source_target_pairs={{0,2},{1,3},{2,0},{3,1},{4,6},{5,7},{6,4},{7,5},{8,10},{9,11},{10,... | collective-permute-start | bytes 1572872 | tf_op jit(solution)/shard_map/ppermute | solution.py:443
  9.6 25.4 %copy-start.10 = (s32[4,8]{1,0:T(4,128)S(1)}, s32[4,8]{1,0:T(4,128)}, u32[]{:S(2)}) copy-start(s32[4,8]{1,0:T(4,128)} %param.10) | copy-start | bytes 388
  9.6 46.0 %copy-start = (f32[16384]{0:T(1024)S(1)}, f32[16384]{0:T(1024)}, u32[]{:S(2)}) copy-start(f32[16384]{0:T(1024)} %param.8) | copy-start | bytes 196612
  9.6 46.0 %copy-start.3 = (bf16[32,8192]{1,0:T(8,128)(2,1)S(1)}, bf16[32,8192]{1,0:T(8,128)(2,1)}, u32[]{:S(2)}) copy-start(bf16[32,8192]{1,0:T(8,128)(2,1)} %get-tuple-element.27.rest_0_) | copy-start | bytes 1572868
  9.6 35.5 %collective-permute-start.5 = (bf16[32,8192]{1,0:T(8,128)(2,1)}, bf16[32,8192]{1,0:T(8,128)(2,1)S(1)}, u32[]{:S(2)}, u32[]{:S(2)}) collective-permute-start(bf16[32,8192]{1,0:T(8,128)(2,1)} %get-tuple-element.30), channel_id=1, source_target_pairs={{0,3},{1,0},{2,1},{3,2},{4,7},{5,4},{6,5},{7,6},{8,11},{9,8},{10,9... | collective-permute-start | bytes 1572872 | tf_op jit(solution)/shard_map/ppermute | solution.py:443
  18.6 40.7 %copy-start.4 = (bf16[32,8192]{1,0:T(8,128)(2,1)S(1)}, bf16[32,8192]{1,0:T(8,128)(2,1)}, u32[]{:S(2)}) copy-start(bf16[32,8192]{1,0:T(8,128)(2,1)} %get-tuple-element.23.rest_0_.rest_4_) | copy-start | bytes 1572868
  18.6 36.1 %collective-permute-start = (bf16[32,8192]{1,0:T(8,128)(2,1)}, bf16[32,8192]{1,0:T(8,128)(2,1)S(1)}, u32[]{:S(2)}, u32[]{:S(2)}) collective-permute-start(bf16[32,8192]{1,0:T(8,128)(2,1)} %get-tuple-element.24), channel_id=1, source_target_pairs={{0,1},{1,2},{2,3},{3,0},{4,5},{5,6},{6,7},{7,4},{8,9},{9,10},{10,1... | collective-permute-start | bytes 1572872 | tf_op jit(solution)/shard_map/ppermute | solution.py:443
  18.7 38.4 %collective-permute-start.1 = (bf16[32,8192]{1,0:T(8,128)(2,1)}, bf16[32,8192]{1,0:T(8,128)(2,1)}, u32[]{:S(2)}, u32[]{:S(2)}) collective-permute-start(bf16[32,8192]{1,0:T(8,128)(2,1)} %get-tuple-element.25), channel_id=1, source_target_pairs={{0,2},{1,3},{2,0},{3,1},{4,6},{5,7},{6,4},{7,5},{8,10},{9,11},{10,... | collective-permute-start | bytes 1572872 | tf_op jit(solution)/shard_map/ppermute | solution.py:443
  32.2 27.0 %collective-permute-start.2 = (bf16[32,8192]{1,0:T(8,128)(2,1)}, bf16[32,8192]{1,0:T(8,128)(2,1)}, u32[]{:S(2)}, u32[]{:S(2)}) collective-permute-start(bf16[32,8192]{1,0:T(8,128)(2,1)} %get-tuple-element.26), channel_id=1, source_target_pairs={{0,3},{1,0},{2,1},{3,2},{4,7},{5,4},{6,5},{7,6},{8,11},{9,8},{10,9... | collective-permute-start | bytes 1572872 | tf_op jit(solution)/shard_map/ppermute | solution.py:443
  32.2 41.8 %collective-permute-start.10 = (bf16[32,8192]{1,0:T(8,128)(2,1)}, bf16[32,8192]{1,0:T(8,128)(2,1)}, u32[]{:S(2)}, u32[]{:S(2)}) collective-permute-start(bf16[32,8192]{1,0:T(8,128)(2,1)} %get-tuple-element.38), channel_id=1, source_target_pairs={{0,1},{1,2},{2,3},{3,0},{4,5},{5,6},{6,7},{7,4},{8,9},{9,10},{10,1... | collective-permute-start | bytes 1572872 | tf_op jit(solution)/shard_map/ppermute | solution.py:443
  45.2 31.6 %collective-permute-start.11 = (bf16[32,8192]{1,0:T(8,128)(2,1)}, bf16[32,8192]{1,0:T(8,128)(2,1)}, u32[]{:S(2)}, u32[]{:S(2)}) collective-permute-start(bf16[32,8192]{1,0:T(8,128)(2,1)} %get-tuple-element.39), channel_id=1, source_target_pairs={{0,2},{1,3},{2,0},{3,1},{4,6},{5,7},{6,4},{7,5},{8,10},{9,11},{10,... | collective-permute-start | bytes 1572872 | tf_op jit(solution)/shard_map/ppermute | solution.py:443
  54.7 0.9 copy-start.5
  55.5 34.8 %collective-permute-start.12 = (bf16[32,8192]{1,0:T(8,128)(2,1)}, bf16[32,8192]{1,0:T(8,128)(2,1)}, u32[]{:S(2)}, u32[]{:S(2)}) collective-permute-start(bf16[32,8192]{1,0:T(8,128)(2,1)} %get-tuple-element.40), channel_id=1, source_target_pairs={{0,3},{1,0},{2,1},{3,2},{4,7},{5,4},{6,5},{7,6},{8,11},{9,8},{10,9... | collective-permute-start | bytes 1572872 | tf_op jit(solution)/shard_map/ppermute | solution.py:443
  55.6 3.7 %copy-start.6 = (bf16[32,8192]{1,0:T(8,128)(2,1)S(1)}, bf16[32,8192]{1,0:T(8,128)(2,1)}, u32[]{:S(2)}) copy-start(bf16[32,8192]{1,0:T(8,128)(2,1)} %copy-done.5) | copy-start | bytes 1572868
  57.1 33.2 %copy-start.1 = (bf16[32,8192]{1,0:T(8,128)(2,1)S(1)}, bf16[32,8192]{1,0:T(8,128)(2,1)}, u32[]{:S(2)}) copy-start(bf16[32,8192]{1,0:T(8,128)(2,1)} %get-tuple-element.37.rest_0_) | copy-start | bytes 1572868
  61.6 31.1 %copy-start.8 = (s32[16384]{0:T(1024)S(1)}, s32[16384]{0:T(1024)}, u32[]{:S(2)}) copy-start(s32[16384]{0:T(1024)} %param.9) | copy-start | bytes 196612
  61.7 31.1 %copy-start.9 = (f32[4,2,8,128]{3,2,1,0:T(8,128)S(1)}, f32[4,2,8,128]{3,2,1,0:T(8,128)}, u32[]{:S(2)}) copy-start(f32[4,2,8,128]{3,2,1,0:T(8,128)} %constant.28.clone.start_ref) | copy-start | bytes 98308
  61.7 1.3 collective-permute-start.6
  63.7 29.0 %all-to-all-start = ((f32[16,2,24,128]{3,2,1,0:T(8,128)}), f32[16,2,24,128]{3,2,1,0:T(8,128)}, u32[]{:S(2)}, u32[]{:S(2)}) async-start(f32[16,2,24,128]{3,2,1,0:T(8,128)} %broadcast_in_dim.6), calls=%async_computation | async-start | bytes 786432 | tf_op jit(solution)/shard_map/all_to_all | solution.py:418
  71.7 32.8 %collective-permute-start.7 = (bf16[32,8192]{1,0:T(8,128)(2,1)}, bf16[32,8192]{1,0:T(8,128)(2,1)}, u32[]{:S(2)}, u32[]{:S(2)}) collective-permute-start(bf16[32,8192]{1,0:T(8,128)(2,1)} %get-tuple-element.34), channel_id=1, source_target_pairs={{0,1},{1,2},{2,3},{3,0},{4,5},{5,6},{6,7},{7,4},{8,9},{9,10},{10,1... | collective-permute-start | bytes 1572872 | tf_op jit(solution)/shard_map/ppermute | solution.py:443
  72.5 32.0 %collective-permute-start.8 = (bf16[32,8192]{1,0:T(8,128)(2,1)}, bf16[32,8192]{1,0:T(8,128)(2,1)}, u32[]{:S(2)}, u32[]{:S(2)}) collective-permute-start(bf16[32,8192]{1,0:T(8,128)(2,1)} %get-tuple-element.35), channel_id=1, source_target_pairs={{0,2},{1,3},{2,0},{3,1},{4,6},{5,7},{6,4},{7,5},{8,10},{9,11},{10,... | collective-permute-start | bytes 1572872 | tf_op jit(solution)/shard_map/ppermute | solution.py:443
  74.0 30.4 %collective-permute-start.9 = (bf16[32,8192]{1,0:T(8,128)(2,1)}, bf16[32,8192]{1,0:T(8,128)(2,1)}, u32[]{:S(2)}, u32[]{:S(2)}) collective-permute-start(bf16[32,8192]{1,0:T(8,128)(2,1)} %get-tuple-element.36), channel_id=1, source_target_pairs={{0,3},{1,0},{2,1},{3,2},{4,7},{5,4},{6,5},{7,6},{8,11},{9,8},{10,9... | collective-permute-start | bytes 1572872 | tf_op jit(solution)/shard_map/ppermute | solution.py:443
  92.8 1.0 copy-start.7
  93.8 10.7 %copy-start.2 = (bf16[32,8192]{1,0:T(8,128)(2,1)S(1)}, bf16[32,8192]{1,0:T(8,128)(2,1)}, u32[]{:S(2)}) copy-start(bf16[32,8192]{1,0:T(8,128)(2,1)} %get-tuple-element.33.rest_0_.rest_4_) | copy-start | bytes 1572868
  106.9 1.3 collective-permute-start.13
  137.1 1.2 collective-permute-start.14

commit v3 on v2

--- a/solution.py
+++ b/solution.py
@@ -434,7 +434,7 @@
     degrees = degrees.reshape(1, rows_dev)
     start = jnp.asarray(start_basis())
 
-    halves = [spectra_call(snapshots, half, 2048) for half in range(HALVES)]
+    halves = [spectra_call(snapshots, half, 4096) for half in range(HALVES)]
     pieces = {}
     for pair in range(PAIR):
         for half in range(HALVES):
@@ -449,11 +449,11 @@
         for half in range(HALVES):
             known = weights if before is None or half < HALVES - 1 else after(weights, before[1])
             gram = gram_call(
-                half, pieces[pair, half], known, pivot_local[PAIR * pair : PAIR * pair + PAIR], gram, 4096
+                half, pieces[pair, half], known, pivot_local[PAIR * pair : PAIR * pair + PAIR], gram, 8192
             )
         before = modes_call(
             pair, place, start, weights, degrees, gather_chips(gram),
-            pieces[pair, 0], pieces[pair, 1], before, row_count, 4096,
+            pieces[pair, 0], pieces[pair, 1], before, row_count, 8192,
         )
     modes, energy = before
     return modes, energy_call(gather_chips(energy))

time: 151 us -> 150 us (level)
  Pallas kernels: 44.7 us -> 41.9 us
  waiting for transfers between devices: 49 us -> 50.9 us
    pallas_call x2, Pallas kernels: 13 us -> 11.1 us  [spectra_call(): pl.pallas_call(kernel, grid=(steps,), in_specs=[pl.BlockSpec((GROUPS, row...]
    ppermute x12, waiting for transfers between devices: 45.5 us -> 47.4 us  [per_device(): lax.ppermute(sent[k], 'blk', [(g, (g + k) % GROUPS) for g in range(GROUPS)])]
  transfers between devices with their start and end apart: 16 -> 16, of which waited for: 8 -> 8; matrix products, arithmetic and copies ran while one was open for 1% -> 1% of each run, Pallas kernels for 15% -> 14%
where the time goes in v3:
time: 150 us; the launch traced here: 149 us
  waiting for transfers between devices  50.9 us (34%)
  Pallas kernels  41.9 us (28%)
  blocking collectives  29 us (19%)
  starting transfers between devices  23.8 us (16%)
  local copies, waits for them, and re-layouts  2.93 us (2%)
    ppermute x12, waiting for transfers between devices, per_device(): lax.ppermute(sent[k], 'blk', [(g, (g + k) % GROUPS) for g in range(GROUPS)])  47.4 us
    all_to_all x2, blocking collectives, gather_chips(): return lax.all_to_all(spread, ('z', 'x'), 0, 0, tiled=True)  29 us
    pallas_call x2, Pallas kernels, modes_call(): pl.pallas_call(kernel, grid_spec=pltpu.PrefetchScalarGridSpec(num_scalar_...  21.1 us
    ppermute x12, starting transfers between devices, per_device(): lax.ppermute(sent[k], 'blk', [(g, (g + k) % GROUPS) for g in range(GROUPS)])  15.7 us
    pallas_call x2, Pallas kernels, spectra_call(): pl.pallas_call(kernel, grid=(steps,), in_specs=[pl.BlockSpec((GROUPS, row...  11.1 us
    pallas_call x4, Pallas kernels, gram_call(): pl.pallas_call(kernel, grid=(steps,), in_specs=[pl.BlockSpec((PAIR, MODES...  8.07 us
    all_to_all x1, starting transfers between devices, gather_chips(): return lax.all_to_all(spread, ('z', 'x'), 0, 0, tiled=True)  7.92 us
    ppermute x3, waiting for transfers between devices, gather_chips(): value = value + lax.ppermute(value, 'core', [(0, 1), (1, 0)])  3.53 us
  transfers between devices with their start and end apart: 16, of which 8 were waited for; matrix products, arithmetic and copies ran while one was open for 1% of the time, Pallas kernels for 14%

profile of v3, /device:TPU:8, one launch (start us, length us, event | category | flops | bytes accessed | tf_op | source)
XLA Modules:
  0.0 149.4 jit_solution(3967016887430078807)
XLA Ops:
  0.6 5.6 %spectra.3 = (bf16[32,8192]{1,0:T(8,128)(2,1)}, bf16[32,8192]{1,0:T(8,128)(2,1)}, bf16[32,8192]{1,0:T(8,128)(2,1)}, bf16[32,8192]{1,0:T(8,128)(2,1)}, bf16[32,81...) custom-call(bf16[4,32,256]{2,1,0:T(8,128)(2,1)} %constant.29.clone.lhs_ref, ...), custom_call_target="tpu_custom_call" | custom-call | flops 1073741824 | bytes 12582912 | tf_op jit(solution)/shard_map/spectra/pallas_call | solution.py:98
  6.3 1.6 %collective-permute-start.3 = (bf16[32,8192]{1,0:T(8,128)(2,1)}, bf16[32,8192]{1,0:T(8,128)(2,1)S(1)}, u32[]{:S(2)}, u32[]{:S(2)}) collective-permute-start(bf16[32,8192]{1,0:T(8,128)(2,1)} %get-tuple-element.28), channel_id=1, source_target_pairs={{0,1},{1,2},{2,3},{3,0},{4,5},{5,6},{6,7},{7,4},{8,9},{9,10},{10,1... | collective-permute-start | bytes 1572872 | tf_op jit(solution)/shard_map/ppermute | solution.py:443
  7.8 0.9 collective-permute-start.4
  8.7 2.5 %collective-permute-start.5 = (bf16[32,8192]{1,0:T(8,128)(2,1)}, bf16[32,8192]{1,0:T(8,128)(2,1)S(1)}, u32[]{:S(2)}, u32[]{:S(2)}) collective-permute-start(bf16[32,8192]{1,0:T(8,128)(2,1)} %get-tuple-element.30), channel_id=1, source_target_pairs={{0,3},{1,0},{2,1},{3,2},{4,7},{5,4},{6,5},{7,6},{8,11},{9,8},{10,9... | collective-permute-start | bytes 1572872 | tf_op jit(solution)/shard_map/ppermute | solution.py:443
  11.2 5.5 %spectra.2 = (bf16[32,8192]{1,0:T(8,128)(2,1)}, bf16[32,8192]{1,0:T(8,128)(2,1)}, bf16[32,8192]{1,0:T(8,128)(2,1)}, bf16[32,8192]{1,0:T(8,128)(2,1)}, bf16[32,81...) custom-call(bf16[4,32,256]{2,1,0:T(8,128)(2,1)} %constant.29.clone.lhs_ref, ...), custom_call_target="tpu_custom_call" | custom-call | flops 1073741824 | bytes 12582912 | tf_op jit(solution)/shard_map/spectra/pallas_call | solution.py:98
  16.8 3.4 %collective-permute-start.1 = (bf16[32,8192]{1,0:T(8,128)(2,1)}, bf16[32,8192]{1,0:T(8,128)(2,1)}, u32[]{:S(2)}, u32[]{:S(2)}) collective-permute-start(bf16[32,8192]{1,0:T(8,128)(2,1)} %get-tuple-element.25), channel_id=1, source_target_pairs={{0,2},{1,3},{2,0},{3,1},{4,6},{5,7},{6,4},{7,5},{8,10},{9,11},{10,... | collective-permute-start | bytes 1572872 | tf_op jit(solution)/shard_map/ppermute | solution.py:443
  20.2 11.1 %collective-permute-done.3.rest_1_ = bf16[32,8192]{1,0:T(8,128)(2,1)S(1)} collective-permute-done((bf16[32,8192]{1,0:T(8,128)(2,1)}, bf16[32,8192]{1,0:T(8,128)(2,1)S(1)}, u32[]{:S(2)}, u32[]{:S(2)}) %collective-permute-start.3) | collective-permute-done | bytes 524320 | tf_op jit(solution)/shard_map/ppermute | solution.py:443
  31.3 2.8 %collective-permute-start.10 = (bf16[32,8192]{1,0:T(8,128)(2,1)}, bf16[32,8192]{1,0:T(8,128)(2,1)}, u32[]{:S(2)}, u32[]{:S(2)}) collective-permute-start(bf16[32,8192]{1,0:T(8,128)(2,1)} %get-tuple-element.38), channel_id=1, source_target_pairs={{0,1},{1,2},{2,3},{3,0},{4,5},{5,6},{6,7},{7,4},{8,9},{9,10},{10,1... | collective-permute-start | bytes 1572872 | tf_op jit(solution)/shard_map/ppermute | solution.py:443
  34.1 10.1 %collective-permute-done.5.rest_3_ = bf16[32,8192]{1,0:T(8,128)(2,1)S(1)} collective-permute-done((bf16[32,8192]{1,0:T(8,128)(2,1)}, bf16[32,8192]{1,0:T(8,128)(2,1)S(1)}, u32[]{:S(2)}, u32[]{:S(2)}) %collective-permute-start.5) | collective-permute-done | bytes 524320 | tf_op jit(solution)/shard_map/ppermute | solution.py:443
  44.2 9.5 %collective-permute-done.rest_1_.rest_5_ = bf16[32,8192]{1,0:T(8,128)(2,1)S(1)} collective-permute-done((bf16[32,8192]{1,0:T(8,128)(2,1)}, bf16[32,8192]{1,0:T(8,128)(2,1)S(1)}, u32[]{:S(2)}, u32[]{:S(2)}) %collective-permute-start) | collective-permute-done | bytes 524320 | tf_op jit(solution)/shard_map/ppermute | solution.py:443
  53.7 0.9 copy-done.5
  54.6 0.1 copy.11.p_ref
  54.7 1.0 gram.4.rest_4_
  55.7 2.6 %collective-permute-done.2.rest_3_.rest_7_ = bf16[32,8192]{1,0:T(8,128)(2,1)} collective-permute-done((bf16[32,8192]{1,0:T(8,128)(2,1)}, bf16[32,8192]{1,0:T(8,128)(2,1)}, u32[]{:S(2)}, u32[]{:S(2)}) %collective-permute-start.2) | collective-permute-done | bytes 524320 | tf_op jit(solution)/shard_map/ppermute | solution.py:443
  58.3 2.2 %gram.5 = f32[2,24,128]{2,1,0:T(8,128)S(1)} custom-call(s32[2,8,1]{2,1,0:T(8,128)S(1)} %copy.11.p_ref, f32[1,16384]{1,0:T(1,128)S(1)} %bitcast.10, bf16[32,8192]{1,0:T(8,128)(2,1)S(1)} %copy-done.4, bf16[32,8192]{1,0:T(8,128)(2,1)S(1)} %copy-done.6, bf16[32,8192]{1,0:T(8,128)(2,1)} %collective-permute-done.1.rest_2_.rest_6_, ...), custom_call_target="tpu_custom_call" | custom-call | flops 536870912 | bytes 2097152 | tf_op jit(solution)/shard_map/gram/pallas_call | solution.py:187
  60.7 1.2 collective-permute-done.6
  61.9 0.8 broadcast_in_dim.6
  62.7 7.9 %all-to-all-start = ((f32[16,2,24,128]{3,2,1,0:T(8,128)}), f32[16,2,24,128]{3,2,1,0:T(8,128)}, u32[]{:S(2)}, u32[]{:S(2)}) async-start(f32[16,2,24,128]{3,2,1,0:T(8,128)} %broadcast_in_dim.6), calls=%async_computation | async-start | bytes 786432 | tf_op jit(solution)/shard_map/all_to_all | solution.py:418
  70.6 0.6 collective-permute-start.7
  71.1 1.4 collective-permute-start.8
  72.6 2.5 %collective-permute-start.9 = (bf16[32,8192]{1,0:T(8,128)(2,1)}, bf16[32,8192]{1,0:T(8,128)(2,1)}, u32[]{:S(2)}, u32[]{:S(2)}) collective-permute-start(bf16[32,8192]{1,0:T(8,128)(2,1)} %get-tuple-element.36), channel_id=1, source_target_pairs={{0,3},{1,0},{2,1},{3,2},{4,7},{5,4},{6,5},{7,6},{8,11},{9,8},{10,9... | collective-permute-start | bytes 1572872 | tf_op jit(solution)/shard_map/ppermute | solution.py:443
  75.3 14.1 %collective-permute-done.12.rest_3_ = bf16[32,8192]{1,0:T(8,128)(2,1)} collective-permute-done((bf16[32,8192]{1,0:T(8,128)(2,1)}, bf16[32,8192]{1,0:T(8,128)(2,1)}, u32[]{:S(2)}, u32[]{:S(2)}) %collective-permute-start.12) | collective-permute-done | bytes 524320 | tf_op jit(solution)/shard_map/ppermute | solution.py:443
  89.3 2.4 %gram.6.rest_4_ = f32[2,24,128]{2,1,0:T(8,128)S(1)} custom-call(s32[2,8,1]{2,1,0:T(8,128)S(1)} %copy.13.p_ref, f32[1,16384]{1,0:T(1,128)S(1)} %bitcast.11, bf16[32,8192]{1,0:T(8,128)(2,1)S(1)} %copy-done.1, bf16[32,8192]{1,0:T(8,128)(2,1)} %collective-permute-done.10.rest_1_, bf16[32,8192]{1,0:T(8,128)(2,1)} %collective-permute-done.11.rest_2_, ...), custom_call_target="tpu_custom_call" | custom-call | flops 536870912 | bytes 2097152 | tf_op jit(solution)/shard_map/gram/pallas_call | solution.py:187
  91.8 1.0 copy-done.7
  92.8 10.3 %modes.2 = (bf16[4,2,8,16384]{3,2,1,0:T(8,128)(2,1)}, f32[8,128]{1,0:T(8,128)S(1)}) custom-call(s32[3]{0:T(128)S(1)} %pad_add_fusion.place_ref, f32[4,2,8,128]{3,2,1,0:T(8,128)S(1)} %copy-done.9, f32[1,16384]{1,0:T(1,128)S(1)} %bitcast.12, s32[1,16384]{1,0:T(1,128)S(1)} %bitcast.15, f32[16,2,24,128]{3,2,1,0:T(8,128)} %all-to-all-done.sum_ref, ...), custom_call_target="tpu_custom_call" | custom-call | flops 2073741824 | bytes 5242880 | tf_op jit(solution)/shard_map/modes/pallas_call | solution.py:354
  103.1 2.4 %gram.7 = f32[2,24,128]{2,1,0:T(8,128)S(1)} custom-call(s32[2,8,1]{2,1,0:T(8,128)S(1)} %copy.13.p_ref, f32[1,16384]{1,0:T(1,128)S(1)} %bitcast.13, bf16[32,8192]{1,0:T(8,128)(2,1)S(1)} %copy-done.2, bf16[32,8192]{1,0:T(8,128)(2,1)} %collective-permute-done.7.rest_1_.rest_5_, bf16[32,8192]{1,0:T(8,128)(2,1)} %collective-permute-done.8.rest_2_.rest_6_, ...), custom_call_target="tpu_custom_call" | custom-call | flops 536870912 | bytes 2097152 | tf_op jit(solution)/shard_map/gram/pallas_call | solution.py:187
  105.6 1.2 collective-permute-done.13
  106.8 18.1 %all_to_all.15.sum_ref = f32[16,2,24,128]{3,2,1,0:T(8,128)S(1)} all-to-all(f32[16,2,24,128]{3,2,1,0:T(8,128)S(1)} %broadcast_in_dim.7), channel_id=1, replica_groups=mesh['z'=4,'x'=4,'core'=2,'blk'=4] {'z','x'}, dimensions={0} | all-to-all | bytes 786432 | tf_op jit(solution)/shard_map/all_to_all | solution.py:418
  124.9 10.8 %modes.3 = (bf16[4,2,8,16384]{3,2,1,0:T(8,128)(2,1)}, f32[8,128]{1,0:T(8,128)S(1)}) custom-call(s32[3]{0:T(128)S(1)} %pad_add_fusion.place_ref, f32[4,2,8,128]{3,2,1,0:T(8,128)S(1)} %copy-done.9, f32[1,16384]{1,0:T(1,128)S(1)} %bitcast.14, s32[1,16384]{1,0:T(1,128)S(1)} %bitcast.16, ...), custom_call_target="tpu_custom_call", output_to_operand_aliasing={{0}: (13, {})} | custom-call | flops 2073741824 | bytes 5242880 | tf_op jit(solution)/shard_map/modes/pallas_call | solution.py:354
  135.8 1.2 collective-permute-done.14
  136.9 10.9 %all_to_all.16.in_ref = f32[16,8,128]{2,1,0:T(8,128)} all-to-all(f32[16,8,128]{2,1,0:T(8,128)S(1)} %broadcast_in_dim.8), channel_id=1, replica_groups=mesh['z'=4,'x'=4,'core'=2,'blk'=4] {'z','x'}, dimensions={0} | all-to-all | bytes 131072 | tf_op jit(solution)/shard_map/all_to_all | solution.py:418
  147.8 1.6 %energy.1 = f32[4,8,384]{2,1,0:T(8,128)} custom-call(f32[16,8,128]{2,1,0:T(8,128)} %all_to_all.16.in_ref), custom_call_target="tpu_custom_call" | custom-call | tf_op jit(solution)/shard_map/energy/pallas_call | solution.py:407
  (44 shorter events, 0.5 us)
Async XLA Ops:
  6.3 25.0 %collective-permute-start.3 = (bf16[32,8192]{1,0:T(8,128)(2,1)}, bf16[32,8192]{1,0:T(8,128)(2,1)S(1)}, u32[]{:S(2)}, u32[]{:S(2)}) collective-permute-start(bf16[32,8192]{1,0:T(8,128)(2,1)} %get-tuple-element.28), channel_id=1, source_target_pairs={{0,1},{1,2},{2,3},{3,0},{4,5},{5,6},{6,7},{7,4},{8,9},{9,10},{10,1... | collective-permute-start | bytes 1572872 | tf_op jit(solution)/shard_map/ppermute | solution.py:443
  7.8 23.4 %collective-permute-start.4 = (bf16[32,8192]{1,0:T(8,128)(2,1)}, bf16[32,8192]{1,0:T(8,128)(2,1)S(1)}, u32[]{:S(2)}, u32[]{:S(2)}) collective-permute-start(bf16[32,8192]{1,0:T(8,128)(2,1)} %get-tuple-element.29), channel_id=1, source_target_pairs={{0,2},{1,3},{2,0},{3,1},{4,6},{5,7},{6,4},{7,5},{8,10},{9,11},{10,... | collective-permute-start | bytes 1572872 | tf_op jit(solution)/shard_map/ppermute | solution.py:443
  8.7 25.4 %copy-start.10 = (s32[4,8]{1,0:T(4,128)S(1)}, s32[4,8]{1,0:T(4,128)}, u32[]{:S(2)}) copy-start(s32[4,8]{1,0:T(4,128)} %param.10) | copy-start | bytes 388
  8.7 46.0 %copy-start = (f32[16384]{0:T(1024)S(1)}, f32[16384]{0:T(1024)}, u32[]{:S(2)}) copy-start(f32[16384]{0:T(1024)} %param.8) | copy-start | bytes 196612
  8.7 46.0 %copy-start.3 = (bf16[32,8192]{1,0:T(8,128)(2,1)S(1)}, bf16[32,8192]{1,0:T(8,128)(2,1)}, u32[]{:S(2)}) copy-start(bf16[32,8192]{1,0:T(8,128)(2,1)} %get-tuple-element.27.rest_0_) | copy-start | bytes 1572868
  8.7 35.5 %collective-permute-start.5 = (bf16[32,8192]{1,0:T(8,128)(2,1)}, bf16[32,8192]{1,0:T(8,128)(2,1)S(1)}, u32[]{:S(2)}, u32[]{:S(2)}) collective-permute-start(bf16[32,8192]{1,0:T(8,128)(2,1)} %get-tuple-element.30), channel_id=1, source_target_pairs={{0,3},{1,0},{2,1},{3,2},{4,7},{5,4},{6,5},{7,6},{8,11},{9,8},{10,9... | collective-permute-start | bytes 1572872 | tf_op jit(solution)/shard_map/ppermute | solution.py:443
  16.7 41.6 %copy-start.4 = (bf16[32,8192]{1,0:T(8,128)(2,1)S(1)}, bf16[32,8192]{1,0:T(8,128)(2,1)}, u32[]{:S(2)}) copy-start(bf16[32,8192]{1,0:T(8,128)(2,1)} %get-tuple-element.23.rest_0_.rest_4_) | copy-start | bytes 1572868
  16.7 37.0 %collective-permute-start = (bf16[32,8192]{1,0:T(8,128)(2,1)}, bf16[32,8192]{1,0:T(8,128)(2,1)S(1)}, u32[]{:S(2)}, u32[]{:S(2)}) collective-permute-start(bf16[32,8192]{1,0:T(8,128)(2,1)} %get-tuple-element.24), channel_id=1, source_target_pairs={{0,1},{1,2},{2,3},{3,0},{4,5},{5,6},{6,7},{7,4},{8,9},{9,10},{10,1... | collective-permute-start | bytes 1572872 | tf_op jit(solution)/shard_map/ppermute | solution.py:443
  16.8 38.9 %collective-permute-start.1 = (bf16[32,8192]{1,0:T(8,128)(2,1)}, bf16[32,8192]{1,0:T(8,128)(2,1)}, u32[]{:S(2)}, u32[]{:S(2)}) collective-permute-start(bf16[32,8192]{1,0:T(8,128)(2,1)} %get-tuple-element.25), channel_id=1, source_target_pairs={{0,2},{1,3},{2,0},{3,1},{4,6},{5,7},{6,4},{7,5},{8,10},{9,11},{10,... | collective-permute-start | bytes 1572872 | tf_op jit(solution)/shard_map/ppermute | solution.py:443
  31.3 27.1 %collective-permute-start.2 = (bf16[32,8192]{1,0:T(8,128)(2,1)}, bf16[32,8192]{1,0:T(8,128)(2,1)}, u32[]{:S(2)}, u32[]{:S(2)}) collective-permute-start(bf16[32,8192]{1,0:T(8,128)(2,1)} %get-tuple-element.26), channel_id=1, source_target_pairs={{0,3},{1,0},{2,1},{3,2},{4,7},{5,4},{6,5},{7,6},{8,11},{9,8},{10,9... | collective-permute-start | bytes 1572872 | tf_op jit(solution)/shard_map/ppermute | solution.py:443
  31.3 41.3 %collective-permute-start.10 = (bf16[32,8192]{1,0:T(8,128)(2,1)}, bf16[32,8192]{1,0:T(8,128)(2,1)}, u32[]{:S(2)}, u32[]{:S(2)}) collective-permute-start(bf16[32,8192]{1,0:T(8,128)(2,1)} %get-tuple-element.38), channel_id=1, source_target_pairs={{0,1},{1,2},{2,3},{3,0},{4,5},{5,6},{6,7},{7,4},{8,9},{9,10},{10,1... | collective-permute-start | bytes 1572872 | tf_op jit(solution)/shard_map/ppermute | solution.py:443
  44.2 31.1 %collective-permute-start.11 = (bf16[32,8192]{1,0:T(8,128)(2,1)}, bf16[32,8192]{1,0:T(8,128)(2,1)}, u32[]{:S(2)}, u32[]{:S(2)}) collective-permute-start(bf16[32,8192]{1,0:T(8,128)(2,1)} %get-tuple-element.39), channel_id=1, source_target_pairs={{0,2},{1,3},{2,0},{3,1},{4,6},{5,7},{6,4},{7,5},{8,10},{9,11},{10,... | collective-permute-start | bytes 1572872 | tf_op jit(solution)/shard_map/ppermute | solution.py:443
  53.7 0.9 copy-start.5
  54.6 34.8 %collective-permute-start.12 = (bf16[32,8192]{1,0:T(8,128)(2,1)}, bf16[32,8192]{1,0:T(8,128)(2,1)}, u32[]{:S(2)}, u32[]{:S(2)}) collective-permute-start(bf16[32,8192]{1,0:T(8,128)(2,1)} %get-tuple-element.40), channel_id=1, source_target_pairs={{0,3},{1,0},{2,1},{3,2},{4,7},{5,4},{6,5},{7,6},{8,11},{9,8},{10,9... | collective-permute-start | bytes 1572872 | tf_op jit(solution)/shard_map/ppermute | solution.py:443
  54.6 3.7 %copy-start.6 = (bf16[32,8192]{1,0:T(8,128)(2,1)S(1)}, bf16[32,8192]{1,0:T(8,128)(2,1)}, u32[]{:S(2)}) copy-start(bf16[32,8192]{1,0:T(8,128)(2,1)} %copy-done.5) | copy-start | bytes 1572868
  55.7 33.6 %copy-start.1 = (bf16[32,8192]{1,0:T(8,128)(2,1)S(1)}, bf16[32,8192]{1,0:T(8,128)(2,1)}, u32[]{:S(2)}) copy-start(bf16[32,8192]{1,0:T(8,128)(2,1)} %get-tuple-element.37.rest_0_) | copy-start | bytes 1572868
  60.6 31.2 %copy-start.8 = (s32[16384]{0:T(1024)S(1)}, s32[16384]{0:T(1024)}, u32[]{:S(2)}) copy-start(s32[16384]{0:T(1024)} %param.9) | copy-start | bytes 196612
  60.6 31.2 %copy-start.9 = (f32[4,2,8,128]{3,2,1,0:T(8,128)S(1)}, f32[4,2,8,128]{3,2,1,0:T(8,128)}, u32[]{:S(2)}) copy-start(f32[4,2,8,128]{3,2,1,0:T(8,128)} %constant.28.clone.start_ref) | copy-start | bytes 98308
  60.6 1.3 collective-permute-start.6
  62.7 29.1 %all-to-all-start = ((f32[16,2,24,128]{3,2,1,0:T(8,128)}), f32[16,2,24,128]{3,2,1,0:T(8,128)}, u32[]{:S(2)}, u32[]{:S(2)}) async-start(f32[16,2,24,128]{3,2,1,0:T(8,128)} %broadcast_in_dim.6), calls=%async_computation | async-start | bytes 786432 | tf_op jit(solution)/shard_map/all_to_all | solution.py:418
  70.6 32.5 %collective-permute-start.7 = (bf16[32,8192]{1,0:T(8,128)(2,1)}, bf16[32,8192]{1,0:T(8,128)(2,1)}, u32[]{:S(2)}, u32[]{:S(2)}) collective-permute-start(bf16[32,8192]{1,0:T(8,128)(2,1)} %get-tuple-element.34), channel_id=1, source_target_pairs={{0,1},{1,2},{2,3},{3,0},{4,5},{5,6},{6,7},{7,4},{8,9},{9,10},{10,1... | collective-permute-start | bytes 1572872 | tf_op jit(solution)/shard_map/ppermute | solution.py:443
  71.1 32.0 %collective-permute-start.8 = (bf16[32,8192]{1,0:T(8,128)(2,1)}, bf16[32,8192]{1,0:T(8,128)(2,1)}, u32[]{:S(2)}, u32[]{:S(2)}) collective-permute-start(bf16[32,8192]{1,0:T(8,128)(2,1)} %get-tuple-element.35), channel_id=1, source_target_pairs={{0,2},{1,3},{2,0},{3,1},{4,6},{5,7},{6,4},{7,5},{8,10},{9,11},{10,... | collective-permute-start | bytes 1572872 | tf_op jit(solution)/shard_map/ppermute | solution.py:443
  72.6 30.5 %collective-permute-start.9 = (bf16[32,8192]{1,0:T(8,128)(2,1)}, bf16[32,8192]{1,0:T(8,128)(2,1)}, u32[]{:S(2)}, u32[]{:S(2)}) collective-permute-start(bf16[32,8192]{1,0:T(8,128)(2,1)} %get-tuple-element.36), channel_id=1, source_target_pairs={{0,3},{1,0},{2,1},{3,2},{4,7},{5,4},{6,5},{7,6},{8,11},{9,8},{10,9... | collective-permute-start | bytes 1572872 | tf_op jit(solution)/shard_map/ppermute | solution.py:443
  91.8 1.0 copy-start.7
  92.8 10.3 %copy-start.2 = (bf16[32,8192]{1,0:T(8,128)(2,1)S(1)}, bf16[32,8192]{1,0:T(8,128)(2,1)}, u32[]{:S(2)}) copy-start(bf16[32,8192]{1,0:T(8,128)(2,1)} %get-tuple-element.33.rest_0_.rest_4_) | copy-start | bytes 1572868
  105.5 1.3 collective-permute-start.13
  135.8 1.2 collective-permute-start.14

commit v4 on v3

--- a/solution.py
+++ b/solution.py
@@ -145,57 +145,33 @@
     return jnp.where(odd_lanes(value.shape), other, -other)
 
 
-def gram_call(half, pieces, weights, pivot_local, before, tile):
+def gram_call(half, pieces, weights, pivot_local, before):
     part = pieces[0].shape[1]
-    steps = part // tile
 
     def kernel(p_ref, w_ref, *rest):
         x_refs, rest = rest[:GROUPS], rest[GROUPS:]
-        out_ref, acc = rest[-2:]
-        n = pl.program_id(0)
-
-        @pl.when(n == 0)
-        def _():
-            acc[...] = jnp.zeros_like(acc)
-
-        lane = lax.broadcasted_iota(jnp.int32, (MODES, tile), 1) + (n + half * steps) * tile
+        out_ref = rest[-1]
+        lane = lax.broadcasted_iota(jnp.int32, (MODES, part), 1) + half * part
         for f in range(PAIR):
             x = jnp.concatenate([r[16 * f : 16 * f + 16] for r in x_refs], axis=0)
-            wx = x.astype(F32) * w_ref[...]
+            wx = x.astype(F32) * w_ref[:, half * part : (half + 1) * part]
             hot = jnp.where(lane == p_ref[f], 1.0, 0.0)
             left = jnp.concatenate([wx, hot, jnp.zeros_like(hot)], axis=0).astype(BF16)
-            acc[f, :, :64] += lax.dot_general(
-                left, x, (((1,), (1,)), ((), ())), preferred_element_type=F32
-            )
-
-        @pl.when(n == steps - 1)
-        def _():
-            for f in range(PAIR):
-                total = acc[f]
-                total = total + pltpu.roll(total, 64, 1)
-                gram = total[:64]
-                same = low_rows(gram.shape) != odd_lanes(gram.shape)
-                cross = other_lanes(other_rows(gram)) + jnp.where(same, gram, -gram)
-                cross = jnp.where(low_rows((32, 128)), cross[:32], other_rows(cross[32:]))
-                packed = jnp.where(low_lanes((16, 128)), cross[:16], cross[16:])
-                packed = jnp.concatenate([packed, total[64:72]], axis=0)
-                if before is not None:
-                    packed = packed + rest[0][f]
-                out_ref[f] = packed
-
-    whole = pl.BlockSpec((PAIR, 24, 128), lambda n: (0, 0, 0))
+            total = lax.dot_general(left, x, (((1,), (1,)), ((), ())), preferred_element_type=F32)
+            total = jnp.concatenate([total, total], axis=1)
+            gram = total[:64]
+            same = low_rows(gram.shape) != odd_lanes(gram.shape)
+            cross = other_lanes(other_rows(gram)) + jnp.where(same, gram, -gram)
+            cross = jnp.where(low_rows((32, 128)), cross[:32], other_rows(cross[32:]))
+            packed = jnp.where(low_lanes((16, 128)), cross[:16], cross[16:])
+            packed = jnp.concatenate([packed, total[64:72]], axis=0)
+            if before is not None:
+                packed = packed + rest[0][f]
+            out_ref[f] = packed
+
     return pl.pallas_call(
         kernel,
-        grid=(steps,),
-        in_specs=[
-            pl.BlockSpec((PAIR, MODES, 1), lambda n: (0, 0, 0)),
-            pl.BlockSpec((1, tile), lambda n: (0, n + half * steps)),
-        ]
-        + [pl.BlockSpec((32, tile), lambda n: (0, n))] * GROUPS
-        + [whole] * (before is not None),
-        out_specs=whole,
         out_shape=jax.ShapeDtypeStruct((PAIR, 24, 128), F32),
-        scratch_shapes=[pltpu.VMEM((PAIR, 80, 128), F32)],
         compiler_params=pltpu.CompilerParams(vmem_limit_bytes=SMALL),
         cost_estimate=pl.CostEstimate(
             flops=2 * PAIR * 64 * 256 * part, bytes_accessed=4 * 64 * part, transcendentals=0
@@ -262,110 +238,91 @@
     return vec, alt
 
 
-def modes_call(pair, place, start, weights, degrees, sums, early, late, before, row_count, tile):
+def modes_call(pair, place, start, weights, degrees, sums, early, late, before, row_count):
     rows_dev = weights.shape[1]
-    steps = rows_dev // tile
-    part_steps = steps // HALVES
+    tile = rows_dev // HALVES
     bands = tile * DEGREES // row_count
 
     def kernel(place_ref, start_ref, w_ref, deg_ref, sum_ref, *rest):
         x_refs, rest = rest[: HALVES * GROUPS], rest[HALVES * GROUPS :]
-        modes_ref, energy_ref, expand, phase = rest[-4:]
-        n = pl.program_id(0)
-
-        @pl.when(n == 0)
-        def _():
-            total = jnp.sum(sum_ref[...], axis=0)
-            crosses = []
-            for f in range(PAIR):
-                packed = total[f, :16] * (1.0 / row_count)
-                swap = pltpu.roll(packed, 64, 1)
-                low = low_lanes(packed.shape)
-                crosses.append(
-                    jnp.concatenate(
-                        [jnp.where(low, packed, swap), jnp.where(low, swap, packed)], axis=0
-                    )
+        modes_ref, energy_ref, stage, sems = rest[-4:]
+        total = jnp.sum(sum_ref[...], axis=0)
+        crosses = []
+        for f in range(PAIR):
+            packed = total[f, :16] * (1.0 / row_count)
+            swap = pltpu.roll(packed, 64, 1)
+            low = low_lanes(packed.shape)
+            crosses.append(
+                jnp.concatenate(
+                    [jnp.where(low, packed, swap), jnp.where(low, swap, packed)], axis=0
                 )
-            vec, alt = leading_basis(crosses, start_ref[place_ref[0]])
-            odd = odd_lanes(vec.shape)
-            low = low_lanes(vec.shape)
-            upper = jnp.where(odd, -vec, vec).astype(BF16).astype(F32)
-            lower = jnp.where(odd, alt, -alt).astype(BF16).astype(F32)
-            at = jnp.where(low, total[:, 16:24], 0.0)
-            z_re = jnp.sum(upper * at, axis=2, keepdims=True)
-            z_im = jnp.sum(lower * at, axis=2, keepdims=True)
-            inverse = lax.rsqrt(z_re * z_re + z_im * z_im + 1.0)
-            phase[0] = jnp.broadcast_to(z_re * inverse, vec.shape)
-            phase[1] = jnp.broadcast_to(z_im * inverse, vec.shape)
-            expand[:, :8] = upper
-            expand[:, 8:] = lower
-            energy_ref[...] = jnp.zeros_like(energy_ref) if before is None else rest[1][...]
-
-        def tile_of(half):
-            w = w_ref[...]
-            lane = lax.broadcasted_iota(jnp.int32, (MODES, 128), 1)
-            base = place_ref[1] + n * bands
-            hits = [deg_ref[...] == base + m for m in range(bands + 1)]
-            total = jnp.zeros((MODES, 128), F32)
+            )
+        vec, alt = leading_basis(crosses, start_ref[place_ref[0]])
+        odd = odd_lanes(vec.shape)
+        low = low_lanes(vec.shape)
+        upper = jnp.where(odd, -vec, vec).astype(BF16).astype(F32)
+        lower = jnp.where(odd, alt, -alt).astype(BF16).astype(F32)
+        at = jnp.where(low, total[:, 16:24], 0.0)
+        z_re = jnp.sum(upper * at, axis=2, keepdims=True)
+        z_im = jnp.sum(lower * at, axis=2, keepdims=True)
+        inverse = lax.rsqrt(z_re * z_re + z_im * z_im + 1.0)
+        s_re = z_re * inverse
+        s_im = z_im * inverse
+        expand = jnp.concatenate([upper, lower], axis=1).astype(BF16)
+        total = jnp.zeros((MODES, 128), F32) if before is None else rest[1][...]
+
+        lane = lax.broadcasted_iota(jnp.int32, (MODES, 128), 1)
+        copies = []
+        for half in range(HALVES):
+            span = slice(half * tile, (half + 1) * tile)
+            w = w_ref[:, span]
+            level_of = deg_ref[:, span]
+            base = place_ref[1] + half * bands
+            hits = [level_of == base + m for m in range(bands + 1)]
             for f in range(PAIR):
                 rows = slice(16 * f, 16 * f + 16)
                 x = jnp.concatenate(
                     [r[rows] for r in x_refs[GROUPS * half : GROUPS * half + GROUPS]], axis=0
                 )
-                psi = jnp.dot(expand[f][:, :64].astype(BF16), x, preferred_element_type=F32)
-                s_re = phase[0, f, :, :1]
-                s_im = phase[1, f, :, :1]
+                psi = jnp.dot(expand[f][:, :64], x, preferred_element_type=F32)
                 p_re, p_im = psi[:8], psi[8:]
-                out_re = p_re * s_re + p_im * s_im
-                out_im = p_im * s_re - p_re * s_im
-                modes_ref[f, 0] = out_re.astype(BF16)
-                modes_ref[f, 1] = out_im.astype(BF16)
+                out_re = p_re * s_re[f] + p_im * s_im[f]
+                out_im = p_im * s_re[f] - p_re * s_im[f]
+                stage[half, f, 0] = out_re.astype(BF16)
+                stage[half, f, 1] = out_im.astype(BF16)
                 power = w * (out_re * out_re + out_im * out_im)
                 for m in range(bands + 1):
                     level = jnp.sum(jnp.where(hits[m], power, 0.0), axis=1, keepdims=True)
-                    spot = (pair * PAIR + f) * 32 + place_ref[2] + n * bands + m
+                    spot = (pair * PAIR + f) * 32 + place_ref[2] + half * bands + m
                     total = total + jnp.where(lane == spot, level * (DEGREES / row_count), 0.0)
-            energy_ref[...] += total
-
-        for half in range(HALVES):
-            pl.when(n // part_steps == half)(functools.partial(tile_of, half))
-
-    in_specs = [
-        pl.BlockSpec((GROUPS, 2, MODES, 128), lambda n, p: (0, 0, 0, 0)),
-        pl.BlockSpec((1, tile), lambda n, p: (0, n)),
-        pl.BlockSpec((1, tile), lambda n, p: (0, n)),
-        pl.BlockSpec(sums.shape, lambda n, p: (0, 0, 0, 0)),
-    ]
-    in_specs += [
-        pl.BlockSpec((32, tile), lambda n, p: (0, jnp.minimum(n, part_steps - 1)))
-    ] * GROUPS
-    in_specs += [
-        pl.BlockSpec((32, tile), lambda n, p: (0, jnp.maximum(n - part_steps, 0)))
-    ] * GROUPS
+            copy = pltpu.make_async_copy(
+                stage.at[half],
+                modes_ref.at[pl.ds(pair * PAIR, PAIR), :, :, pl.ds(half * tile, tile)],
+                sems.at[half],
+            )
+            copy.start()
+            copies.append(copy)
+        energy_ref[...] = total
+        for copy in copies:
+            copy.wait()
+
+    vmem = pl.BlockSpec(memory_space=pltpu.VMEM)
+    raw = pl.BlockSpec(memory_space=pl.ANY)
     args = [place, start, weights, degrees, sums, *early, *late]
+    in_specs = [pl.BlockSpec(memory_space=pltpu.SMEM)] + [vmem] * (len(args) - 1)
     aliases = {}
     if before is not None:
-        in_specs += [
-            pl.BlockSpec(memory_space=pl.ANY),
-            pl.BlockSpec((MODES, 128), lambda n, p: (0, 0)),
-        ]
+        in_specs += [raw, vmem]
         aliases = {len(args): 0}
         args += list(before)
     return pl.pallas_call(
         kernel,
-        grid_spec=pltpu.PrefetchScalarGridSpec(
-            num_scalar_prefetch=1,
-            grid=(steps,),
-            in_specs=in_specs,
-            out_specs=[
-                pl.BlockSpec((PAIR, 2, MODES, tile), lambda n, p: (pair, 0, 0, n)),
-                pl.BlockSpec((MODES, 128), lambda n, p: (0, 0)),
-            ],
-            scratch_shapes=[
-                pltpu.VMEM((PAIR, 16, 128), F32),
-                pltpu.VMEM((2, PAIR, MODES, 128), F32),
-            ],
-        ),
+        in_specs=in_specs,
+        out_specs=[raw, vmem],
+        scratch_shapes=[
+            pltpu.VMEM((HALVES, PAIR, 2, MODES, tile), BF16),
+            pltpu.SemaphoreType.DMA((HALVES,)),
+        ],
         out_shape=[
             jax.ShapeDtypeStruct((OWNED, 2, MODES, rows_dev), BF16),
             jax.ShapeDtypeStruct((MODES, 128), F32),
@@ -449,11 +406,11 @@
         for half in range(HALVES):
             known = weights if before is None or half < HALVES - 1 else after(weights, before[1])
             gram = gram_call(
-                half, pieces[pair, half], known, pivot_local[PAIR * pair : PAIR * pair + PAIR], gram, 8192
+                half, pieces[pair, half], known, pivot_local[PAIR * pair : PAIR * pair + PAIR], gram
             )
         before = modes_call(
             pair, place, start, weights, degrees, gather_chips(gram),
-            pieces[pair, 0], pieces[pair, 1], before, row_count, 8192,
+            pieces[pair, 0], pieces[pair, 1], before, row_count,
         )
     modes, energy = before
     return modes, energy_call(gather_chips(energy))

time: 150 us -> 148 us (0.987)
  Pallas kernels: 41.9 us -> 39.8 us
    pallas_call x6, Pallas kernels: 29.2 us -> 27.1 us  [the longest x2 19.1 us: modes_call(): pl.pallas_call(kernel, in_specs=in_specs, out_specs=[raw, vmem], scratch_...]
where the time goes in v4:
time: 148 us; the launch traced here: 147 us
  waiting for transfers between devices  50.9 us (34%)
  Pallas kernels  39.8 us (27%)
  blocking collectives  29 us (20%)
  starting transfers between devices  23.9 us (16%)
  local copies, waits for them, and re-layouts  2.93 us (2%)
    ppermute x12, waiting for transfers between devices, per_device(): lax.ppermute(sent[k], 'blk', [(g, (g + k) % GROUPS) for g in range(GROUPS)])  47.4 us
    all_to_all x2, blocking collectives, gather_chips(): return lax.all_to_all(spread, ('z', 'x'), 0, 0, tiled=True)  29 us
    pallas_call x2, Pallas kernels, modes_call(): pl.pallas_call(kernel, in_specs=in_specs, out_specs=[raw, vmem], scratch_...  19.1 us
    ppermute x12, starting transfers between devices, per_device(): lax.ppermute(sent[k], 'blk', [(g, (g + k) % GROUPS) for g in range(GROUPS)])  15.7 us
    pallas_call x2, Pallas kernels, spectra_call(): pl.pallas_call(kernel, grid=(steps,), in_specs=[pl.BlockSpec((GROUPS, row...  11.1 us
    pallas_call x4, Pallas kernels, gram_call(): pl.pallas_call(kernel, out_shape=jax.ShapeDtypeStruct((PAIR, 24, 128), F3...  8.01 us
    all_to_all x1, starting transfers between devices, gather_chips(): return lax.all_to_all(spread, ('z', 'x'), 0, 0, tiled=True)  7.93 us
    ppermute x3, waiting for transfers between devices, gather_chips(): value = value + lax.ppermute(value, 'core', [(0, 1), (1, 0)])  3.52 us
  transfers between devices with their start and end apart: 16, of which 8 were waited for; matrix products, arithmetic and copies ran while one was open for 1% of the time, Pallas kernels for 14%

profile of v4, /device:TPU:8, one launch (start us, length us, event | category | flops | bytes accessed | tf_op | source)
XLA Modules:
  0.0 147.5 jit_solution(7446886492989251152)
XLA Ops:
  0.6 5.6 %spectra.3 = (bf16[32,8192]{1,0:T(8,128)(2,1)}, bf16[32,8192]{1,0:T(8,128)(2,1)}, bf16[32,8192]{1,0:T(8,128)(2,1)}, bf16[32,8192]{1,0:T(8,128)(2,1)}, bf16[32,81...) custom-call(bf16[4,32,256]{2,1,0:T(8,128)(2,1)} %constant.29.clone.lhs_ref, ...), custom_call_target="tpu_custom_call" | custom-call | flops 1073741824 | bytes 12582912 | tf_op jit(solution)/shard_map/spectra/pallas_call | solution.py:98
  6.3 1.6 %collective-permute-start.3 = (bf16[32,8192]{1,0:T(8,128)(2,1)}, bf16[32,8192]{1,0:T(8,128)(2,1)S(1)}, u32[]{:S(2)}, u32[]{:S(2)}) collective-permute-start(bf16[32,8192]{1,0:T(8,128)(2,1)} %get-tuple-element.28), channel_id=1, source_target_pairs={{0,1},{1,2},{2,3},{3,0},{4,5},{5,6},{6,7},{7,4},{8,9},{9,10},{10,1... | collective-permute-start | bytes 1572872 | tf_op jit(solution)/shard_map/ppermute | solution.py:400
  7.8 0.9 collective-permute-start.4
  8.7 2.5 %collective-permute-start.5 = (bf16[32,8192]{1,0:T(8,128)(2,1)}, bf16[32,8192]{1,0:T(8,128)(2,1)S(1)}, u32[]{:S(2)}, u32[]{:S(2)}) collective-permute-start(bf16[32,8192]{1,0:T(8,128)(2,1)} %get-tuple-element.30), channel_id=1, source_target_pairs={{0,3},{1,0},{2,1},{3,2},{4,7},{5,4},{6,5},{7,6},{8,11},{9,8},{10,9... | collective-permute-start | bytes 1572872 | tf_op jit(solution)/shard_map/ppermute | solution.py:400
  11.2 5.5 %spectra.2 = (bf16[32,8192]{1,0:T(8,128)(2,1)}, bf16[32,8192]{1,0:T(8,128)(2,1)}, bf16[32,8192]{1,0:T(8,128)(2,1)}, bf16[32,8192]{1,0:T(8,128)(2,1)}, bf16[32,81...) custom-call(bf16[4,32,256]{2,1,0:T(8,128)(2,1)} %constant.29.clone.lhs_ref, ...), custom_call_target="tpu_custom_call" | custom-call | flops 1073741824 | bytes 12582912 | tf_op jit(solution)/shard_map/spectra/pallas_call | solution.py:98
  16.8 3.4 %collective-permute-start.1 = (bf16[32,8192]{1,0:T(8,128)(2,1)}, bf16[32,8192]{1,0:T(8,128)(2,1)}, u32[]{:S(2)}, u32[]{:S(2)}) collective-permute-start(bf16[32,8192]{1,0:T(8,128)(2,1)} %get-tuple-element.25), channel_id=1, source_target_pairs={{0,2},{1,3},{2,0},{3,1},{4,6},{5,7},{6,4},{7,5},{8,10},{9,11},{10,... | collective-permute-start | bytes 1572872 | tf_op jit(solution)/shard_map/ppermute | solution.py:400
  20.2 11.1 %collective-permute-done.3.rest_1_ = bf16[32,8192]{1,0:T(8,128)(2,1)S(1)} collective-permute-done((bf16[32,8192]{1,0:T(8,128)(2,1)}, bf16[32,8192]{1,0:T(8,128)(2,1)S(1)}, u32[]{:S(2)}, u32[]{:S(2)}) %collective-permute-start.3) | collective-permute-done | bytes 524320 | tf_op jit(solution)/shard_map/ppermute | solution.py:400
  31.3 2.8 %collective-permute-start.10 = (bf16[32,8192]{1,0:T(8,128)(2,1)}, bf16[32,8192]{1,0:T(8,128)(2,1)}, u32[]{:S(2)}, u32[]{:S(2)}) collective-permute-start(bf16[32,8192]{1,0:T(8,128)(2,1)} %get-tuple-element.38), channel_id=1, source_target_pairs={{0,1},{1,2},{2,3},{3,0},{4,5},{5,6},{6,7},{7,4},{8,9},{9,10},{10,1... | collective-permute-start | bytes 1572872 | tf_op jit(solution)/shard_map/ppermute | solution.py:400
  34.1 10.1 %collective-permute-done.5.rest_3_ = bf16[32,8192]{1,0:T(8,128)(2,1)S(1)} collective-permute-done((bf16[32,8192]{1,0:T(8,128)(2,1)}, bf16[32,8192]{1,0:T(8,128)(2,1)S(1)}, u32[]{:S(2)}, u32[]{:S(2)}) %collective-permute-start.5) | collective-permute-done | bytes 524320 | tf_op jit(solution)/shard_map/ppermute | solution.py:400
  44.2 9.5 %collective-permute-done.rest_1_.rest_5_ = bf16[32,8192]{1,0:T(8,128)(2,1)S(1)} collective-permute-done((bf16[32,8192]{1,0:T(8,128)(2,1)}, bf16[32,8192]{1,0:T(8,128)(2,1)S(1)}, u32[]{:S(2)}, u32[]{:S(2)}) %collective-permute-start) | collective-permute-done | bytes 524320 | tf_op jit(solution)/shard_map/ppermute | solution.py:400
  53.7 0.9 copy-done.5
  54.6 0.1 copy.11.p_ref
  54.7 1.0 gram.4.rest_4_
  55.7 2.6 %collective-permute-done.2.rest_3_.rest_7_ = bf16[32,8192]{1,0:T(8,128)(2,1)} collective-permute-done((bf16[32,8192]{1,0:T(8,128)(2,1)}, bf16[32,8192]{1,0:T(8,128)(2,1)}, u32[]{:S(2)}, u32[]{:S(2)}) %collective-permute-start.2) | collective-permute-done | bytes 524320 | tf_op jit(solution)/shard_map/ppermute | solution.py:400
  58.3 2.2 %gram.5 = f32[2,24,128]{2,1,0:T(8,128)S(1)} custom-call(s32[2,8,1]{2,1,0:T(8,128)S(1)} %copy.11.p_ref, f32[1,16384]{1,0:T(1,128)S(1)} %bitcast.10, bf16[32,8192]{1,0:T(8,128)(2,1)S(1)} %copy-done.4, bf16[32,8192]{1,0:T(8,128)(2,1)S(1)} %copy-done.6, bf16[32,8192]{1,0:T(8,128)(2,1)} %collective-permute-done.1.rest_2_.rest_6_, ...), custom_call_target="tpu_custom_call" | custom-call | flops 536870912 | bytes 2097152 | tf_op jit(solution)/shard_map/gram/pallas_call | solution.py:172
  60.7 1.2 collective-permute-done.6
  61.9 0.8 broadcast_in_dim.6
  62.6 7.9 %all-to-all-start = ((f32[16,2,24,128]{3,2,1,0:T(8,128)}), f32[16,2,24,128]{3,2,1,0:T(8,128)}, u32[]{:S(2)}, u32[]{:S(2)}) async-start(f32[16,2,24,128]{3,2,1,0:T(8,128)} %broadcast_in_dim.6), calls=%async_computation | async-start | bytes 786432 | tf_op jit(solution)/shard_map/all_to_all | solution.py:375
  70.6 0.5 collective-permute-start.7
  71.1 1.4 collective-permute-start.8
  72.5 2.5 %collective-permute-start.9 = (bf16[32,8192]{1,0:T(8,128)(2,1)}, bf16[32,8192]{1,0:T(8,128)(2,1)}, u32[]{:S(2)}, u32[]{:S(2)}) collective-permute-start(bf16[32,8192]{1,0:T(8,128)(2,1)} %get-tuple-element.36), channel_id=1, source_target_pairs={{0,3},{1,0},{2,1},{3,2},{4,7},{5,4},{6,5},{7,6},{8,11},{9,8},{10,9... | collective-permute-start | bytes 1572872 | tf_op jit(solution)/shard_map/ppermute | solution.py:400
  75.2 14.1 %collective-permute-done.12.rest_3_ = bf16[32,8192]{1,0:T(8,128)(2,1)} collective-permute-done((bf16[32,8192]{1,0:T(8,128)(2,1)}, bf16[32,8192]{1,0:T(8,128)(2,1)}, u32[]{:S(2)}, u32[]{:S(2)}) %collective-permute-start.12) | collective-permute-done | bytes 524320 | tf_op jit(solution)/shard_map/ppermute | solution.py:400
  89.3 2.4 %gram.6.rest_4_ = f32[2,24,128]{2,1,0:T(8,128)S(1)} custom-call(s32[2,8,1]{2,1,0:T(8,128)S(1)} %copy.13.p_ref, f32[1,16384]{1,0:T(1,128)S(1)} %bitcast.11, bf16[32,8192]{1,0:T(8,128)(2,1)S(1)} %copy-done.1, bf16[32,8192]{1,0:T(8,128)(2,1)} %collective-permute-done.10.rest_1_, bf16[32,8192]{1,0:T(8,128)(2,1)} %collective-permute-done.11.rest_2_, ...), custom_call_target="tpu_custom_call" | custom-call | flops 536870912 | bytes 2097152 | tf_op jit(solution)/shard_map/gram/pallas_call | solution.py:172
  91.8 1.0 copy-done.7
  92.8 9.3 %modes.2 = (bf16[4,2,8,16384]{3,2,1,0:T(8,128)(2,1)}, f32[8,128]{1,0:T(8,128)S(1)}) custom-call(s32[3]{0:T(128)S(1)} %pad_add_fusion.place_ref, f32[4,2,8,128]{3,2,1,0:T(8,128)S(1)} %copy-done.9, f32[1,16384]{1,0:T(1,128)S(1)} %bitcast.12, s32[1,16384]{1,0:T(1,128)S(1)} %bitcast.15, f32[16,2,24,128]{3,2,1,0:T(8,128)} %all-to-all-done.sum_ref, ...), custom_call_target="tpu_custom_call" | custom-call | flops 2073741824 | bytes 5242880 | tf_op jit(solution)/shard_map/modes/pallas_call | solution.py:318
  102.2 2.4 %gram.7 = f32[2,24,128]{2,1,0:T(8,128)S(1)} custom-call(s32[2,8,1]{2,1,0:T(8,128)S(1)} %copy.13.p_ref, f32[1,16384]{1,0:T(1,128)S(1)} %bitcast.13, bf16[32,8192]{1,0:T(8,128)(2,1)S(1)} %copy-done.2, bf16[32,8192]{1,0:T(8,128)(2,1)} %collective-permute-done.7.rest_1_.rest_5_, bf16[32,8192]{1,0:T(8,128)(2,1)} %collective-permute-done.8.rest_2_.rest_6_, ...), custom_call_target="tpu_custom_call" | custom-call | flops 536870912 | bytes 2097152 | tf_op jit(solution)/shard_map/gram/pallas_call | solution.py:172
  104.6 1.2 collective-permute-done.13
  105.9 18.1 %all_to_all.15.sum_ref = f32[16,2,24,128]{3,2,1,0:T(8,128)S(1)} all-to-all(f32[16,2,24,128]{3,2,1,0:T(8,128)S(1)} %broadcast_in_dim.7), channel_id=1, replica_groups=mesh['z'=4,'x'=4,'core'=2,'blk'=4] {'z','x'}, dimensions={0} | all-to-all | bytes 786432 | tf_op jit(solution)/shard_map/all_to_all | solution.py:375
  124.0 9.8 %modes.3 = (bf16[4,2,8,16384]{3,2,1,0:T(8,128)(2,1)}, f32[8,128]{1,0:T(8,128)S(1)}) custom-call(s32[3]{0:T(128)S(1)} %pad_add_fusion.place_ref, f32[4,2,8,128]{3,2,1,0:T(8,128)S(1)} %copy-done.9, f32[1,16384]{1,0:T(1,128)S(1)} %bitcast.14, s32[1,16384]{1,0:T(1,128)S(1)} %bitcast.16, ...), custom_call_target="tpu_custom_call", output_to_operand_aliasing={{0}: (13, {})} | custom-call | flops 2073741824 | bytes 5242880 | tf_op jit(solution)/shard_map/modes/pallas_call | solution.py:318
  133.8 1.2 collective-permute-done.14
  135.0 10.9 %all_to_all.16.in_ref = f32[16,8,128]{2,1,0:T(8,128)} all-to-all(f32[16,8,128]{2,1,0:T(8,128)S(1)} %broadcast_in_dim.8), channel_id=1, replica_groups=mesh['z'=4,'x'=4,'core'=2,'blk'=4] {'z','x'}, dimensions={0} | all-to-all | bytes 131072 | tf_op jit(solution)/shard_map/all_to_all | solution.py:375
  145.9 1.6 %energy.1 = f32[4,8,384]{2,1,0:T(8,128)} custom-call(f32[16,8,128]{2,1,0:T(8,128)} %all_to_all.16.in_ref), custom_call_target="tpu_custom_call" | custom-call | tf_op jit(solution)/shard_map/energy/pallas_call | solution.py:364
  (44 shorter events, 0.6 us)
Async XLA Ops:
  6.3 25.0 %collective-permute-start.3 = (bf16[32,8192]{1,0:T(8,128)(2,1)}, bf16[32,8192]{1,0:T(8,128)(2,1)S(1)}, u32[]{:S(2)}, u32[]{:S(2)}) collective-permute-start(bf16[32,8192]{1,0:T(8,128)(2,1)} %get-tuple-element.28), channel_id=1, source_target_pairs={{0,1},{1,2},{2,3},{3,0},{4,5},{5,6},{6,7},{7,4},{8,9},{9,10},{10,1... | collective-permute-start | bytes 1572872 | tf_op jit(solution)/shard_map/ppermute | solution.py:400
  7.8 23.4 %collective-permute-start.4 = (bf16[32,8192]{1,0:T(8,128)(2,1)}, bf16[32,8192]{1,0:T(8,128)(2,1)S(1)}, u32[]{:S(2)}, u32[]{:S(2)}) collective-permute-start(bf16[32,8192]{1,0:T(8,128)(2,1)} %get-tuple-element.29), channel_id=1, source_target_pairs={{0,2},{1,3},{2,0},{3,1},{4,6},{5,7},{6,4},{7,5},{8,10},{9,11},{10,... | collective-permute-start | bytes 1572872 | tf_op jit(solution)/shard_map/ppermute | solution.py:400
  8.7 25.4 %copy-start.10 = (s32[4,8]{1,0:T(4,128)S(1)}, s32[4,8]{1,0:T(4,128)}, u32[]{:S(2)}) copy-start(s32[4,8]{1,0:T(4,128)} %param.10) | copy-start | bytes 388
  8.7 46.0 %copy-start = (f32[16384]{0:T(1024)S(1)}, f32[16384]{0:T(1024)}, u32[]{:S(2)}) copy-start(f32[16384]{0:T(1024)} %param.8) | copy-start | bytes 196612
  8.7 46.0 %copy-start.3 = (bf16[32,8192]{1,0:T(8,128)(2,1)S(1)}, bf16[32,8192]{1,0:T(8,128)(2,1)}, u32[]{:S(2)}) copy-start(bf16[32,8192]{1,0:T(8,128)(2,1)} %get-tuple-element.27.rest_0_) | copy-start | bytes 1572868
  8.7 35.5 %collective-permute-start.5 = (bf16[32,8192]{1,0:T(8,128)(2,1)}, bf16[32,8192]{1,0:T(8,128)(2,1)S(1)}, u32[]{:S(2)}, u32[]{:S(2)}) collective-permute-start(bf16[32,8192]{1,0:T(8,128)(2,1)} %get-tuple-element.30), channel_id=1, source_target_pairs={{0,3},{1,0},{2,1},{3,2},{4,7},{5,4},{6,5},{7,6},{8,11},{9,8},{10,9... | collective-permute-start | bytes 1572872 | tf_op jit(solution)/shard_map/ppermute | solution.py:400
  16.7 41.6 %copy-start.4 = (bf16[32,8192]{1,0:T(8,128)(2,1)S(1)}, bf16[32,8192]{1,0:T(8,128)(2,1)}, u32[]{:S(2)}) copy-start(bf16[32,8192]{1,0:T(8,128)(2,1)} %get-tuple-element.23.rest_0_.rest_4_) | copy-start | bytes 1572868
  16.7 37.0 %collective-permute-start = (bf16[32,8192]{1,0:T(8,128)(2,1)}, bf16[32,8192]{1,0:T(8,128)(2,1)S(1)}, u32[]{:S(2)}, u32[]{:S(2)}) collective-permute-start(bf16[32,8192]{1,0:T(8,128)(2,1)} %get-tuple-element.24), channel_id=1, source_target_pairs={{0,1},{1,2},{2,3},{3,0},{4,5},{5,6},{6,7},{7,4},{8,9},{9,10},{10,1... | collective-permute-start | bytes 1572872 | tf_op jit(solution)/shard_map/ppermute | solution.py:400
  16.8 38.9 %collective-permute-start.1 = (bf16[32,8192]{1,0:T(8,128)(2,1)}, bf16[32,8192]{1,0:T(8,128)(2,1)}, u32[]{:S(2)}, u32[]{:S(2)}) collective-permute-start(bf16[32,8192]{1,0:T(8,128)(2,1)} %get-tuple-element.25), channel_id=1, source_target_pairs={{0,2},{1,3},{2,0},{3,1},{4,6},{5,7},{6,4},{7,5},{8,10},{9,11},{10,... | collective-permute-start | bytes 1572872 | tf_op jit(solution)/shard_map/ppermute | solution.py:400
  31.3 27.1 %collective-permute-start.2 = (bf16[32,8192]{1,0:T(8,128)(2,1)}, bf16[32,8192]{1,0:T(8,128)(2,1)}, u32[]{:S(2)}, u32[]{:S(2)}) collective-permute-start(bf16[32,8192]{1,0:T(8,128)(2,1)} %get-tuple-element.26), channel_id=1, source_target_pairs={{0,3},{1,0},{2,1},{3,2},{4,7},{5,4},{6,5},{7,6},{8,11},{9,8},{10,9... | collective-permute-start | bytes 1572872 | tf_op jit(solution)/shard_map/ppermute | solution.py:400
  31.3 41.3 %collective-permute-start.10 = (bf16[32,8192]{1,0:T(8,128)(2,1)}, bf16[32,8192]{1,0:T(8,128)(2,1)}, u32[]{:S(2)}, u32[]{:S(2)}) collective-permute-start(bf16[32,8192]{1,0:T(8,128)(2,1)} %get-tuple-element.38), channel_id=1, source_target_pairs={{0,1},{1,2},{2,3},{3,0},{4,5},{5,6},{6,7},{7,4},{8,9},{9,10},{10,1... | collective-permute-start | bytes 1572872 | tf_op jit(solution)/shard_map/ppermute | solution.py:400
  44.2 31.0 %collective-permute-start.11 = (bf16[32,8192]{1,0:T(8,128)(2,1)}, bf16[32,8192]{1,0:T(8,128)(2,1)}, u32[]{:S(2)}, u32[]{:S(2)}) collective-permute-start(bf16[32,8192]{1,0:T(8,128)(2,1)} %get-tuple-element.39), channel_id=1, source_target_pairs={{0,2},{1,3},{2,0},{3,1},{4,6},{5,7},{6,4},{7,5},{8,10},{9,11},{10,... | collective-permute-start | bytes 1572872 | tf_op jit(solution)/shard_map/ppermute | solution.py:400
  53.7 0.9 copy-start.5
  54.6 34.8 %collective-permute-start.12 = (bf16[32,8192]{1,0:T(8,128)(2,1)}, bf16[32,8192]{1,0:T(8,128)(2,1)}, u32[]{:S(2)}, u32[]{:S(2)}) collective-permute-start(bf16[32,8192]{1,0:T(8,128)(2,1)} %get-tuple-element.40), channel_id=1, source_target_pairs={{0,3},{1,0},{2,1},{3,2},{4,7},{5,4},{6,5},{7,6},{8,11},{9,8},{10,9... | collective-permute-start | bytes 1572872 | tf_op jit(solution)/shard_map/ppermute | solution.py:400
  54.6 3.7 %copy-start.6 = (bf16[32,8192]{1,0:T(8,128)(2,1)S(1)}, bf16[32,8192]{1,0:T(8,128)(2,1)}, u32[]{:S(2)}) copy-start(bf16[32,8192]{1,0:T(8,128)(2,1)} %copy-done.5) | copy-start | bytes 1572868
  55.7 33.6 %copy-start.1 = (bf16[32,8192]{1,0:T(8,128)(2,1)S(1)}, bf16[32,8192]{1,0:T(8,128)(2,1)}, u32[]{:S(2)}) copy-start(bf16[32,8192]{1,0:T(8,128)(2,1)} %get-tuple-element.37.rest_0_) | copy-start | bytes 1572868
  60.6 31.2 %copy-start.8 = (s32[16384]{0:T(1024)S(1)}, s32[16384]{0:T(1024)}, u32[]{:S(2)}) copy-start(s32[16384]{0:T(1024)} %param.9) | copy-start | bytes 196612
  60.6 31.2 %copy-start.9 = (f32[4,2,8,128]{3,2,1,0:T(8,128)S(1)}, f32[4,2,8,128]{3,2,1,0:T(8,128)}, u32[]{:S(2)}) copy-start(f32[4,2,8,128]{3,2,1,0:T(8,128)} %constant.28.clone.start_ref) | copy-start | bytes 98308
  60.6 1.3 collective-permute-start.6
  62.6 29.1 %all-to-all-start = ((f32[16,2,24,128]{3,2,1,0:T(8,128)}), f32[16,2,24,128]{3,2,1,0:T(8,128)}, u32[]{:S(2)}, u32[]{:S(2)}) async-start(f32[16,2,24,128]{3,2,1,0:T(8,128)} %broadcast_in_dim.6), calls=%async_computation | async-start | bytes 786432 | tf_op jit(solution)/shard_map/all_to_all | solution.py:375
  70.6 31.6 %collective-permute-start.7 = (bf16[32,8192]{1,0:T(8,128)(2,1)}, bf16[32,8192]{1,0:T(8,128)(2,1)}, u32[]{:S(2)}, u32[]{:S(2)}) collective-permute-start(bf16[32,8192]{1,0:T(8,128)(2,1)} %get-tuple-element.34), channel_id=1, source_target_pairs={{0,1},{1,2},{2,3},{3,0},{4,5},{5,6},{6,7},{7,4},{8,9},{9,10},{10,1... | collective-permute-start | bytes 1572872 | tf_op jit(solution)/shard_map/ppermute | solution.py:400
  71.1 31.0 %collective-permute-start.8 = (bf16[32,8192]{1,0:T(8,128)(2,1)}, bf16[32,8192]{1,0:T(8,128)(2,1)}, u32[]{:S(2)}, u32[]{:S(2)}) collective-permute-start(bf16[32,8192]{1,0:T(8,128)(2,1)} %get-tuple-element.35), channel_id=1, source_target_pairs={{0,2},{1,3},{2,0},{3,1},{4,6},{5,7},{6,4},{7,5},{8,10},{9,11},{10,... | collective-permute-start | bytes 1572872 | tf_op jit(solution)/shard_map/ppermute | solution.py:400
  72.5 29.6 %collective-permute-start.9 = (bf16[32,8192]{1,0:T(8,128)(2,1)}, bf16[32,8192]{1,0:T(8,128)(2,1)}, u32[]{:S(2)}, u32[]{:S(2)}) collective-permute-start(bf16[32,8192]{1,0:T(8,128)(2,1)} %get-tuple-element.36), channel_id=1, source_target_pairs={{0,3},{1,0},{2,1},{3,2},{4,7},{5,4},{6,5},{7,6},{8,11},{9,8},{10,9... | collective-permute-start | bytes 1572872 | tf_op jit(solution)/shard_map/ppermute | solution.py:400
  91.8 1.0 copy-start.7
  92.8 9.4 %copy-start.2 = (bf16[32,8192]{1,0:T(8,128)(2,1)S(1)}, bf16[32,8192]{1,0:T(8,128)(2,1)}, u32[]{:S(2)}) copy-start(bf16[32,8192]{1,0:T(8,128)(2,1)} %get-tuple-element.33.rest_0_.rest_4_) | copy-start | bytes 1572868
  104.5 1.3 collective-permute-start.13
  133.7 1.2 collective-permute-start.14

commit v5 on v4

--- a/solution.py
+++ b/solution.py
@@ -152,6 +152,8 @@
         x_refs, rest = rest[:GROUPS], rest[GROUPS:]
         out_ref = rest[-1]
         lane = lax.broadcasted_iota(jnp.int32, (MODES, part), 1) + half * part
+        parts = []
+        pivots = []
         for f in range(PAIR):
             x = jnp.concatenate([r[16 * f : 16 * f + 16] for r in x_refs], axis=0)
             wx = x.astype(F32) * w_ref[:, half * part : (half + 1) * part]
@@ -164,14 +166,15 @@
             cross = other_lanes(other_rows(gram)) + jnp.where(same, gram, -gram)
             cross = jnp.where(low_rows((32, 128)), cross[:32], other_rows(cross[32:]))
             packed = jnp.where(low_lanes((16, 128)), cross[:16], cross[16:])
-            packed = jnp.concatenate([packed, total[64:72]], axis=0)
-            if before is not None:
-                packed = packed + rest[0][f]
-            out_ref[f] = packed
+            parts.append(packed)
+            pivots.append(total[64:72])
+        parts.append(jnp.where(low_lanes((MODES, 128)), pivots[0], pivots[1]))
+        result = jnp.concatenate(parts, axis=0)
+        out_ref[...] = result if before is None else result + rest[0][...]
 
     return pl.pallas_call(
         kernel,
-        out_shape=jax.ShapeDtypeStruct((PAIR, 24, 128), F32),
+        out_shape=jax.ShapeDtypeStruct((16 * PAIR + MODES, 128), F32),
         compiler_params=pltpu.CompilerParams(vmem_limit_bytes=SMALL),
         cost_estimate=pl.CostEstimate(
             flops=2 * PAIR * 64 * 256 * part, bytes_accessed=4 * 64 * part, transcendentals=0
@@ -249,7 +252,7 @@
         total = jnp.sum(sum_ref[...], axis=0)
         crosses = []
         for f in range(PAIR):
-            packed = total[f, :16] * (1.0 / row_count)
+            packed = total[16 * f : 16 * f + 16] * (1.0 / row_count)
             swap = pltpu.roll(packed, 64, 1)
             low = low_lanes(packed.shape)
             crosses.append(
@@ -262,7 +265,8 @@
         low = low_lanes(vec.shape)
         upper = jnp.where(odd, -vec, vec).astype(BF16).astype(F32)
         lower = jnp.where(odd, alt, -alt).astype(BF16).astype(F32)
-        at = jnp.where(low, total[:, 16:24], 0.0)
+        pivots = total[16 * PAIR :]
+        at = jnp.where(low, jnp.stack([pivots, pltpu.roll(pivots, 64, 1)]), 0.0)
         z_re = jnp.sum(upper * at, axis=2, keepdims=True)
         z_im = jnp.sum(lower * at, axis=2, keepdims=True)
         inverse = lax.rsqrt(z_re * z_re + z_im * z_im + 1.0)

time: 148 us -> 151 us (1.020)
  blocking collectives: 29 us -> 23.5 us
  waiting for transfers between devices: 50.9 us -> 56.4 us
  local copies, waits for them, and re-layouts: 2.93 us -> 5.08 us
    all_to_all x1, waiting for transfers between devices: 0.01 us -> 5.86 us  [gather_chips(): return lax.all_to_all(spread, ('z', 'x'), 0, 0, tiled=True)]
    all_to_all x2, blocking collectives: 29 us -> 23.5 us  [gather_chips(): return lax.all_to_all(spread, ('z', 'x'), 0, 0, tiled=True)]
    unnamed x22 -> x26, local copies, waits for them, and re-layouts: 1.94 us -> 4.12 us
where the time goes in v5:
time: 151 us
  waiting for transfers between devices  56.4 us (37%)
  Pallas kernels  39.7 us (26%)
  starting transfers between devices  25 us (17%)
  blocking collectives  23.5 us (16%)
  local copies, waits for them, and re-layouts  5.08 us (3%)
    ppermute x12, waiting for transfers between devices, per_device(): lax.ppermute(sent[k], 'blk', [(g, (g + k) % GROUPS) for g in range(GROUPS)])  48.2 us
    all_to_all x2, blocking collectives, gather_chips(): return lax.all_to_all(spread, ('z', 'x'), 0, 0, tiled=True)  23.5 us
    pallas_call x2, Pallas kernels, modes_call(): pl.pallas_call(kernel, in_specs=in_specs, out_specs=[raw, vmem], scratch_...  19 us
    ppermute x12, starting transfers between devices, per_device(): lax.ppermute(sent[k], 'blk', [(g, (g + k) % GROUPS) for g in range(GROUPS)])  16.8 us
    pallas_call x2, Pallas kernels, spectra_call(): pl.pallas_call(kernel, grid=(steps,), in_specs=[pl.BlockSpec((GROUPS, row...  11.1 us
    pallas_call x4, Pallas kernels, gram_call(): pl.pallas_call(kernel, out_shape=jax.ShapeDtypeStruct((16 * PAIR + MODES,...  8.02 us
    all_to_all x1, starting transfers between devices, gather_chips(): return lax.all_to_all(spread, ('z', 'x'), 0, 0, tiled=True)  7.9 us
    all_to_all x1, waiting for transfers between devices, gather_chips(): return lax.all_to_all(spread, ('z', 'x'), 0, 0, tiled=True)  5.86 us
  transfers between devices with their start and end apart: 16, of which 8 were waited for; matrix products, arithmetic and copies ran while one was open for 1% of the time, Pallas kernels for 14%

profile of v5, /device:TPU:8, one launch (start us, length us, event | category | flops | bytes accessed | tf_op | source)
XLA Modules:
  0.0 150.6 jit_solution(365581772503081038)
XLA Ops:
  0.6 5.6 %spectra.3 = (bf16[32,8192]{1,0:T(8,128)(2,1)}, bf16[32,8192]{1,0:T(8,128)(2,1)}, bf16[32,8192]{1,0:T(8,128)(2,1)}, bf16[32,8192]{1,0:T(8,128)(2,1)}, bf16[32,81...) custom-call(bf16[4,32,256]{2,1,0:T(8,128)(2,1)} %constant.29.clone.lhs_ref, ...), custom_call_target="tpu_custom_call" | custom-call | flops 1073741824 | bytes 12582912 | tf_op jit(solution)/shard_map/spectra/pallas_call | solution.py:98
  6.2 1.6 %collective-permute-start.3 = (bf16[32,8192]{1,0:T(8,128)(2,1)}, bf16[32,8192]{1,0:T(8,128)(2,1)S(1)}, u32[]{:S(2)}, u32[]{:S(2)}) collective-permute-start(bf16[32,8192]{1,0:T(8,128)(2,1)} %get-tuple-element.28), channel_id=1, source_target_pairs={{0,1},{1,2},{2,3},{3,0},{4,5},{5,6},{6,7},{7,4},{8,9},{9,10},{10,1... | collective-permute-start | bytes 1572872 | tf_op jit(solution)/shard_map/ppermute | solution.py:404
  7.8 0.9 collective-permute-start.4
  8.7 2.5 %collective-permute-start.5 = (bf16[32,8192]{1,0:T(8,128)(2,1)}, bf16[32,8192]{1,0:T(8,128)(2,1)S(1)}, u32[]{:S(2)}, u32[]{:S(2)}) collective-permute-start(bf16[32,8192]{1,0:T(8,128)(2,1)} %get-tuple-element.30), channel_id=1, source_target_pairs={{0,3},{1,0},{2,1},{3,2},{4,7},{5,4},{6,5},{7,6},{8,11},{9,8},{10,9... | collective-permute-start | bytes 1572872 | tf_op jit(solution)/shard_map/ppermute | solution.py:404
  11.2 5.5 %spectra.2 = (bf16[32,8192]{1,0:T(8,128)(2,1)}, bf16[32,8192]{1,0:T(8,128)(2,1)}, bf16[32,8192]{1,0:T(8,128)(2,1)}, bf16[32,8192]{1,0:T(8,128)(2,1)}, bf16[32,81...) custom-call(bf16[4,32,256]{2,1,0:T(8,128)(2,1)} %constant.29.clone.lhs_ref, ...), custom_call_target="tpu_custom_call" | custom-call | flops 1073741824 | bytes 12582912 | tf_op jit(solution)/shard_map/spectra/pallas_call | solution.py:98
  16.8 3.4 %collective-permute-start.1 = (bf16[32,8192]{1,0:T(8,128)(2,1)}, bf16[32,8192]{1,0:T(8,128)(2,1)}, u32[]{:S(2)}, u32[]{:S(2)}) collective-permute-start(bf16[32,8192]{1,0:T(8,128)(2,1)} %get-tuple-element.25), channel_id=1, source_target_pairs={{0,2},{1,3},{2,0},{3,1},{4,6},{5,7},{6,4},{7,5},{8,10},{9,11},{10,... | collective-permute-start | bytes 1572872 | tf_op jit(solution)/shard_map/ppermute | solution.py:404
  20.2 11.1 %collective-permute-done.3.rest_1_ = bf16[32,8192]{1,0:T(8,128)(2,1)S(1)} collective-permute-done((bf16[32,8192]{1,0:T(8,128)(2,1)}, bf16[32,8192]{1,0:T(8,128)(2,1)S(1)}, u32[]{:S(2)}, u32[]{:S(2)}) %collective-permute-start.3) | collective-permute-done | bytes 524320 | tf_op jit(solution)/shard_map/ppermute | solution.py:404
  31.3 2.8 %collective-permute-start.10 = (bf16[32,8192]{1,0:T(8,128)(2,1)}, bf16[32,8192]{1,0:T(8,128)(2,1)}, u32[]{:S(2)}, u32[]{:S(2)}) collective-permute-start(bf16[32,8192]{1,0:T(8,128)(2,1)} %get-tuple-element.38), channel_id=1, source_target_pairs={{0,1},{1,2},{2,3},{3,0},{4,5},{5,6},{6,7},{7,4},{8,9},{9,10},{10,1... | collective-permute-start | bytes 1572872 | tf_op jit(solution)/shard_map/ppermute | solution.py:404
  34.1 10.1 %collective-permute-done.5.rest_3_ = bf16[32,8192]{1,0:T(8,128)(2,1)S(1)} collective-permute-done((bf16[32,8192]{1,0:T(8,128)(2,1)}, bf16[32,8192]{1,0:T(8,128)(2,1)S(1)}, u32[]{:S(2)}, u32[]{:S(2)}) %collective-permute-start.5) | collective-permute-done | bytes 524320 | tf_op jit(solution)/shard_map/ppermute | solution.py:404
  44.2 9.5 %collective-permute-done.rest_1_.rest_5_ = bf16[32,8192]{1,0:T(8,128)(2,1)S(1)} collective-permute-done((bf16[32,8192]{1,0:T(8,128)(2,1)}, bf16[32,8192]{1,0:T(8,128)(2,1)S(1)}, u32[]{:S(2)}, u32[]{:S(2)}) %collective-permute-start) | collective-permute-done | bytes 524320 | tf_op jit(solution)/shard_map/ppermute | solution.py:404
  53.7 0.8 copy-done.5
  54.6 1.0 gram.4.rest_4_
  55.7 2.6 %collective-permute-done.2.rest_3_.rest_7_ = bf16[32,8192]{1,0:T(8,128)(2,1)} collective-permute-done((bf16[32,8192]{1,0:T(8,128)(2,1)}, bf16[32,8192]{1,0:T(8,128)(2,1)}, u32[]{:S(2)}, u32[]{:S(2)}) %collective-permute-start.2) | collective-permute-done | bytes 524320 | tf_op jit(solution)/shard_map/ppermute | solution.py:404
  58.3 2.2 %gram.5 = f32[40,128]{1,0:T(8,128)S(1)} custom-call(s32[2,8,1]{2,1,0:T(8,128)S(1)} %copy.11.p_ref, f32[1,16384]{1,0:T(1,128)S(1)} %bitcast.10, bf16[32,8192]{1,0:T(8,128)(2,1)S(1)} %copy-done.4, bf16[32,8192]{1,0:T(8,128)(2,1)S(1)} %copy-done.6, bf16[32,8192]{1,0:T(8,128)(2,1)} %collective-permute-done.1.rest_2_.rest_6_, ...), custom_call_target="tpu_custom_call" | custom-call | flops 536870912 | bytes 2097152 | tf_op jit(solution)/shard_map/gram/pallas_call | solution.py:175
  61.2 14.9 %collective-permute-done.10.rest_1_ = bf16[32,8192]{1,0:T(8,128)(2,1)} collective-permute-done((bf16[32,8192]{1,0:T(8,128)(2,1)}, bf16[32,8192]{1,0:T(8,128)(2,1)}, u32[]{:S(2)}, u32[]{:S(2)}) %collective-permute-start.10) | collective-permute-done | bytes 524320 | tf_op jit(solution)/shard_map/ppermute | solution.py:404
  76.1 5.0 %collective-permute-start.9 = (bf16[32,8192]{1,0:T(8,128)(2,1)}, bf16[32,8192]{1,0:T(8,128)(2,1)}, u32[]{:S(2)}, u32[]{:S(2)}) collective-permute-start(bf16[32,8192]{1,0:T(8,128)(2,1)} %get-tuple-element.36), channel_id=1, source_target_pairs={{0,3},{1,0},{2,1},{3,2},{4,7},{5,4},{6,5},{7,6},{8,11},{9,8},{10,9... | collective-permute-start | bytes 1572872 | tf_op jit(solution)/shard_map/ppermute | solution.py:404
  81.2 0.7 broadcast_in_dim.6
  81.9 7.9 %all-to-all-start = ((f32[16,40,128]{2,1,0:T(8,128)}), f32[16,40,128]{2,1,0:T(8,128)S(1)}, u32[]{:S(2)}, u32[]{:S(2)}) async-start(f32[16,40,128]{2,1,0:T(8,128)} %broadcast_in_dim.6), calls=%async_computation | async-start | bytes 655360 | tf_op jit(solution)/shard_map/all_to_all | solution.py:379
  90.0 2.4 %gram.6.rest_4_ = f32[40,128]{1,0:T(8,128)S(1)} custom-call(s32[2,8,1]{2,1,0:T(8,128)S(1)} %copy.13.p_ref, f32[1,16384]{1,0:T(1,128)S(1)} %bitcast.11, bf16[32,8192]{1,0:T(8,128)(2,1)S(1)} %copy-done.1, bf16[32,8192]{1,0:T(8,128)(2,1)} %collective-permute-done.10.rest_1_, bf16[32,8192]{1,0:T(8,128)(2,1)} %collective-permute-done.11.rest_2_, ...), custom_call_target="tpu_custom_call" | custom-call | flops 536870912 | bytes 2097152 | tf_op jit(solution)/shard_map/gram/pallas_call | solution.py:175
  92.4 0.6 copy-done.8
  93.0 5.9 %all-to-all-done.sum_ref = f32[16,40,128]{2,1,0:T(8,128)S(1)} async-done(((f32[16,40,128]{2,1,0:T(8,128)}), f32[16,40,128]{2,1,0:T(8,128)S(1)}, u32[]{:S(2)}, u32[]{:S(2)}) %all-to-all-start) | async-done | bytes 327712 | tf_op jit(solution)/shard_map/all_to_all | solution.py:379
  98.8 1.0 copy-done.7
  99.9 0.8 copy-done.10
  100.7 0.8 copy-done.11
  101.5 9.2 %modes.2 = (bf16[4,2,8,16384]{3,2,1,0:T(8,128)(2,1)}, f32[8,128]{1,0:T(8,128)S(1)}) custom-call(s32[3]{0:T(128)S(1)} %pad_add_fusion.place_ref, f32[4,2,8,128]{3,2,1,0:T(8,128)S(1)} %copy-done.11, f32[1,16384]{1,0:T(1,128)S(1)} %bitcast.12, s32[1,16384]{1,0:T(1,128)S(1)} %bitcast.15, f32[16,40,128]{2,1,0:T(8,128)S(1)} %all-to-all-done.sum_ref, ...), custom_call_target="tpu_custom_call" | custom-call | flops 2073741824 | bytes 5242880 | tf_op jit(solution)/shard_map/modes/pallas_call | solution.py:322
  110.7 2.4 %gram.7 = f32[40,128]{1,0:T(8,128)S(1)} custom-call(s32[2,8,1]{2,1,0:T(8,128)S(1)} %copy.13.p_ref, f32[1,16384]{1,0:T(1,128)S(1)} %bitcast.13, bf16[32,8192]{1,0:T(8,128)(2,1)S(1)} %copy-done.2, bf16[32,8192]{1,0:T(8,128)(2,1)} %collective-permute-done.7.rest_1_.rest_5_, bf16[32,8192]{1,0:T(8,128)(2,1)} %collective-permute-done.8.rest_2_.rest_6_, ...), custom_call_target="tpu_custom_call" | custom-call | flops 536870912 | bytes 2097152 | tf_op jit(solution)/shard_map/gram/pallas_call | solution.py:175
  113.2 1.2 collective-permute-done.13
  114.4 12.6 %all_to_all.15.sum_ref = f32[16,40,128]{2,1,0:T(8,128)S(1)} all-to-all(f32[16,40,128]{2,1,0:T(8,128)S(1)} %broadcast_in_dim.7), channel_id=1, replica_groups=mesh['z'=4,'x'=4,'core'=2,'blk'=4] {'z','x'}, dimensions={0} | all-to-all | bytes 655360 | tf_op jit(solution)/shard_map/all_to_all | solution.py:379
  127.0 9.8 %modes.3 = (bf16[4,2,8,16384]{3,2,1,0:T(8,128)(2,1)}, f32[8,128]{1,0:T(8,128)S(1)}) custom-call(s32[3]{0:T(128)S(1)} %pad_add_fusion.place_ref, f32[4,2,8,128]{3,2,1,0:T(8,128)S(1)} %copy-done.11, f32[1,16384]{1,0:T(1,128)S(1)} %bitcast.14, s32[1,16384]{1,0:T(1,128)S(1)} %bitcast.16, ...), custom_call_target="tpu_custom_call", output_to_operand_aliasing={{0}: (13, {})} | custom-call | flops 2073741824 | bytes 5242880 | tf_op jit(solution)/shard_map/modes/pallas_call | solution.py:322
  136.9 1.2 collective-permute-done.14
  138.1 10.9 %all_to_all.16.in_ref = f32[16,8,128]{2,1,0:T(8,128)} all-to-all(f32[16,8,128]{2,1,0:T(8,128)S(1)} %broadcast_in_dim.8), channel_id=1, replica_groups=mesh['z'=4,'x'=4,'core'=2,'blk'=4] {'z','x'}, dimensions={0} | all-to-all | bytes 131072 | tf_op jit(solution)/shard_map/all_to_all | solution.py:379
  149.0 1.6 %energy.1 = f32[4,8,384]{2,1,0:T(8,128)} custom-call(f32[16,8,128]{2,1,0:T(8,128)} %all_to_all.16.in_ref), custom_call_target="tpu_custom_call" | custom-call | tf_op jit(solution)/shard_map/energy/pallas_call | solution.py:368
  (48 shorter events, 1.3 us)
Async XLA Ops:
  6.2 25.0 %collective-permute-start.3 = (bf16[32,8192]{1,0:T(8,128)(2,1)}, bf16[32,8192]{1,0:T(8,128)(2,1)S(1)}, u32[]{:S(2)}, u32[]{:S(2)}) collective-permute-start(bf16[32,8192]{1,0:T(8,128)(2,1)} %get-tuple-element.28), channel_id=1, source_target_pairs={{0,1},{1,2},{2,3},{3,0},{4,5},{5,6},{6,7},{7,4},{8,9},{9,10},{10,1... | collective-permute-start | bytes 1572872 | tf_op jit(solution)/shard_map/ppermute | solution.py:404
  7.8 23.4 %collective-permute-start.4 = (bf16[32,8192]{1,0:T(8,128)(2,1)}, bf16[32,8192]{1,0:T(8,128)(2,1)S(1)}, u32[]{:S(2)}, u32[]{:S(2)}) collective-permute-start(bf16[32,8192]{1,0:T(8,128)(2,1)} %get-tuple-element.29), channel_id=1, source_target_pairs={{0,2},{1,3},{2,0},{3,1},{4,6},{5,7},{6,4},{7,5},{8,10},{9,11},{10,... | collective-permute-start | bytes 1572872 | tf_op jit(solution)/shard_map/ppermute | solution.py:404
  8.7 25.4 %copy-start.12 = (s32[4,8]{1,0:T(4,128)S(1)}, s32[4,8]{1,0:T(4,128)}, u32[]{:S(2)}) copy-start(s32[4,8]{1,0:T(4,128)} %param.10) | copy-start | bytes 388
  8.7 45.9 %copy-start = (f32[16384]{0:T(1024)S(1)}, f32[16384]{0:T(1024)}, u32[]{:S(2)}) copy-start(f32[16384]{0:T(1024)} %param.8) | copy-start | bytes 196612
  8.7 45.9 %copy-start.3 = (bf16[32,8192]{1,0:T(8,128)(2,1)S(1)}, bf16[32,8192]{1,0:T(8,128)(2,1)}, u32[]{:S(2)}) copy-start(bf16[32,8192]{1,0:T(8,128)(2,1)} %get-tuple-element.27.rest_0_) | copy-start | bytes 1572868
  8.7 35.5 %collective-permute-start.5 = (bf16[32,8192]{1,0:T(8,128)(2,1)}, bf16[32,8192]{1,0:T(8,128)(2,1)S(1)}, u32[]{:S(2)}, u32[]{:S(2)}) collective-permute-start(bf16[32,8192]{1,0:T(8,128)(2,1)} %get-tuple-element.30), channel_id=1, source_target_pairs={{0,3},{1,0},{2,1},{3,2},{4,7},{5,4},{6,5},{7,6},{8,11},{9,8},{10,9... | collective-permute-start | bytes 1572872 | tf_op jit(solution)/shard_map/ppermute | solution.py:404
  16.7 41.6 %copy-start.4 = (bf16[32,8192]{1,0:T(8,128)(2,1)S(1)}, bf16[32,8192]{1,0:T(8,128)(2,1)}, u32[]{:S(2)}) copy-start(bf16[32,8192]{1,0:T(8,128)(2,1)} %get-tuple-element.23.rest_0_.rest_4_) | copy-start | bytes 1572868
  16.7 37.0 %collective-permute-start = (bf16[32,8192]{1,0:T(8,128)(2,1)}, bf16[32,8192]{1,0:T(8,128)(2,1)S(1)}, u32[]{:S(2)}, u32[]{:S(2)}) collective-permute-start(bf16[32,8192]{1,0:T(8,128)(2,1)} %get-tuple-element.24), channel_id=1, source_target_pairs={{0,1},{1,2},{2,3},{3,0},{4,5},{5,6},{6,7},{7,4},{8,9},{9,10},{10,1... | collective-permute-start | bytes 1572872 | tf_op jit(solution)/shard_map/ppermute | solution.py:404
  16.8 38.9 %collective-permute-start.1 = (bf16[32,8192]{1,0:T(8,128)(2,1)}, bf16[32,8192]{1,0:T(8,128)(2,1)}, u32[]{:S(2)}, u32[]{:S(2)}) collective-permute-start(bf16[32,8192]{1,0:T(8,128)(2,1)} %get-tuple-element.25), channel_id=1, source_target_pairs={{0,2},{1,3},{2,0},{3,1},{4,6},{5,7},{6,4},{7,5},{8,10},{9,11},{10,... | collective-permute-start | bytes 1572872 | tf_op jit(solution)/shard_map/ppermute | solution.py:404
  31.2 27.1 %collective-permute-start.2 = (bf16[32,8192]{1,0:T(8,128)(2,1)}, bf16[32,8192]{1,0:T(8,128)(2,1)}, u32[]{:S(2)}, u32[]{:S(2)}) collective-permute-start(bf16[32,8192]{1,0:T(8,128)(2,1)} %get-tuple-element.26), channel_id=1, source_target_pairs={{0,3},{1,0},{2,1},{3,2},{4,7},{5,4},{6,5},{7,6},{8,11},{9,8},{10,9... | collective-permute-start | bytes 1572872 | tf_op jit(solution)/shard_map/ppermute | solution.py:404
  31.3 44.8 %collective-permute-start.10 = (bf16[32,8192]{1,0:T(8,128)(2,1)}, bf16[32,8192]{1,0:T(8,128)(2,1)}, u32[]{:S(2)}, u32[]{:S(2)}) collective-permute-start(bf16[32,8192]{1,0:T(8,128)(2,1)} %get-tuple-element.38), channel_id=1, source_target_pairs={{0,1},{1,2},{2,3},{3,0},{4,5},{5,6},{6,7},{7,4},{8,9},{9,10},{10,1... | collective-permute-start | bytes 1572872 | tf_op jit(solution)/shard_map/ppermute | solution.py:404
  44.2 45.8 %collective-permute-start.11 = (bf16[32,8192]{1,0:T(8,128)(2,1)}, bf16[32,8192]{1,0:T(8,128)(2,1)}, u32[]{:S(2)}, u32[]{:S(2)}) collective-permute-start(bf16[32,8192]{1,0:T(8,128)(2,1)} %get-tuple-element.39), channel_id=1, source_target_pairs={{0,2},{1,3},{2,0},{3,1},{4,6},{5,7},{6,4},{7,5},{8,10},{9,11},{10,... | collective-permute-start | bytes 1572872 | tf_op jit(solution)/shard_map/ppermute | solution.py:404
  53.7 0.8 copy-start.5
  54.5 35.5 %collective-permute-start.12 = (bf16[32,8192]{1,0:T(8,128)(2,1)}, bf16[32,8192]{1,0:T(8,128)(2,1)}, u32[]{:S(2)}, u32[]{:S(2)}) collective-permute-start(bf16[32,8192]{1,0:T(8,128)(2,1)} %get-tuple-element.40), channel_id=1, source_target_pairs={{0,3},{1,0},{2,1},{3,2},{4,7},{5,4},{6,5},{7,6},{8,11},{9,8},{10,9... | collective-permute-start | bytes 1572872 | tf_op jit(solution)/shard_map/ppermute | solution.py:404
  54.6 3.7 %copy-start.6 = (bf16[32,8192]{1,0:T(8,128)(2,1)S(1)}, bf16[32,8192]{1,0:T(8,128)(2,1)}, u32[]{:S(2)}) copy-start(bf16[32,8192]{1,0:T(8,128)(2,1)} %copy-done.5) | copy-start | bytes 1572868
  55.7 34.3 %copy-start.1 = (bf16[32,8192]{1,0:T(8,128)(2,1)S(1)}, bf16[32,8192]{1,0:T(8,128)(2,1)}, u32[]{:S(2)}) copy-start(bf16[32,8192]{1,0:T(8,128)(2,1)} %get-tuple-element.37.rest_0_) | copy-start | bytes 1572868
  60.5 15.6 %collective-permute-start.6 = (f32[40,128]{1,0:T(8,128)S(1)}, f32[40,128]{1,0:T(8,128)S(1)}, u32[]{:S(2)}, u32[]{:S(2)}) collective-permute-start(f32[40,128]{1,0:T(8,128)S(1)} %gram.5), channel_id=1, source_target_pairs={{0,4},{4,0},{1,5},{5,1},{2,6},{6,2},{3,7},{7,3},{8,12},{12,8},{9,1... | collective-permute-start | bytes 61448 | tf_op jit(solution)/shard_map/ppermute | solution.py:376
  60.6 50.1 %collective-permute-start.7 = (bf16[32,8192]{1,0:T(8,128)(2,1)}, bf16[32,8192]{1,0:T(8,128)(2,1)}, u32[]{:S(2)}, u32[]{:S(2)}) collective-permute-start(bf16[32,8192]{1,0:T(8,128)(2,1)} %get-tuple-element.34), channel_id=1, source_target_pairs={{0,1},{1,2},{2,3},{3,0},{4,5},{5,6},{6,7},{7,4},{8,9},{9,10},{10,1... | collective-permute-start | bytes 1572872 | tf_op jit(solution)/shard_map/ppermute | solution.py:404
  76.1 34.6 %collective-permute-start.8 = (bf16[32,8192]{1,0:T(8,128)(2,1)}, bf16[32,8192]{1,0:T(8,128)(2,1)}, u32[]{:S(2)}, u32[]{:S(2)}) collective-permute-start(bf16[32,8192]{1,0:T(8,128)(2,1)} %get-tuple-element.35), channel_id=1, source_target_pairs={{0,2},{1,3},{2,0},{3,1},{4,6},{5,7},{6,4},{7,5},{8,10},{9,11},{10,... | collective-permute-start | bytes 1572872 | tf_op jit(solution)/shard_map/ppermute | solution.py:404
  76.1 34.6 %collective-permute-start.9 = (bf16[32,8192]{1,0:T(8,128)(2,1)}, bf16[32,8192]{1,0:T(8,128)(2,1)}, u32[]{:S(2)}, u32[]{:S(2)}) collective-permute-start(bf16[32,8192]{1,0:T(8,128)(2,1)} %get-tuple-element.36), channel_id=1, source_target_pairs={{0,3},{1,0},{2,1},{3,2},{4,7},{5,4},{6,5},{7,6},{8,11},{9,8},{10,9... | collective-permute-start | bytes 1572872 | tf_op jit(solution)/shard_map/ppermute | solution.py:404
  81.9 16.9 %all-to-all-start = ((f32[16,40,128]{2,1,0:T(8,128)}), f32[16,40,128]{2,1,0:T(8,128)S(1)}, u32[]{:S(2)}, u32[]{:S(2)}) async-start(f32[16,40,128]{2,1,0:T(8,128)} %broadcast_in_dim.6), calls=%async_computation | async-start | bytes 655360 | tf_op jit(solution)/shard_map/all_to_all | solution.py:379
  92.4 0.6 copy-start.8
  98.8 1.0 copy-start.7
  99.9 0.8 copy-start.10
  100.7 0.8 copy-start.11
  101.5 9.2 %copy-start.2 = (bf16[32,8192]{1,0:T(8,128)(2,1)S(1)}, bf16[32,8192]{1,0:T(8,128)(2,1)}, u32[]{:S(2)}) copy-start(bf16[32,8192]{1,0:T(8,128)(2,1)} %get-tuple-element.33.rest_0_.rest_4_) | copy-start | bytes 1572868
  101.5 9.3 %copy-start.9 = (f32[40,128]{1,0:T(8,128)S(1)}, f32[40,128]{1,0:T(8,128)}, u32[]{:S(2)}) copy-start(f32[40,128]{1,0:T(8,128)} %copy-done.8) | copy-start | bytes 61444
  113.1 1.3 collective-permute-start.13
  136.8 1.2 collective-permute-start.14

commit v6 on v4

--- a/solution.py
+++ b/solution.py
@@ -245,7 +245,12 @@
 
     def kernel(place_ref, start_ref, w_ref, deg_ref, sum_ref, *rest):
         x_refs, rest = rest[: HALVES * GROUPS], rest[HALVES * GROUPS :]
-        modes_ref, energy_ref, stage, sems = rest[-4:]
+        modes_ref, energy_ref, stage, held, sems, x_sems = rest[-6:]
+        fetches = []
+        for i, r in enumerate(x_refs):
+            fetch = pltpu.make_async_copy(r, held.at[i], x_sems.at[i])
+            fetch.start()
+            fetches.append(fetch)
         total = jnp.sum(sum_ref[...], axis=0)
         crosses = []
         for f in range(PAIR):
@@ -274,6 +279,8 @@
         lane = lax.broadcasted_iota(jnp.int32, (MODES, 128), 1)
         copies = []
         for half in range(HALVES):
+            for fetch in fetches[GROUPS * half : GROUPS * half + GROUPS]:
+                fetch.wait()
             span = slice(half * tile, (half + 1) * tile)
             w = w_ref[:, span]
             level_of = deg_ref[:, span]
@@ -282,7 +289,7 @@
             for f in range(PAIR):
                 rows = slice(16 * f, 16 * f + 16)
                 x = jnp.concatenate(
-                    [r[rows] for r in x_refs[GROUPS * half : GROUPS * half + GROUPS]], axis=0
+                    [held[GROUPS * half + k, rows] for k in range(GROUPS)], axis=0
                 )
                 psi = jnp.dot(expand[f][:, :64], x, preferred_element_type=F32)
                 p_re, p_im = psi[:8], psi[8:]
@@ -309,7 +316,8 @@
     vmem = pl.BlockSpec(memory_space=pltpu.VMEM)
     raw = pl.BlockSpec(memory_space=pl.ANY)
     args = [place, start, weights, degrees, sums, *early, *late]
-    in_specs = [pl.BlockSpec(memory_space=pltpu.SMEM)] + [vmem] * (len(args) - 1)
+    source = pl.BlockSpec(memory_space=pltpu.HBM)
+    in_specs = [pl.BlockSpec(memory_space=pltpu.SMEM)] + [vmem] * 4 + [source] * (HALVES * GROUPS)
     aliases = {}
     if before is not None:
         in_specs += [raw, vmem]
@@ -321,7 +329,9 @@
         out_specs=[raw, vmem],
         scratch_shapes=[
             pltpu.VMEM((HALVES, PAIR, 2, MODES, tile), BF16),
+            pltpu.VMEM((HALVES * GROUPS, 16 * PAIR, tile), BF16),
             pltpu.SemaphoreType.DMA((HALVES,)),
+            pltpu.SemaphoreType.DMA((HALVES * GROUPS,)),
         ],
         out_shape=[
             jax.ShapeDtypeStruct((OWNED, 2, MODES, rows_dev), BF16),

time: 148 us -> 147 us (level)
  no operation moved by 1% of the time
where the time goes in v6:
time: 147 us
  waiting for transfers between devices  50.9 us (35%)
  Pallas kernels  39.1 us (27%)
  blocking collectives  29 us (20%)
  starting transfers between devices  23.9 us (16%)
  local copies, waits for them, and re-layouts  2.93 us (2%)
    ppermute x12, waiting for transfers between devices, per_device(): lax.ppermute(sent[k], 'blk', [(g, (g + k) % GROUPS) for g in range(GROUPS)])  47.4 us
    all_to_all x2, blocking collectives, gather_chips(): return lax.all_to_all(spread, ('z', 'x'), 0, 0, tiled=True)  29 us
    pallas_call x2, Pallas kernels, modes_call(): pl.pallas_call(kernel, in_specs=in_specs, out_specs=[raw, vmem], scratch_...  18.4 us
    ppermute x12, starting transfers between devices, per_device(): lax.ppermute(sent[k], 'blk', [(g, (g + k) % GROUPS) for g in range(GROUPS)])  15.7 us
    pallas_call x2, Pallas kernels, spectra_call(): pl.pallas_call(kernel, grid=(steps,), in_specs=[pl.BlockSpec((GROUPS, row...  11.1 us
    pallas_call x4, Pallas kernels, gram_call(): pl.pallas_call(kernel, out_shape=jax.ShapeDtypeStruct((PAIR, 24, 128), F3...  8.01 us
    all_to_all x1, starting transfers between devices, gather_chips(): return lax.all_to_all(spread, ('z', 'x'), 0, 0, tiled=True)  7.93 us
    ppermute x3, waiting for transfers between devices, gather_chips(): value = value + lax.ppermute(value, 'core', [(0, 1), (1, 0)])  3.52 us
  transfers between devices with their start and end apart: 16, of which 8 were waited for; matrix products, arithmetic and copies ran while one was open for 1% of the time, Pallas kernels for 14%

profile of v6, /device:TPU:8, one launch (start us, length us, event | category | flops | bytes accessed | tf_op | source)
XLA Modules:
  0.0 146.8 jit_solution(9118938011961103802)
XLA Ops:
  0.6 5.6 %spectra.3 = (bf16[32,8192]{1,0:T(8,128)(2,1)}, bf16[32,8192]{1,0:T(8,128)(2,1)}, bf16[32,8192]{1,0:T(8,128)(2,1)}, bf16[32,8192]{1,0:T(8,128)(2,1)}, bf16[32,81...) custom-call(bf16[4,32,256]{2,1,0:T(8,128)(2,1)} %constant.29.clone.lhs_ref, ...), custom_call_target="tpu_custom_call" | custom-call | flops 1073741824 | bytes 12582912 | tf_op jit(solution)/shard_map/spectra/pallas_call | solution.py:98
  6.3 1.6 %collective-permute-start.3 = (bf16[32,8192]{1,0:T(8,128)(2,1)}, bf16[32,8192]{1,0:T(8,128)(2,1)S(1)}, u32[]{:S(2)}, u32[]{:S(2)}) collective-permute-start(bf16[32,8192]{1,0:T(8,128)(2,1)} %get-tuple-element.28), channel_id=1, source_target_pairs={{0,1},{1,2},{2,3},{3,0},{4,5},{5,6},{6,7},{7,4},{8,9},{9,10},{10,1... | collective-permute-start | bytes 1572872 | tf_op jit(solution)/shard_map/ppermute | solution.py:410
  7.8 0.9 collective-permute-start.4
  8.7 2.5 %collective-permute-start.5 = (bf16[32,8192]{1,0:T(8,128)(2,1)}, bf16[32,8192]{1,0:T(8,128)(2,1)S(1)}, u32[]{:S(2)}, u32[]{:S(2)}) collective-permute-start(bf16[32,8192]{1,0:T(8,128)(2,1)} %get-tuple-element.30), channel_id=1, source_target_pairs={{0,3},{1,0},{2,1},{3,2},{4,7},{5,4},{6,5},{7,6},{8,11},{9,8},{10,9... | collective-permute-start | bytes 1572872 | tf_op jit(solution)/shard_map/ppermute | solution.py:410
  11.2 5.5 %spectra.2 = (bf16[32,8192]{1,0:T(8,128)(2,1)}, bf16[32,8192]{1,0:T(8,128)(2,1)}, bf16[32,8192]{1,0:T(8,128)(2,1)}, bf16[32,8192]{1,0:T(8,128)(2,1)}, bf16[32,81...) custom-call(bf16[4,32,256]{2,1,0:T(8,128)(2,1)} %constant.29.clone.lhs_ref, ...), custom_call_target="tpu_custom_call" | custom-call | flops 1073741824 | bytes 12582912 | tf_op jit(solution)/shard_map/spectra/pallas_call | solution.py:98
  16.8 3.4 %collective-permute-start.1 = (bf16[32,8192]{1,0:T(8,128)(2,1)}, bf16[32,8192]{1,0:T(8,128)(2,1)}, u32[]{:S(2)}, u32[]{:S(2)}) collective-permute-start(bf16[32,8192]{1,0:T(8,128)(2,1)} %get-tuple-element.25), channel_id=1, source_target_pairs={{0,2},{1,3},{2,0},{3,1},{4,6},{5,7},{6,4},{7,5},{8,10},{9,11},{10,... | collective-permute-start | bytes 1572872 | tf_op jit(solution)/shard_map/ppermute | solution.py:410
  20.2 11.1 %collective-permute-done.3.rest_1_ = bf16[32,8192]{1,0:T(8,128)(2,1)S(1)} collective-permute-done((bf16[32,8192]{1,0:T(8,128)(2,1)}, bf16[32,8192]{1,0:T(8,128)(2,1)S(1)}, u32[]{:S(2)}, u32[]{:S(2)}) %collective-permute-start.3) | collective-permute-done | bytes 524320 | tf_op jit(solution)/shard_map/ppermute | solution.py:410
  31.3 2.8 %collective-permute-start.10 = (bf16[32,8192]{1,0:T(8,128)(2,1)}, bf16[32,8192]{1,0:T(8,128)(2,1)}, u32[]{:S(2)}, u32[]{:S(2)}) collective-permute-start(bf16[32,8192]{1,0:T(8,128)(2,1)} %get-tuple-element.38), channel_id=1, source_target_pairs={{0,1},{1,2},{2,3},{3,0},{4,5},{5,6},{6,7},{7,4},{8,9},{9,10},{10,1... | collective-permute-start | bytes 1572872 | tf_op jit(solution)/shard_map/ppermute | solution.py:410
  34.1 10.1 %collective-permute-done.5.rest_3_ = bf16[32,8192]{1,0:T(8,128)(2,1)S(1)} collective-permute-done((bf16[32,8192]{1,0:T(8,128)(2,1)}, bf16[32,8192]{1,0:T(8,128)(2,1)S(1)}, u32[]{:S(2)}, u32[]{:S(2)}) %collective-permute-start.5) | collective-permute-done | bytes 524320 | tf_op jit(solution)/shard_map/ppermute | solution.py:410
  44.2 9.5 %collective-permute-done.rest_1_.rest_5_ = bf16[32,8192]{1,0:T(8,128)(2,1)S(1)} collective-permute-done((bf16[32,8192]{1,0:T(8,128)(2,1)}, bf16[32,8192]{1,0:T(8,128)(2,1)S(1)}, u32[]{:S(2)}, u32[]{:S(2)}) %collective-permute-start) | collective-permute-done | bytes 524320 | tf_op jit(solution)/shard_map/ppermute | solution.py:410
  53.7 0.9 copy-done.5
  54.6 0.1 copy.11.p_ref
  54.7 1.0 gram.4.rest_4_
  55.7 2.6 %collective-permute-done.2.rest_3_.rest_7_ = bf16[32,8192]{1,0:T(8,128)(2,1)} collective-permute-done((bf16[32,8192]{1,0:T(8,128)(2,1)}, bf16[32,8192]{1,0:T(8,128)(2,1)}, u32[]{:S(2)}, u32[]{:S(2)}) %collective-permute-start.2) | collective-permute-done | bytes 524320 | tf_op jit(solution)/shard_map/ppermute | solution.py:410
  58.3 2.2 %gram.5 = f32[2,24,128]{2,1,0:T(8,128)S(1)} custom-call(s32[2,8,1]{2,1,0:T(8,128)S(1)} %copy.11.p_ref, f32[1,16384]{1,0:T(1,128)S(1)} %bitcast.10, bf16[32,8192]{1,0:T(8,128)(2,1)S(1)} %copy-done.4, bf16[32,8192]{1,0:T(8,128)(2,1)S(1)} %copy-done.6, bf16[32,8192]{1,0:T(8,128)(2,1)} %collective-permute-done.1.rest_2_.rest_6_, ...), custom_call_target="tpu_custom_call" | custom-call | flops 536870912 | bytes 2097152 | tf_op jit(solution)/shard_map/gram/pallas_call | solution.py:172
  60.7 1.2 collective-permute-done.6
  61.9 0.8 broadcast_in_dim.6
  62.6 7.9 %all-to-all-start = ((f32[16,2,24,128]{3,2,1,0:T(8,128)}), f32[16,2,24,128]{3,2,1,0:T(8,128)}, u32[]{:S(2)}, u32[]{:S(2)}) async-start(f32[16,2,24,128]{3,2,1,0:T(8,128)} %broadcast_in_dim.6), calls=%async_computation | async-start | bytes 786432 | tf_op jit(solution)/shard_map/all_to_all | solution.py:385
  70.6 0.5 collective-permute-start.7
  71.1 1.4 collective-permute-start.8
  72.5 2.5 %collective-permute-start.9 = (bf16[32,8192]{1,0:T(8,128)(2,1)}, bf16[32,8192]{1,0:T(8,128)(2,1)}, u32[]{:S(2)}, u32[]{:S(2)}) collective-permute-start(bf16[32,8192]{1,0:T(8,128)(2,1)} %get-tuple-element.36), channel_id=1, source_target_pairs={{0,3},{1,0},{2,1},{3,2},{4,7},{5,4},{6,5},{7,6},{8,11},{9,8},{10,9... | collective-permute-start | bytes 1572872 | tf_op jit(solution)/shard_map/ppermute | solution.py:410
  75.2 14.1 %collective-permute-done.12.rest_3_ = bf16[32,8192]{1,0:T(8,128)(2,1)} collective-permute-done((bf16[32,8192]{1,0:T(8,128)(2,1)}, bf16[32,8192]{1,0:T(8,128)(2,1)}, u32[]{:S(2)}, u32[]{:S(2)}) %collective-permute-start.12) | collective-permute-done | bytes 524320 | tf_op jit(solution)/shard_map/ppermute | solution.py:410
  89.3 2.4 %gram.6.rest_4_ = f32[2,24,128]{2,1,0:T(8,128)S(1)} custom-call(s32[2,8,1]{2,1,0:T(8,128)S(1)} %copy.13.p_ref, f32[1,16384]{1,0:T(1,128)S(1)} %bitcast.11, bf16[32,8192]{1,0:T(8,128)(2,1)S(1)} %copy-done.1, bf16[32,8192]{1,0:T(8,128)(2,1)} %collective-permute-done.10.rest_1_, bf16[32,8192]{1,0:T(8,128)(2,1)} %collective-permute-done.11.rest_2_, ...), custom_call_target="tpu_custom_call" | custom-call | flops 536870912 | bytes 2097152 | tf_op jit(solution)/shard_map/gram/pallas_call | solution.py:172
  91.8 1.0 copy-done.7
  92.8 9.4 %modes.2 = (bf16[4,2,8,16384]{3,2,1,0:T(8,128)(2,1)}, f32[8,128]{1,0:T(8,128)S(1)}) custom-call(s32[3]{0:T(128)S(1)} %pad_add_fusion.place_ref, f32[4,2,8,128]{3,2,1,0:T(8,128)S(1)} %copy-done.9, f32[1,16384]{1,0:T(1,128)S(1)} %bitcast.12, s32[1,16384]{1,0:T(1,128)S(1)} %bitcast.15, f32[16,2,24,128]{3,2,1,0:T(8,128)} %all-to-all-done.sum_ref, ...), custom_call_target="tpu_custom_call" | custom-call | flops 2073741824 | bytes 5242880 | tf_op jit(solution)/shard_map/modes/pallas_call | solution.py:326
  102.3 2.4 %gram.7 = f32[2,24,128]{2,1,0:T(8,128)S(1)} custom-call(s32[2,8,1]{2,1,0:T(8,128)S(1)} %copy.13.p_ref, f32[1,16384]{1,0:T(1,128)S(1)} %bitcast.13, bf16[32,8192]{1,0:T(8,128)(2,1)S(1)} %copy-done.2, bf16[32,8192]{1,0:T(8,128)(2,1)} %collective-permute-done.7.rest_1_.rest_5_, bf16[32,8192]{1,0:T(8,128)(2,1)} %collective-permute-done.8.rest_2_.rest_6_, ...), custom_call_target="tpu_custom_call" | custom-call | flops 536870912 | bytes 2097152 | tf_op jit(solution)/shard_map/gram/pallas_call | solution.py:172
  104.7 1.2 collective-permute-done.13
  106.0 18.1 %all_to_all.15.sum_ref = f32[16,2,24,128]{3,2,1,0:T(8,128)S(1)} all-to-all(f32[16,2,24,128]{3,2,1,0:T(8,128)S(1)} %broadcast_in_dim.7), channel_id=1, replica_groups=mesh['z'=4,'x'=4,'core'=2,'blk'=4] {'z','x'}, dimensions={0} | all-to-all | bytes 786432 | tf_op jit(solution)/shard_map/all_to_all | solution.py:385
  124.1 9.0 %modes.3 = (bf16[4,2,8,16384]{3,2,1,0:T(8,128)(2,1)}, f32[8,128]{1,0:T(8,128)S(1)}) custom-call(s32[3]{0:T(128)S(1)} %pad_add_fusion.place_ref, f32[4,2,8,128]{3,2,1,0:T(8,128)S(1)} %copy-done.9, f32[1,16384]{1,0:T(1,128)S(1)} %bitcast.14, s32[1,16384]{1,0:T(1,128)S(1)} %bitcast.16, ...), custom_call_target="tpu_custom_call", output_to_operand_aliasing={{0}: (13, {})} | custom-call | flops 2073741824 | bytes 5242880 | tf_op jit(solution)/shard_map/modes/pallas_call | solution.py:326
  133.1 1.2 collective-permute-done.14
  134.3 10.9 %all_to_all.16.in_ref = f32[16,8,128]{2,1,0:T(8,128)} all-to-all(f32[16,8,128]{2,1,0:T(8,128)S(1)} %broadcast_in_dim.8), channel_id=1, replica_groups=mesh['z'=4,'x'=4,'core'=2,'blk'=4] {'z','x'}, dimensions={0} | all-to-all | bytes 131072 | tf_op jit(solution)/shard_map/all_to_all | solution.py:385
  145.2 1.6 %energy.1 = f32[4,8,384]{2,1,0:T(8,128)} custom-call(f32[16,8,128]{2,1,0:T(8,128)} %all_to_all.16.in_ref), custom_call_target="tpu_custom_call" | custom-call | tf_op jit(solution)/shard_map/energy/pallas_call | solution.py:374
  (44 shorter events, 0.6 us)
Async XLA Ops:
  6.3 25.0 %collective-permute-start.3 = (bf16[32,8192]{1,0:T(8,128)(2,1)}, bf16[32,8192]{1,0:T(8,128)(2,1)S(1)}, u32[]{:S(2)}, u32[]{:S(2)}) collective-permute-start(bf16[32,8192]{1,0:T(8,128)(2,1)} %get-tuple-element.28), channel_id=1, source_target_pairs={{0,1},{1,2},{2,3},{3,0},{4,5},{5,6},{6,7},{7,4},{8,9},{9,10},{10,1... | collective-permute-start | bytes 1572872 | tf_op jit(solution)/shard_map/ppermute | solution.py:410
  7.8 23.4 %collective-permute-start.4 = (bf16[32,8192]{1,0:T(8,128)(2,1)}, bf16[32,8192]{1,0:T(8,128)(2,1)S(1)}, u32[]{:S(2)}, u32[]{:S(2)}) collective-permute-start(bf16[32,8192]{1,0:T(8,128)(2,1)} %get-tuple-element.29), channel_id=1, source_target_pairs={{0,2},{1,3},{2,0},{3,1},{4,6},{5,7},{6,4},{7,5},{8,10},{9,11},{10,... | collective-permute-start | bytes 1572872 | tf_op jit(solution)/shard_map/ppermute | solution.py:410
  8.7 25.4 %copy-start.10 = (s32[4,8]{1,0:T(4,128)S(1)}, s32[4,8]{1,0:T(4,128)}, u32[]{:S(2)}) copy-start(s32[4,8]{1,0:T(4,128)} %param.10) | copy-start | bytes 388
  8.7 46.0 %copy-start = (f32[16384]{0:T(1024)S(1)}, f32[16384]{0:T(1024)}, u32[]{:S(2)}) copy-start(f32[16384]{0:T(1024)} %param.8) | copy-start | bytes 196612
  8.7 46.0 %copy-start.3 = (bf16[32,8192]{1,0:T(8,128)(2,1)S(1)}, bf16[32,8192]{1,0:T(8,128)(2,1)}, u32[]{:S(2)}) copy-start(bf16[32,8192]{1,0:T(8,128)(2,1)} %get-tuple-element.27.rest_0_) | copy-start | bytes 1572868
  8.7 35.5 %collective-permute-start.5 = (bf16[32,8192]{1,0:T(8,128)(2,1)}, bf16[32,8192]{1,0:T(8,128)(2,1)S(1)}, u32[]{:S(2)}, u32[]{:S(2)}) collective-permute-start(bf16[32,8192]{1,0:T(8,128)(2,1)} %get-tuple-element.30), channel_id=1, source_target_pairs={{0,3},{1,0},{2,1},{3,2},{4,7},{5,4},{6,5},{7,6},{8,11},{9,8},{10,9... | collective-permute-start | bytes 1572872 | tf_op jit(solution)/shard_map/ppermute | solution.py:410
  16.7 41.6 %copy-start.4 = (bf16[32,8192]{1,0:T(8,128)(2,1)S(1)}, bf16[32,8192]{1,0:T(8,128)(2,1)}, u32[]{:S(2)}) copy-start(bf16[32,8192]{1,0:T(8,128)(2,1)} %get-tuple-element.23.rest_0_.rest_4_) | copy-start | bytes 1572868
  16.7 37.0 %collective-permute-start = (bf16[32,8192]{1,0:T(8,128)(2,1)}, bf16[32,8192]{1,0:T(8,128)(2,1)S(1)}, u32[]{:S(2)}, u32[]{:S(2)}) collective-permute-start(bf16[32,8192]{1,0:T(8,128)(2,1)} %get-tuple-element.24), channel_id=1, source_target_pairs={{0,1},{1,2},{2,3},{3,0},{4,5},{5,6},{6,7},{7,4},{8,9},{9,10},{10,1... | collective-permute-start | bytes 1572872 | tf_op jit(solution)/shard_map/ppermute | solution.py:410
  16.8 38.9 %collective-permute-start.1 = (bf16[32,8192]{1,0:T(8,128)(2,1)}, bf16[32,8192]{1,0:T(8,128)(2,1)}, u32[]{:S(2)}, u32[]{:S(2)}) collective-permute-start(bf16[32,8192]{1,0:T(8,128)(2,1)} %get-tuple-element.25), channel_id=1, source_target_pairs={{0,2},{1,3},{2,0},{3,1},{4,6},{5,7},{6,4},{7,5},{8,10},{9,11},{10,... | collective-permute-start | bytes 1572872 | tf_op jit(solution)/shard_map/ppermute | solution.py:410
  31.3 27.1 %collective-permute-start.2 = (bf16[32,8192]{1,0:T(8,128)(2,1)}, bf16[32,8192]{1,0:T(8,128)(2,1)}, u32[]{:S(2)}, u32[]{:S(2)}) collective-permute-start(bf16[32,8192]{1,0:T(8,128)(2,1)} %get-tuple-element.26), channel_id=1, source_target_pairs={{0,3},{1,0},{2,1},{3,2},{4,7},{5,4},{6,5},{7,6},{8,11},{9,8},{10,9... | collective-permute-start | bytes 1572872 | tf_op jit(solution)/shard_map/ppermute | solution.py:410
  31.3 41.3 %collective-permute-start.10 = (bf16[32,8192]{1,0:T(8,128)(2,1)}, bf16[32,8192]{1,0:T(8,128)(2,1)}, u32[]{:S(2)}, u32[]{:S(2)}) collective-permute-start(bf16[32,8192]{1,0:T(8,128)(2,1)} %get-tuple-element.38), channel_id=1, source_target_pairs={{0,1},{1,2},{2,3},{3,0},{4,5},{5,6},{6,7},{7,4},{8,9},{9,10},{10,1... | collective-permute-start | bytes 1572872 | tf_op jit(solution)/shard_map/ppermute | solution.py:410
  44.2 31.0 %collective-permute-start.11 = (bf16[32,8192]{1,0:T(8,128)(2,1)}, bf16[32,8192]{1,0:T(8,128)(2,1)}, u32[]{:S(2)}, u32[]{:S(2)}) collective-permute-start(bf16[32,8192]{1,0:T(8,128)(2,1)} %get-tuple-element.39), channel_id=1, source_target_pairs={{0,2},{1,3},{2,0},{3,1},{4,6},{5,7},{6,4},{7,5},{8,10},{9,11},{10,... | collective-permute-start | bytes 1572872 | tf_op jit(solution)/shard_map/ppermute | solution.py:410
  53.7 0.9 copy-start.5
  54.6 34.8 %collective-permute-start.12 = (bf16[32,8192]{1,0:T(8,128)(2,1)}, bf16[32,8192]{1,0:T(8,128)(2,1)}, u32[]{:S(2)}, u32[]{:S(2)}) collective-permute-start(bf16[32,8192]{1,0:T(8,128)(2,1)} %get-tuple-element.40), channel_id=1, source_target_pairs={{0,3},{1,0},{2,1},{3,2},{4,7},{5,4},{6,5},{7,6},{8,11},{9,8},{10,9... | collective-permute-start | bytes 1572872 | tf_op jit(solution)/shard_map/ppermute | solution.py:410
  54.6 3.7 %copy-start.6 = (bf16[32,8192]{1,0:T(8,128)(2,1)S(1)}, bf16[32,8192]{1,0:T(8,128)(2,1)}, u32[]{:S(2)}) copy-start(bf16[32,8192]{1,0:T(8,128)(2,1)} %copy-done.5) | copy-start | bytes 1572868
  55.7 33.6 %copy-start.1 = (bf16[32,8192]{1,0:T(8,128)(2,1)S(1)}, bf16[32,8192]{1,0:T(8,128)(2,1)}, u32[]{:S(2)}) copy-start(bf16[32,8192]{1,0:T(8,128)(2,1)} %get-tuple-element.37.rest_0_) | copy-start | bytes 1572868
  60.6 31.2 %copy-start.8 = (s32[16384]{0:T(1024)S(1)}, s32[16384]{0:T(1024)}, u32[]{:S(2)}) copy-start(s32[16384]{0:T(1024)} %param.9) | copy-start | bytes 196612
  60.6 31.2 %copy-start.9 = (f32[4,2,8,128]{3,2,1,0:T(8,128)S(1)}, f32[4,2,8,128]{3,2,1,0:T(8,128)}, u32[]{:S(2)}) copy-start(f32[4,2,8,128]{3,2,1,0:T(8,128)} %constant.28.clone.start_ref) | copy-start | bytes 98308
  60.6 1.3 collective-permute-start.6
  62.6 29.1 %all-to-all-start = ((f32[16,2,24,128]{3,2,1,0:T(8,128)}), f32[16,2,24,128]{3,2,1,0:T(8,128)}, u32[]{:S(2)}, u32[]{:S(2)}) async-start(f32[16,2,24,128]{3,2,1,0:T(8,128)} %broadcast_in_dim.6), calls=%async_computation | async-start | bytes 786432 | tf_op jit(solution)/shard_map/all_to_all | solution.py:385
  70.6 31.7 %collective-permute-start.7 = (bf16[32,8192]{1,0:T(8,128)(2,1)}, bf16[32,8192]{1,0:T(8,128)(2,1)}, u32[]{:S(2)}, u32[]{:S(2)}) collective-permute-start(bf16[32,8192]{1,0:T(8,128)(2,1)} %get-tuple-element.34), channel_id=1, source_target_pairs={{0,1},{1,2},{2,3},{3,0},{4,5},{5,6},{6,7},{7,4},{8,9},{9,10},{10,1... | collective-permute-start | bytes 1572872 | tf_op jit(solution)/shard_map/ppermute | solution.py:410
  71.1 31.1 %collective-permute-start.8 = (bf16[32,8192]{1,0:T(8,128)(2,1)}, bf16[32,8192]{1,0:T(8,128)(2,1)}, u32[]{:S(2)}, u32[]{:S(2)}) collective-permute-start(bf16[32,8192]{1,0:T(8,128)(2,1)} %get-tuple-element.35), channel_id=1, source_target_pairs={{0,2},{1,3},{2,0},{3,1},{4,6},{5,7},{6,4},{7,5},{8,10},{9,11},{10,... | collective-permute-start | bytes 1572872 | tf_op jit(solution)/shard_map/ppermute | solution.py:410
  72.5 29.7 %collective-permute-start.9 = (bf16[32,8192]{1,0:T(8,128)(2,1)}, bf16[32,8192]{1,0:T(8,128)(2,1)}, u32[]{:S(2)}, u32[]{:S(2)}) collective-permute-start(bf16[32,8192]{1,0:T(8,128)(2,1)} %get-tuple-element.36), channel_id=1, source_target_pairs={{0,3},{1,0},{2,1},{3,2},{4,7},{5,4},{6,5},{7,6},{8,11},{9,8},{10,9... | collective-permute-start | bytes 1572872 | tf_op jit(solution)/shard_map/ppermute | solution.py:410
  91.8 1.0 copy-start.7
  92.8 9.5 %copy-start.2 = (bf16[32,8192]{1,0:T(8,128)(2,1)S(1)}, bf16[32,8192]{1,0:T(8,128)(2,1)}, u32[]{:S(2)}) copy-start(bf16[32,8192]{1,0:T(8,128)(2,1)} %get-tuple-element.33.rest_0_.rest_4_) | copy-start | bytes 1572868
  104.7 1.3 collective-permute-start.13
  133.0 1.2 collective-permute-start.14

commit v7 on v6

--- a/solution.py
+++ b/solution.py
@@ -145,13 +145,15 @@
     return jnp.where(odd_lanes(value.shape), other, -other)
 
 
-def gram_call(half, pieces, weights, pivot_local, before):
+def gram_call(half, pieces, weights, pivot_local, before, rows):
     part = pieces[0].shape[1]
 
     def kernel(p_ref, w_ref, *rest):
         x_refs, rest = rest[:GROUPS], rest[GROUPS:]
         out_ref = rest[-1]
         lane = lax.broadcasted_iota(jnp.int32, (MODES, part), 1) + half * part
+        parts = []
+        pivots = []
         for f in range(PAIR):
             x = jnp.concatenate([r[16 * f : 16 * f + 16] for r in x_refs], axis=0)
             wx = x.astype(F32) * w_ref[:, half * part : (half + 1) * part]
@@ -164,14 +166,17 @@
             cross = other_lanes(other_rows(gram)) + jnp.where(same, gram, -gram)
             cross = jnp.where(low_rows((32, 128)), cross[:32], other_rows(cross[32:]))
             packed = jnp.where(low_lanes((16, 128)), cross[:16], cross[16:])
-            packed = jnp.concatenate([packed, total[64:72]], axis=0)
-            if before is not None:
-                packed = packed + rest[0][f]
-            out_ref[f] = packed
+            parts.append(packed)
+            pivots.append(total[64:72])
+        parts.append(jnp.where(low_lanes((MODES, 128)), pivots[0], pivots[1]))
+        if rows > 16 * PAIR + MODES:
+            parts.append(jnp.zeros((rows - 16 * PAIR - MODES, 128), F32))
+        result = jnp.concatenate(parts, axis=0)
+        out_ref[...] = result if before is None else result + rest[0][...]
 
     return pl.pallas_call(
         kernel,
-        out_shape=jax.ShapeDtypeStruct((PAIR, 24, 128), F32),
+        out_shape=jax.ShapeDtypeStruct((rows, 128), F32),
         compiler_params=pltpu.CompilerParams(vmem_limit_bytes=SMALL),
         cost_estimate=pl.CostEstimate(
             flops=2 * PAIR * 64 * 256 * part, bytes_accessed=4 * 64 * part, transcendentals=0
@@ -254,7 +259,7 @@
         total = jnp.sum(sum_ref[...], axis=0)
         crosses = []
         for f in range(PAIR):
-            packed = total[f, :16] * (1.0 / row_count)
+            packed = total[16 * f : 16 * f + 16] * (1.0 / row_count)
             swap = pltpu.roll(packed, 64, 1)
             low = low_lanes(packed.shape)
             crosses.append(
@@ -267,7 +272,8 @@
         low = low_lanes(vec.shape)
         upper = jnp.where(odd, -vec, vec).astype(BF16).astype(F32)
         lower = jnp.where(odd, alt, -alt).astype(BF16).astype(F32)
-        at = jnp.where(low, total[:, 16:24], 0.0)
+        pivots = total[16 * PAIR : 16 * PAIR + MODES]
+        at = jnp.where(low, jnp.stack([pivots, pltpu.roll(pivots, 64, 1)]), 0.0)
         z_re = jnp.sum(upper * at, axis=2, keepdims=True)
         z_im = jnp.sum(lower * at, axis=2, keepdims=True)
         inverse = lax.rsqrt(z_re * z_re + z_im * z_im + 1.0)
@@ -416,7 +422,8 @@
         for half in range(HALVES):
             known = weights if before is None or half < HALVES - 1 else after(weights, before[1])
             gram = gram_call(
-                half, pieces[pair, half], known, pivot_local[PAIR * pair : PAIR * pair + PAIR], gram
+                half, pieces[pair, half], known, pivot_local[PAIR * pair : PAIR * pair + PAIR], gram,
+                48 if pair == 0 else 40,
             )
         before = modes_call(
             pair, place, start, weights, degrees, gather_chips(gram),

time: 147 us -> 147 us (level)
  no operation moved by 1% of the time
where the time goes in v7:
time: 147 us; the launch traced here: 146 us
  waiting for transfers between devices  50.9 us (35%)
  Pallas kernels  39.1 us (27%)
  blocking collectives  28.3 us (19%)
  starting transfers between devices  23.9 us (16%)
  local copies, waits for them, and re-layouts  2.93 us (2%)
    ppermute x12, waiting for transfers between devices, per_device(): lax.ppermute(sent[k], 'blk', [(g, (g + k) % GROUPS) for g in range(GROUPS)])  47.4 us
    all_to_all x2, blocking collectives, gather_chips(): return lax.all_to_all(spread, ('z', 'x'), 0, 0, tiled=True)  28.3 us
    pallas_call x2, Pallas kernels, modes_call(): pl.pallas_call(kernel, in_specs=in_specs, out_specs=[raw, vmem], scratch_...  18.4 us
    ppermute x12, starting transfers between devices, per_device(): lax.ppermute(sent[k], 'blk', [(g, (g + k) % GROUPS) for g in range(GROUPS)])  15.7 us
    pallas_call x2, Pallas kernels, spectra_call(): pl.pallas_call(kernel, grid=(steps,), in_specs=[pl.BlockSpec((GROUPS, row...  11.1 us
    pallas_call x4, Pallas kernels, gram_call(): pl.pallas_call(kernel, out_shape=jax.ShapeDtypeStruct((rows, 128), F32),...  8.02 us
    all_to_all x1, starting transfers between devices, gather_chips(): return lax.all_to_all(spread, ('z', 'x'), 0, 0, tiled=True)  7.93 us
    ppermute x3, waiting for transfers between devices, gather_chips(): value = value + lax.ppermute(value, 'core', [(0, 1), (1, 0)])  3.51 us
  transfers between devices with their start and end apart: 16, of which 8 were waited for; matrix products, arithmetic and copies ran while one was open for 1% of the time, Pallas kernels for 14%

profile of v7, /device:TPU:8, one launch (start us, length us, event | category | flops | bytes accessed | tf_op | source)
XLA Modules:
  0.0 146.1 jit_solution(16632089337654403308)
XLA Ops:
  0.6 5.6 %spectra.3 = (bf16[32,8192]{1,0:T(8,128)(2,1)}, bf16[32,8192]{1,0:T(8,128)(2,1)}, bf16[32,8192]{1,0:T(8,128)(2,1)}, bf16[32,8192]{1,0:T(8,128)(2,1)}, bf16[32,81...) custom-call(bf16[4,32,256]{2,1,0:T(8,128)(2,1)} %constant.29.clone.lhs_ref, ...), custom_call_target="tpu_custom_call" | custom-call | flops 1073741824 | bytes 12582912 | tf_op jit(solution)/shard_map/spectra/pallas_call | solution.py:98
  6.3 1.6 %collective-permute-start.3 = (bf16[32,8192]{1,0:T(8,128)(2,1)}, bf16[32,8192]{1,0:T(8,128)(2,1)S(1)}, u32[]{:S(2)}, u32[]{:S(2)}) collective-permute-start(bf16[32,8192]{1,0:T(8,128)(2,1)} %get-tuple-element.28), channel_id=1, source_target_pairs={{0,1},{1,2},{2,3},{3,0},{4,5},{5,6},{6,7},{7,4},{8,9},{9,10},{10,1... | collective-permute-start | bytes 1572872 | tf_op jit(solution)/shard_map/ppermute | solution.py:416
  7.8 0.9 collective-permute-start.4
  8.7 2.5 %collective-permute-start.5 = (bf16[32,8192]{1,0:T(8,128)(2,1)}, bf16[32,8192]{1,0:T(8,128)(2,1)S(1)}, u32[]{:S(2)}, u32[]{:S(2)}) collective-permute-start(bf16[32,8192]{1,0:T(8,128)(2,1)} %get-tuple-element.30), channel_id=1, source_target_pairs={{0,3},{1,0},{2,1},{3,2},{4,7},{5,4},{6,5},{7,6},{8,11},{9,8},{10,9... | collective-permute-start | bytes 1572872 | tf_op jit(solution)/shard_map/ppermute | solution.py:416
  11.2 5.5 %spectra.2 = (bf16[32,8192]{1,0:T(8,128)(2,1)}, bf16[32,8192]{1,0:T(8,128)(2,1)}, bf16[32,8192]{1,0:T(8,128)(2,1)}, bf16[32,8192]{1,0:T(8,128)(2,1)}, bf16[32,81...) custom-call(bf16[4,32,256]{2,1,0:T(8,128)(2,1)} %constant.29.clone.lhs_ref, ...), custom_call_target="tpu_custom_call" | custom-call | flops 1073741824 | bytes 12582912 | tf_op jit(solution)/shard_map/spectra/pallas_call | solution.py:98
  16.8 3.4 %collective-permute-start.1 = (bf16[32,8192]{1,0:T(8,128)(2,1)}, bf16[32,8192]{1,0:T(8,128)(2,1)}, u32[]{:S(2)}, u32[]{:S(2)}) collective-permute-start(bf16[32,8192]{1,0:T(8,128)(2,1)} %get-tuple-element.25), channel_id=1, source_target_pairs={{0,2},{1,3},{2,0},{3,1},{4,6},{5,7},{6,4},{7,5},{8,10},{9,11},{10,... | collective-permute-start | bytes 1572872 | tf_op jit(solution)/shard_map/ppermute | solution.py:416
  20.2 11.1 %collective-permute-done.3.rest_1_ = bf16[32,8192]{1,0:T(8,128)(2,1)S(1)} collective-permute-done((bf16[32,8192]{1,0:T(8,128)(2,1)}, bf16[32,8192]{1,0:T(8,128)(2,1)S(1)}, u32[]{:S(2)}, u32[]{:S(2)}) %collective-permute-start.3) | collective-permute-done | bytes 524320 | tf_op jit(solution)/shard_map/ppermute | solution.py:416
  31.3 2.8 %collective-permute-start.10 = (bf16[32,8192]{1,0:T(8,128)(2,1)}, bf16[32,8192]{1,0:T(8,128)(2,1)}, u32[]{:S(2)}, u32[]{:S(2)}) collective-permute-start(bf16[32,8192]{1,0:T(8,128)(2,1)} %get-tuple-element.38), channel_id=1, source_target_pairs={{0,1},{1,2},{2,3},{3,0},{4,5},{5,6},{6,7},{7,4},{8,9},{9,10},{10,1... | collective-permute-start | bytes 1572872 | tf_op jit(solution)/shard_map/ppermute | solution.py:416
  34.1 10.1 %collective-permute-done.5.rest_3_ = bf16[32,8192]{1,0:T(8,128)(2,1)S(1)} collective-permute-done((bf16[32,8192]{1,0:T(8,128)(2,1)}, bf16[32,8192]{1,0:T(8,128)(2,1)S(1)}, u32[]{:S(2)}, u32[]{:S(2)}) %collective-permute-start.5) | collective-permute-done | bytes 524320 | tf_op jit(solution)/shard_map/ppermute | solution.py:416
  44.2 9.5 %collective-permute-done.rest_1_.rest_5_ = bf16[32,8192]{1,0:T(8,128)(2,1)S(1)} collective-permute-done((bf16[32,8192]{1,0:T(8,128)(2,1)}, bf16[32,8192]{1,0:T(8,128)(2,1)S(1)}, u32[]{:S(2)}, u32[]{:S(2)}) %collective-permute-start) | collective-permute-done | bytes 524320 | tf_op jit(solution)/shard_map/ppermute | solution.py:416
  53.7 0.9 copy-done.5
  54.6 0.1 copy.11.p_ref
  54.7 1.0 gram.4.rest_4_
  55.7 2.6 %collective-permute-done.2.rest_3_.rest_7_ = bf16[32,8192]{1,0:T(8,128)(2,1)} collective-permute-done((bf16[32,8192]{1,0:T(8,128)(2,1)}, bf16[32,8192]{1,0:T(8,128)(2,1)}, u32[]{:S(2)}, u32[]{:S(2)}) %collective-permute-start.2) | collective-permute-done | bytes 524320 | tf_op jit(solution)/shard_map/ppermute | solution.py:416
  58.3 2.2 %gram.5 = f32[48,128]{1,0:T(8,128)S(1)} custom-call(s32[2,8,1]{2,1,0:T(8,128)S(1)} %copy.11.p_ref, f32[1,16384]{1,0:T(1,128)S(1)} %bitcast.10, bf16[32,8192]{1,0:T(8,128)(2,1)S(1)} %copy-done.4, bf16[32,8192]{1,0:T(8,128)(2,1)S(1)} %copy-done.6, bf16[32,8192]{1,0:T(8,128)(2,1)} %collective-permute-done.1.rest_2_.rest_6_, ...), custom_call_target="tpu_custom_call" | custom-call | flops 536870912 | bytes 2097152 | tf_op jit(solution)/shard_map/gram/pallas_call | solution.py:177
  60.7 1.2 collective-permute-done.6
  61.9 0.8 broadcast_in_dim.6
  62.6 7.9 %all-to-all-start = ((f32[16,48,128]{2,1,0:T(8,128)}), f32[16,48,128]{2,1,0:T(8,128)}, u32[]{:S(2)}, u32[]{:S(2)}) async-start(f32[16,48,128]{2,1,0:T(8,128)} %broadcast_in_dim.6), calls=%async_computation | async-start | bytes 786432 | tf_op jit(solution)/shard_map/all_to_all | solution.py:391
  70.6 0.5 collective-permute-start.7
  71.1 1.4 collective-permute-start.8
  72.5 2.5 %collective-permute-start.9 = (bf16[32,8192]{1,0:T(8,128)(2,1)}, bf16[32,8192]{1,0:T(8,128)(2,1)}, u32[]{:S(2)}, u32[]{:S(2)}) collective-permute-start(bf16[32,8192]{1,0:T(8,128)(2,1)} %get-tuple-element.36), channel_id=1, source_target_pairs={{0,3},{1,0},{2,1},{3,2},{4,7},{5,4},{6,5},{7,6},{8,11},{9,8},{10,9... | collective-permute-start | bytes 1572872 | tf_op jit(solution)/shard_map/ppermute | solution.py:416
  75.2 14.1 %collective-permute-done.12.rest_3_ = bf16[32,8192]{1,0:T(8,128)(2,1)} collective-permute-done((bf16[32,8192]{1,0:T(8,128)(2,1)}, bf16[32,8192]{1,0:T(8,128)(2,1)}, u32[]{:S(2)}, u32[]{:S(2)}) %collective-permute-start.12) | collective-permute-done | bytes 524320 | tf_op jit(solution)/shard_map/ppermute | solution.py:416
  89.3 2.4 %gram.6.rest_4_ = f32[40,128]{1,0:T(8,128)S(1)} custom-call(s32[2,8,1]{2,1,0:T(8,128)S(1)} %copy.13.p_ref, f32[1,16384]{1,0:T(1,128)S(1)} %bitcast.11, bf16[32,8192]{1,0:T(8,128)(2,1)S(1)} %copy-done.1, bf16[32,8192]{1,0:T(8,128)(2,1)} %collective-permute-done.10.rest_1_, bf16[32,8192]{1,0:T(8,128)(2,1)} %collective-permute-done.11.rest_2_, ...), custom_call_target="tpu_custom_call" | custom-call | flops 536870912 | bytes 2097152 | tf_op jit(solution)/shard_map/gram/pallas_call | solution.py:177
  91.8 1.0 copy-done.7
  92.8 9.4 %modes.2 = (bf16[4,2,8,16384]{3,2,1,0:T(8,128)(2,1)}, f32[8,128]{1,0:T(8,128)S(1)}) custom-call(s32[3]{0:T(128)S(1)} %pad_add_fusion.place_ref, f32[4,2,8,128]{3,2,1,0:T(8,128)S(1)} %copy-done.9, f32[1,16384]{1,0:T(1,128)S(1)} %bitcast.12, s32[1,16384]{1,0:T(1,128)S(1)} %bitcast.15, f32[16,48,128]{2,1,0:T(8,128)} %all-to-all-done.sum_ref, ...), custom_call_target="tpu_custom_call" | custom-call | flops 2073741824 | bytes 5242880 | tf_op jit(solution)/shard_map/modes/pallas_call | solution.py:332
  102.3 2.4 %gram.7 = f32[40,128]{1,0:T(8,128)S(1)} custom-call(s32[2,8,1]{2,1,0:T(8,128)S(1)} %copy.13.p_ref, f32[1,16384]{1,0:T(1,128)S(1)} %bitcast.13, bf16[32,8192]{1,0:T(8,128)(2,1)S(1)} %copy-done.2, bf16[32,8192]{1,0:T(8,128)(2,1)} %collective-permute-done.7.rest_1_.rest_5_, bf16[32,8192]{1,0:T(8,128)(2,1)} %collective-permute-done.8.rest_2_.rest_6_, ...), custom_call_target="tpu_custom_call" | custom-call | flops 536870912 | bytes 2097152 | tf_op jit(solution)/shard_map/gram/pallas_call | solution.py:177
  104.8 1.2 collective-permute-done.13
  106.0 17.4 %all_to_all.15.sum_ref = f32[16,40,128]{2,1,0:T(8,128)S(1)} all-to-all(f32[16,40,128]{2,1,0:T(8,128)S(1)} %broadcast_in_dim.7), channel_id=1, replica_groups=mesh['z'=4,'x'=4,'core'=2,'blk'=4] {'z','x'}, dimensions={0} | all-to-all | bytes 655360 | tf_op jit(solution)/shard_map/all_to_all | solution.py:391
  123.4 9.0 %modes.3 = (bf16[4,2,8,16384]{3,2,1,0:T(8,128)(2,1)}, f32[8,128]{1,0:T(8,128)S(1)}) custom-call(s32[3]{0:T(128)S(1)} %pad_add_fusion.place_ref, f32[4,2,8,128]{3,2,1,0:T(8,128)S(1)} %copy-done.9, f32[1,16384]{1,0:T(1,128)S(1)} %bitcast.14, s32[1,16384]{1,0:T(1,128)S(1)} %bitcast.16, ...), custom_call_target="tpu_custom_call", output_to_operand_aliasing={{0}: (13, {})} | custom-call | flops 2073741824 | bytes 5242880 | tf_op jit(solution)/shard_map/modes/pallas_call | solution.py:332
  132.4 1.2 collective-permute-done.14
  133.6 10.9 %all_to_all.16.in_ref = f32[16,8,128]{2,1,0:T(8,128)} all-to-all(f32[16,8,128]{2,1,0:T(8,128)S(1)} %broadcast_in_dim.8), channel_id=1, replica_groups=mesh['z'=4,'x'=4,'core'=2,'blk'=4] {'z','x'}, dimensions={0} | all-to-all | bytes 131072 | tf_op jit(solution)/shard_map/all_to_all | solution.py:391
  144.5 1.6 %energy.1 = f32[4,8,384]{2,1,0:T(8,128)} custom-call(f32[16,8,128]{2,1,0:T(8,128)} %all_to_all.16.in_ref), custom_call_target="tpu_custom_call" | custom-call | tf_op jit(solution)/shard_map/energy/pallas_call | solution.py:380
  (44 shorter events, 0.6 us)
Async XLA Ops:
  6.3 25.0 %collective-permute-start.3 = (bf16[32,8192]{1,0:T(8,128)(2,1)}, bf16[32,8192]{1,0:T(8,128)(2,1)S(1)}, u32[]{:S(2)}, u32[]{:S(2)}) collective-permute-start(bf16[32,8192]{1,0:T(8,128)(2,1)} %get-tuple-element.28), channel_id=1, source_target_pairs={{0,1},{1,2},{2,3},{3,0},{4,5},{5,6},{6,7},{7,4},{8,9},{9,10},{10,1... | collective-permute-start | bytes 1572872 | tf_op jit(solution)/shard_map/ppermute | solution.py:416
  7.8 23.4 %collective-permute-start.4 = (bf16[32,8192]{1,0:T(8,128)(2,1)}, bf16[32,8192]{1,0:T(8,128)(2,1)S(1)}, u32[]{:S(2)}, u32[]{:S(2)}) collective-permute-start(bf16[32,8192]{1,0:T(8,128)(2,1)} %get-tuple-element.29), channel_id=1, source_target_pairs={{0,2},{1,3},{2,0},{3,1},{4,6},{5,7},{6,4},{7,5},{8,10},{9,11},{10,... | collective-permute-start | bytes 1572872 | tf_op jit(solution)/shard_map/ppermute | solution.py:416
  8.7 25.4 %copy-start.10 = (s32[4,8]{1,0:T(4,128)S(1)}, s32[4,8]{1,0:T(4,128)}, u32[]{:S(2)}) copy-start(s32[4,8]{1,0:T(4,128)} %param.10) | copy-start | bytes 388
  8.7 46.0 %copy-start = (f32[16384]{0:T(1024)S(1)}, f32[16384]{0:T(1024)}, u32[]{:S(2)}) copy-start(f32[16384]{0:T(1024)} %param.8) | copy-start | bytes 196612
  8.7 46.0 %copy-start.3 = (bf16[32,8192]{1,0:T(8,128)(2,1)S(1)}, bf16[32,8192]{1,0:T(8,128)(2,1)}, u32[]{:S(2)}) copy-start(bf16[32,8192]{1,0:T(8,128)(2,1)} %get-tuple-element.27.rest_0_) | copy-start | bytes 1572868
  8.7 35.5 %collective-permute-start.5 = (bf16[32,8192]{1,0:T(8,128)(2,1)}, bf16[32,8192]{1,0:T(8,128)(2,1)S(1)}, u32[]{:S(2)}, u32[]{:S(2)}) collective-permute-start(bf16[32,8192]{1,0:T(8,128)(2,1)} %get-tuple-element.30), channel_id=1, source_target_pairs={{0,3},{1,0},{2,1},{3,2},{4,7},{5,4},{6,5},{7,6},{8,11},{9,8},{10,9... | collective-permute-start | bytes 1572872 | tf_op jit(solution)/shard_map/ppermute | solution.py:416
  16.7 41.6 %copy-start.4 = (bf16[32,8192]{1,0:T(8,128)(2,1)S(1)}, bf16[32,8192]{1,0:T(8,128)(2,1)}, u32[]{:S(2)}) copy-start(bf16[32,8192]{1,0:T(8,128)(2,1)} %get-tuple-element.23.rest_0_.rest_4_) | copy-start | bytes 1572868
  16.7 37.0 %collective-permute-start = (bf16[32,8192]{1,0:T(8,128)(2,1)}, bf16[32,8192]{1,0:T(8,128)(2,1)S(1)}, u32[]{:S(2)}, u32[]{:S(2)}) collective-permute-start(bf16[32,8192]{1,0:T(8,128)(2,1)} %get-tuple-element.24), channel_id=1, source_target_pairs={{0,1},{1,2},{2,3},{3,0},{4,5},{5,6},{6,7},{7,4},{8,9},{9,10},{10,1... | collective-permute-start | bytes 1572872 | tf_op jit(solution)/shard_map/ppermute | solution.py:416
  16.8 38.9 %collective-permute-start.1 = (bf16[32,8192]{1,0:T(8,128)(2,1)}, bf16[32,8192]{1,0:T(8,128)(2,1)}, u32[]{:S(2)}, u32[]{:S(2)}) collective-permute-start(bf16[32,8192]{1,0:T(8,128)(2,1)} %get-tuple-element.25), channel_id=1, source_target_pairs={{0,2},{1,3},{2,0},{3,1},{4,6},{5,7},{6,4},{7,5},{8,10},{9,11},{10,... | collective-permute-start | bytes 1572872 | tf_op jit(solution)/shard_map/ppermute | solution.py:416
  31.3 27.1 %collective-permute-start.2 = (bf16[32,8192]{1,0:T(8,128)(2,1)}, bf16[32,8192]{1,0:T(8,128)(2,1)}, u32[]{:S(2)}, u32[]{:S(2)}) collective-permute-start(bf16[32,8192]{1,0:T(8,128)(2,1)} %get-tuple-element.26), channel_id=1, source_target_pairs={{0,3},{1,0},{2,1},{3,2},{4,7},{5,4},{6,5},{7,6},{8,11},{9,8},{10,9... | collective-permute-start | bytes 1572872 | tf_op jit(solution)/shard_map/ppermute | solution.py:416
  31.3 41.3 %collective-permute-start.10 = (bf16[32,8192]{1,0:T(8,128)(2,1)}, bf16[32,8192]{1,0:T(8,128)(2,1)}, u32[]{:S(2)}, u32[]{:S(2)}) collective-permute-start(bf16[32,8192]{1,0:T(8,128)(2,1)} %get-tuple-element.38), channel_id=1, source_target_pairs={{0,1},{1,2},{2,3},{3,0},{4,5},{5,6},{6,7},{7,4},{8,9},{9,10},{10,1... | collective-permute-start | bytes 1572872 | tf_op jit(solution)/shard_map/ppermute | solution.py:416
  44.2 31.0 %collective-permute-start.11 = (bf16[32,8192]{1,0:T(8,128)(2,1)}, bf16[32,8192]{1,0:T(8,128)(2,1)}, u32[]{:S(2)}, u32[]{:S(2)}) collective-permute-start(bf16[32,8192]{1,0:T(8,128)(2,1)} %get-tuple-element.39), channel_id=1, source_target_pairs={{0,2},{1,3},{2,0},{3,1},{4,6},{5,7},{6,4},{7,5},{8,10},{9,11},{10,... | collective-permute-start | bytes 1572872 | tf_op jit(solution)/shard_map/ppermute | solution.py:416
  53.7 0.9 copy-start.5
  54.6 34.8 %collective-permute-start.12 = (bf16[32,8192]{1,0:T(8,128)(2,1)}, bf16[32,8192]{1,0:T(8,128)(2,1)}, u32[]{:S(2)}, u32[]{:S(2)}) collective-permute-start(bf16[32,8192]{1,0:T(8,128)(2,1)} %get-tuple-element.40), channel_id=1, source_target_pairs={{0,3},{1,0},{2,1},{3,2},{4,7},{5,4},{6,5},{7,6},{8,11},{9,8},{10,9... | collective-permute-start | bytes 1572872 | tf_op jit(solution)/shard_map/ppermute | solution.py:416
  54.6 3.7 %copy-start.6 = (bf16[32,8192]{1,0:T(8,128)(2,1)S(1)}, bf16[32,8192]{1,0:T(8,128)(2,1)}, u32[]{:S(2)}) copy-start(bf16[32,8192]{1,0:T(8,128)(2,1)} %copy-done.5) | copy-start | bytes 1572868
  55.7 33.6 %copy-start.1 = (bf16[32,8192]{1,0:T(8,128)(2,1)S(1)}, bf16[32,8192]{1,0:T(8,128)(2,1)}, u32[]{:S(2)}) copy-start(bf16[32,8192]{1,0:T(8,128)(2,1)} %get-tuple-element.37.rest_0_) | copy-start | bytes 1572868
  60.6 31.2 %copy-start.8 = (s32[16384]{0:T(1024)S(1)}, s32[16384]{0:T(1024)}, u32[]{:S(2)}) copy-start(s32[16384]{0:T(1024)} %param.9) | copy-start | bytes 196612
  60.6 31.2 %copy-start.9 = (f32[4,2,8,128]{3,2,1,0:T(8,128)S(1)}, f32[4,2,8,128]{3,2,1,0:T(8,128)}, u32[]{:S(2)}) copy-start(f32[4,2,8,128]{3,2,1,0:T(8,128)} %constant.28.clone.start_ref) | copy-start | bytes 98308
  60.6 1.3 collective-permute-start.6
  62.6 29.1 %all-to-all-start = ((f32[16,48,128]{2,1,0:T(8,128)}), f32[16,48,128]{2,1,0:T(8,128)}, u32[]{:S(2)}, u32[]{:S(2)}) async-start(f32[16,48,128]{2,1,0:T(8,128)} %broadcast_in_dim.6), calls=%async_computation | async-start | bytes 786432 | tf_op jit(solution)/shard_map/all_to_all | solution.py:391
  70.6 31.7 %collective-permute-start.7 = (bf16[32,8192]{1,0:T(8,128)(2,1)}, bf16[32,8192]{1,0:T(8,128)(2,1)}, u32[]{:S(2)}, u32[]{:S(2)}) collective-permute-start(bf16[32,8192]{1,0:T(8,128)(2,1)} %get-tuple-element.34), channel_id=1, source_target_pairs={{0,1},{1,2},{2,3},{3,0},{4,5},{5,6},{6,7},{7,4},{8,9},{9,10},{10,1... | collective-permute-start | bytes 1572872 | tf_op jit(solution)/shard_map/ppermute | solution.py:416
  71.1 31.1 %collective-permute-start.8 = (bf16[32,8192]{1,0:T(8,128)(2,1)}, bf16[32,8192]{1,0:T(8,128)(2,1)}, u32[]{:S(2)}, u32[]{:S(2)}) collective-permute-start(bf16[32,8192]{1,0:T(8,128)(2,1)} %get-tuple-element.35), channel_id=1, source_target_pairs={{0,2},{1,3},{2,0},{3,1},{4,6},{5,7},{6,4},{7,5},{8,10},{9,11},{10,... | collective-permute-start | bytes 1572872 | tf_op jit(solution)/shard_map/ppermute | solution.py:416
  72.5 29.7 %collective-permute-start.9 = (bf16[32,8192]{1,0:T(8,128)(2,1)}, bf16[32,8192]{1,0:T(8,128)(2,1)}, u32[]{:S(2)}, u32[]{:S(2)}) collective-permute-start(bf16[32,8192]{1,0:T(8,128)(2,1)} %get-tuple-element.36), channel_id=1, source_target_pairs={{0,3},{1,0},{2,1},{3,2},{4,7},{5,4},{6,5},{7,6},{8,11},{9,8},{10,9... | collective-permute-start | bytes 1572872 | tf_op jit(solution)/shard_map/ppermute | solution.py:416
  91.8 1.0 copy-start.7
  92.8 9.5 %copy-start.2 = (bf16[32,8192]{1,0:T(8,128)(2,1)S(1)}, bf16[32,8192]{1,0:T(8,128)(2,1)}, u32[]{:S(2)}) copy-start(bf16[32,8192]{1,0:T(8,128)(2,1)} %get-tuple-element.33.rest_0_.rest_4_) | copy-start | bytes 1572868
  104.7 1.3 collective-permute-start.13
  132.3 1.2 collective-permute-start.14
